TPU v7x, 256 devices: a whole 4x4x8 slice. The times are simulated.
256 devices in a mesh: rep: 32 (over z_lo, x, core), tp: 8 (over y, z_hi).
Axes of the slice: x: 4, y: 4, z: 8 (z_hi: 2, z_lo: 4; z = z_hi * 4 + z_lo), core: 2. Of those that a mesh axis runs over, the one named last changes fastest.
Arguments:
- prefix_hidden_states: bfloat16 [32, 768, 8192], P('rep', None, 'tp'), may hold values from -6 to 6
- latest_hidden: bfloat16 [1024, 8192], P('rep', 'tp'), may hold values from -6 to 6
- queries: bfloat16 [1024, 8192], P('rep', 'tp'), may hold values from -64 to 64
- suffix_key_cache: bfloat16 [1024, 128, 2048], P('rep', None, 'tp'), may hold values from -6 to 6
- key_value_weight: bfloat16 [8192, 2048], P('tp'), may hold values from -0.0625 to 0.0625
- key_value_bias: bfloat16 [2048], P('tp'), may hold values from -3 to 3
- adapter_down_weight: bfloat16 [8192, 512], P('tp'), may hold values from -0.0625 to 0.0625
- adapter_up_weight: bfloat16 [512, 1024], replicated, may hold values from -0.41992188 to 0.41992188
- parents: int32 [1024, 1], P('rep'), may hold values from 0 to 31; in each aligned block of 32 rows (0 to 31, 32 to 63, ...) at most 2 rows name the same one
- adapter_index: int32 [32], replicated, may hold values from 0 to 7
- suffix_length_count: int32 [1024], P('rep'), may hold values from 1 to 128, as said below
Outputs:
- prefix_kv: bfloat16 [32, 768, 2048], P('rep', None, 'tp')
- latest_key_value: bfloat16 [1024, 2048], P('rep', 'tp')
- attn_out: bfloat16 [1024, 8192], P('rep', 'tp')
Inputs may be any that keep to these rules, and one draw needn't show every extreme that they name: `parents`: among the completions of one index of rep no prompt is named more than 2 times, and every prompt is named by some completion. The new token of completion c sits right after its suffix_length_count[c] cached tokens.
All inputs are finite; a program needn't handle non-finite values.
Results may differ from a plain program's by a relative error of at most 0.01005.
The roundings to bfloat16 on the way count: a program that leaves them out, or rounds other values in their place, can miss the bound.
Values may be sent and summed in bfloat16 or wider, within the bound.
No kernel may reach another device: no remote copies, remote signals or barrier semaphores. Data moves between devices by JAX's collectives and lax.ppermute only.
A program may use at most 128 MiB of HBM per device.

v0:
```python
import jax
import jax.numpy as jnp
from jax import lax
from jax.sharding import PartitionSpec as P

HEAD_WIDTH = 128
ADAPTER_RANK = 32


rope_base = 1000000.0
neg_fill = -1e30


def rotate(values, token_position):
    half_dim = values.shape[-1] // 2
    frequency = rope_base ** (-(jnp.arange(half_dim, dtype=jnp.float32) * 2.0) / values.shape[-1])
    angles = token_position.astype(jnp.float32)[:, None] * frequency[None, :]
    cosine = jnp.cos(angles)[:, None, :]
    sine_wave = jnp.sin(angles)[:, None, :]
    first_half = values[..., :half_dim]
    second_half = values[..., half_dim:]
    return jnp.concatenate(
        [
            first_half * cosine - second_half * sine_wave,
            second_half * cosine + first_half * sine_wave,
        ],
        axis=-1,
    )


def finish(summed, bias_vec, token_position, head_count):
    row_count = summed.shape[0]
    shaped = summed.reshape(row_count, head_count, 2, HEAD_WIDTH) + bias_vec.astype(
        jnp.float32
    ).reshape(head_count, 2, HEAD_WIDTH)
    key_part = rotate(shaped[:, :, 0], token_position)
    return (
        jnp.stack([key_part, shaped[:, :, 1]], axis=2)
        .reshape(row_count, head_count * 2 * HEAD_WIDTH)
        .astype(jnp.bfloat16)
    )


def low_rank(rank_key, rank_value, up_key, up_value, head_count):
    row_count = rank_key.shape[0]
    delta_key = jnp.dot(rank_key, up_key, precision=lax.Precision.HIGHEST).reshape(
        row_count, head_count, 1, HEAD_WIDTH
    )
    delta_value = jnp.dot(rank_value, up_value, precision=lax.Precision.HIGHEST).reshape(
        row_count, head_count, 1, HEAD_WIDTH
    )
    return jnp.concatenate([delta_key, delta_value], axis=2).reshape(
        row_count, head_count * 2 * HEAD_WIDTH
    )


def reduce_terms(first_term, second_term):
    return (
        lax.psum_scatter(first_term, "tp", scatter_dimension=1, tiled=True),
        lax.psum_scatter(second_term, "tp", scatter_dimension=1, tiled=True),
    )


def soft_part(scores, values, form):
    top_score = jnp.max(scores, axis=-1)
    weights_f = jnp.exp(scores - top_score[..., None])
    total_sum = jnp.sum(weights_f, axis=-1)
    out_part = jnp.einsum(
        form, weights_f.astype(jnp.bfloat16), values, preferred_element_type=jnp.float32
    )
    return (out_part, top_score, total_sum)


def on_device(
    prefix_hidden_states,
    latest_hidden,
    queries,
    suffix_key_cache,
    key_value_weight,
    key_value_bias,
    adapter_down_weight,
    adapter_up_weight,
    parents,
    adapter_index,
    suffix_length_count,
):
    tp_count = lax.axis_size("tp")
    rep_index = lax.axis_index("rep")
    tp_index = lax.axis_index("tp")
    every_head = key_value_weight.shape[1] // (2 * HEAD_WIDTH)
    local_heads = every_head // tp_count
    comp_count = latest_hidden.shape[0]
    prompt_count = adapter_index.shape[0]
    adapter_list = adapter_up_weight.shape[0] // (2 * ADAPTER_RANK)
    prefix_len = prefix_hidden_states.shape[1]
    suf_len = suffix_key_cache.shape[1]
    group_size = queries.shape[1] // (local_heads * HEAD_WIDTH)
    scale = HEAD_WIDTH ** (-0.5)
    rows_prefix = prefix_hidden_states[0]
    parent = parents[:, 0]
    prompt_range = jnp.arange(prompt_count, dtype=jnp.int32)
    prompt_adapter = jnp.sum(jnp.where(prompt_range == rep_index, adapter_index, 0))
    new_adapter = jnp.sum(
        jnp.where(parent[:, None] == prompt_range[None, :], adapter_index[None, :], 0), axis=1
    )
    selector_mask = (
        new_adapter[:, None] == jnp.arange(adapter_list, dtype=jnp.int32)[None, :]
    ).astype(jnp.float32)
    up_weight_all = adapter_up_weight.astype(jnp.float32).reshape(
        adapter_list, 2, ADAPTER_RANK, every_head * HEAD_WIDTH
    )
    up_own = lax.dynamic_index_in_dim(up_weight_all, prompt_adapter, 0, keepdims=False)
    column_start = tp_index * (local_heads * HEAD_WIDTH)
    own_cols = lax.dynamic_slice_in_dim(up_own, column_start, local_heads * HEAD_WIDTH, 2)
    all_cols = lax.dynamic_slice_in_dim(up_weight_all, column_start, local_heads * HEAD_WIDTH, 3)
    down_weight_own = lax.dynamic_slice_in_dim(
        adapter_down_weight, prompt_adapter * (2 * ADAPTER_RANK), 2 * ADAPTER_RANK, 1
    )
    part_prefix = jnp.dot(rows_prefix, down_weight_own, preferred_element_type=jnp.float32)
    down_weight_all = jnp.dot(
        latest_hidden, adapter_down_weight, preferred_element_type=jnp.float32
    ).reshape(comp_count, adapter_list, 2 * ADAPTER_RANK)
    part_new = jnp.sum(selector_mask[:, :, None] * down_weight_all, axis=1)
    base_prefix = jnp.dot(rows_prefix, key_value_weight, preferred_element_type=jnp.float32)
    base_new = jnp.dot(latest_hidden, key_value_weight, preferred_element_type=jnp.float32)
    rank_prefix, rank_new = lax.psum((part_prefix, part_new), "tp")
    sum_prefix, sum_new = reduce_terms(base_prefix, base_new)
    picked_new = selector_mask[:, :, None, None] * rank_new.reshape(comp_count, 1, 2, ADAPTER_RANK)
    sum_prefix = sum_prefix + low_rank(
        rank_prefix[:, :ADAPTER_RANK],
        rank_prefix[:, ADAPTER_RANK:],
        own_cols[0],
        own_cols[1],
        local_heads,
    )
    sum_new = sum_new + low_rank(
        picked_new[:, :, 0].reshape(comp_count, adapter_list * ADAPTER_RANK),
        picked_new[:, :, 1].reshape(comp_count, adapter_list * ADAPTER_RANK),
        all_cols[:, 0].reshape(adapter_list * ADAPTER_RANK, local_heads * HEAD_WIDTH),
        all_cols[:, 1].reshape(adapter_list * ADAPTER_RANK, local_heads * HEAD_WIDTH),
        local_heads,
    )
    token_position = prefix_len + suffix_length_count
    prefix_local = finish(
        sum_prefix, key_value_bias, jnp.arange(prefix_len, dtype=jnp.int32), local_heads
    )
    latest_key_value = finish(sum_new, key_value_bias, token_position, local_heads)
    query_rot = rotate(
        queries.astype(jnp.float32).reshape(comp_count, local_heads * group_size, HEAD_WIDTH),
        token_position,
    ).astype(jnp.bfloat16)
    query_rot = query_rot.reshape(comp_count, local_heads, group_size, HEAD_WIDTH)
    cache_rows = suffix_key_cache.reshape(comp_count, suf_len, local_heads, 2, HEAD_WIDTH)
    own_kv = latest_key_value.reshape(comp_count, local_heads, 2, HEAD_WIDTH)
    scores = (
        jnp.einsum(
            "cgqd,cngd->cgqn", query_rot, cache_rows[:, :, :, 0], preferred_element_type=jnp.float32
        )
        * scale
    )
    valid_mask = (jnp.arange(suf_len, dtype=jnp.int32)[None, :] < suffix_length_count[:, None])[
        :, None, None, :
    ]
    scores = jnp.where(valid_mask, scores, neg_fill)
    self_score = (
        jnp.einsum("cgqd,cgd->cgq", query_rot, own_kv[:, :, 0], preferred_element_type=jnp.float32)
        * scale
    )
    top_suffix = jnp.maximum(jnp.max(scores, axis=-1), self_score)
    weights_f = jnp.exp(scores - top_suffix[..., None])
    self_weight = jnp.exp(self_score - top_suffix)
    total_suffix = jnp.sum(weights_f, axis=-1) + self_weight
    self_rounded = lax.optimization_barrier(self_weight.astype(jnp.bfloat16)).astype(jnp.float32)
    out_suffix = jnp.einsum(
        "cgqn,cngd->cgqd",
        weights_f.astype(jnp.bfloat16),
        cache_rows[:, :, :, 1],
        preferred_element_type=jnp.float32,
    )
    out_suffix = (
        out_suffix + self_rounded[..., None] * own_kv[:, :, 1].astype(jnp.float32)[:, :, None, :]
    )
    all_prefix = lax.all_gather(prefix_local[None], "rep", axis=0, tiled=True)
    chosen = jnp.take(all_prefix, parent, axis=0).reshape(
        comp_count, prefix_len, local_heads, 2, HEAD_WIDTH
    )
    prefix_scores = (
        jnp.einsum(
            "cgqd,cngd->cgqn", query_rot, chosen[:, :, :, 0], preferred_element_type=jnp.float32
        )
        * scale
    )
    out_prefix, top_prefix, total_prefix = soft_part(
        prefix_scores, chosen[:, :, :, 1], "cgqn,cngd->cgqd"
    )
    top_all = jnp.maximum(top_prefix, top_suffix)
    alpha_scale = jnp.exp(top_prefix - top_all)
    beta_scale = jnp.exp(top_suffix - top_all)
    merged = (alpha_scale[..., None] * out_prefix + beta_scale[..., None] * out_suffix) / (
        alpha_scale * total_prefix + beta_scale * total_suffix
    )[..., None]
    attn_out = merged.reshape(comp_count, local_heads * group_size * HEAD_WIDTH).astype(
        jnp.bfloat16
    )
    return (prefix_local[None], latest_key_value, attn_out)


def solution(mesh):
    in_specs = (
        P("rep", None, "tp"),
        P("rep", "tp"),
        P("rep", "tp"),
        P("rep", None, "tp"),
        P("tp", None),
        P("tp"),
        P("tp", None),
        P(),
        P("rep", None),
        P(),
        P("rep"),
    )
    out_specs = (P("rep", None, "tp"), P("rep", "tp"), P("rep", "tp"))
    return jax.shard_map(
        on_device, mesh=mesh, in_specs=in_specs, out_specs=out_specs, check_vma=False
    )
```

profile of v0, /device:TPU:1, one launch (start us, length us, event | category | flops | bytes accessed | tf_op | source)
XLA Modules:
  0.0 499.4 jit_solution(6127798422177353601)
XLA Ops:
  7.2 0.0 copy-start
  7.2 0.0 all-reduce.2.cloned.1.call-start
  7.2 1.4 fusion.52
  9.3 2.4 fusion.7
  11.7 0.0 all-reduce.2.cloned.1.call-update
  11.7 0.0 reduce-scatter.3.cloned.1.call-start
  11.7 7.5 %fusion.4 = f32[768,2048]{1,0:T(8,128)} fusion(bf16[1024,2048]{1,0:T(8,128)(2,1)} %param.15, bf16[1,768,1024]{2,1,0:T(8,128)(2,1)S(1)} %copy-done), kind=kOutput, calls=%fused_computation.8 | convolution fusion | flops 3221225472 | bytes 12058624 | tf_op jit(solution)/shard_map/dot_general | solution.py:124
  19.3 0.0 reduce-scatter.3.cloned.1.call-update
  19.3 0.0 reduce-scatter.5.cloned.1.call-start
  19.3 0.8 copy-done.4
  20.1 3.7 fusion.58
  23.8 0.0 reduce-scatter.5.cloned.1.call-update
  23.8 0.0 all-gather.2.cloned.1.call-start
  25.2 0.0 copy-done.7
  25.9 90.8 %all-reduce.2.cloned.1.call-done = f32[768,64]{0,1:T(8,128)} async-done(((f32[768,64]{0,1:T(8,128)}), f32[768,64]{0,1:T(8,128)}) %all-reduce.2.cloned.1.call-update) | async-done | bytes 196624 | tf_op jit(solution)/shard_map/psum | solution.py:126
  116.6 1.3 convolution_bitcast_fusion.1
  118.0 1.3 convolution_bitcast_fusion
  119.3 0.0 copy-start.5
  119.3 0.0 copy-start.8
  119.3 0.0 copy-start.9
  119.3 0.0 copy-start.3
  119.4 0.1 pad_maximum_fusion
  119.4 0.3 copy.97
  119.7 155.0 %reduce-scatter.3.cloned.1.call-done = f32[768,256]{1,0:T(8,128)} async-done(((f32[768,2048]{1,0:T(8,128)}), f32[768,256]{1,0:T(8,128)}) %reduce-scatter.3.cloned.1.call-update) | async-done | bytes 786448 | tf_op jit(solution)/shard_map/reduce_scatter | solution.py:59
  274.6 1.2 add.109
  275.9 0.3 copy.79
  276.2 0.0 copy-start.6
  276.2 0.1 broadcast_add_fusion
  276.4 0.8 fusion.26
  277.2 0.9 copy.94
  278.2 0.0 all-gather.2.cloned.1.call-update
  278.3 0.2 select_reduce_fusion
  278.5 0.1 copy.82
  278.5 0.3 fusion.59
  278.8 0.1 reshape.521
  278.9 0.1 multiply_reduce_fusion
  279.0 0.1 mul.263
  279.1 39.5 %psum.15 = f32[32,2,32]{2,1,0:T(2,128)S(1)} all-reduce(f32[32,2,32]{2,1,0:T(2,128)S(1)} %mul.263), channel_id=1, replica_groups=mesh['rep'=32,'tp'=8] {'tp'}, use_global_device_ids=true, to_apply=%region_6.7 | all-reduce | flops 2048 | bytes 16384 | tf_op jit(solution)/shard_map/psum | solution.py:126
  318.6 0.1 broadcast_multiply_fusion
  318.7 1.1 convolution_bitcast_fusion.2
  319.8 1.1 convolution_bitcast_fusion.3
  321.0 4.1 copy.91
  325.1 0.1 iota_compare_fusion
  325.2 0.1 multiply_cosine_fusion.1
  325.3 0.1 subtract_convert_fusion
  325.4 1.8 fusion.57
  327.2 29.6 %reduce-scatter.5.cloned.1.call-done = f32[32,256]{1,0:T(8,128)} async-done(((f32[32,2048]{1,0:T(8,128)}), f32[32,256]{1,0:T(8,128)}) %reduce-scatter.5.cloned.1.call-update) | async-done | bytes 32784 | tf_op jit(solution)/shard_map/reduce_scatter | solution.py:60
  356.8 0.8 bitcast_add_fusion
  357.6 0.1 fusion.39
  357.7 0.1 maximum_bitcast_fusion.1
  357.9 0.2 fusion.43
  358.1 0.6 copy.115
  358.7 0.2 fusion.29
  358.9 78.2 %all-gather.2.cloned.1.call-done = bf16[32,768,256]{2,1,0:T(8,128)(2,1)} async-done(((bf16[1,768,256]{2,1,0:T(8,128)(2,1)}), bf16[32,768,256]{2,1,0:T(8,128)(2,1)}) %all-gather.2.cloned.1.call-update) | async-done | bytes 12582928 | tf_op jit(solution)/shard_map/all_gather | solution.py:183
  437.2 11.3 %gather_fusion = bf16[32,768,256]{2,1,0:T(8,128)(2,1)} fusion(bf16[32,768,256]{2,1,0:T(8,128)(2,1)} %all-gather.2.cloned.1.call-done, s32[1024]{0:T(1024)S(1)} %pad_clamp_fusion), kind=kCustom, calls=%fused_computation | custom fusion | bytes 25165952 | tf_op jit(solution)/shard_map/jit(_take)/gather | solution.py:184
  448.4 16.6 %copy.89 = bf16[32,768,256]{1,2,0:T(8,128)(2,1)} copy(bf16[32,768,256]{2,1,0:T(8,128)(2,1)} %gather_fusion) | data formatting | bytes 25165824 | tf_op jit(solution)/shard_map/jit(_take)/gather | solution.py:184
  465.0 16.7 %copy.90 = bf16[32,768,1,2,128]{4,1,0,3,2:T(8,128)(2,1)} copy(bf16[32,768,1,2,128]{1,4,3,0,2:T(8,128)(2,1)} %bitcast.126) | data formatting | bytes 25165824 | tf_op jit(solution)/shard_map/jit(_take)/gather | solution.py:184
  481.7 6.6 %broadcast_select_fusion = bf16[32,768,1,2,128]{4,1,0,3,2:T(8,128)(2,1)S(1)} fusion(bf16[32,768,1,2,128]{4,1,0,3,2:T(8,128)(2,1)} %copy.90, pred[32]{0:T(512)(128)(4,1)S(1)} %and_bitcast_fusion), kind=kLoop, calls=%fused_computation.1 | loop fusion | flops 6291456 | bytes 25165856 | tf_op jit(solution)/shard_map/jit(_take)/select_n | solution.py:184
  488.3 0.0 copy-start.1
  488.3 1.8 fusion.56
  490.1 0.3 fusion.16
  490.5 1.0 fusion.14
  491.5 0.7 fusion.15
  492.2 0.7 copy.114
  (38 shorter events, 0.4 us)
Async XLA Ops:
  7.2 2.1 copy-start
  7.2 109.5 %all-reduce.2.cloned.1.call-start = ((), (), s32[]{:S(2)}) async-start(), calls=%async_computation.3 | async-start | bytes 393216 | tf_op jit(solution)/shard_map/psum | solution.py:126
  11.7 263.0 %reduce-scatter.3.cloned.1.call-start = ((), (), s32[]{:S(2)}) async-start(), calls=%async_computation.2 | async-start | bytes 7077888 | tf_op jit(solution)/shard_map/reduce_scatter | solution.py:59
  19.2 0.8 copy-start.4
  19.2 6.0 %copy-start.7 = (bf16[256]{0:T(256)(128)(2,1)S(1)}, bf16[256]{0:T(256)(128)(2,1)}, u32[]{:S(2)}) copy-start(bf16[256]{0:T(256)(128)(2,1)} %param.16) | copy-start | bytes 1540
  19.3 337.5 %reduce-scatter.5.cloned.1.call-start = ((), (), s32[]{:S(2)}) async-start(), calls=%async_computation.4 | async-start | bytes 294912 | tf_op jit(solution)/shard_map/reduce_scatter | solution.py:60
  23.8 413.3 %all-gather.2.cloned.1.call-start = ((), (), s32[]{:S(2)}) async-start(), calls=%async_computation.5 | async-start | bytes 12976128 | tf_op jit(solution)/shard_map/all_gather | solution.py:183
  119.3 158.9 %copy-start.5 = (bf16[32,1024]{1,0:T(8,128)(2,1)S(1)}, bf16[32,1024]{1,0:T(8,128)(2,1)}, u32[]{:S(2)}) copy-start(bf16[32,1024]{1,0:T(8,128)(2,1)} %param.13) | copy-start | bytes 196612
  119.3 158.9 %copy-start.8 = (s32[32]{0:T(128)S(1)}, s32[32]{0:T(128)}, u32[]{:S(2)}) copy-start(s32[32]{0:T(128)} %param.20) | copy-start | bytes 388
  119.3 158.9 %copy-start.9 = (s32[32,1]{0,1:T(1,128)S(1)}, s32[32,1]{0,1:T(1,128)}, u32[]{:S(2)}) copy-start(s32[32,1]{0,1:T(1,128)} %param.19) | copy-start | bytes 388
  119.3 159.2 %copy-start.3 = (bf16[1024,512]{1,0:T(8,128)(2,1)S(1)}, bf16[1024,512]{1,0:T(8,128)(2,1)}, u32[]{:S(2)}) copy-start(bf16[1024,512]{1,0:T(8,128)(2,1)} %param.17) | copy-start | bytes 3145732
  276.2 48.9 %copy-start.6 = (s32[32]{0:T(128)S(1)}, s32[32]{0:T(128)}, u32[]{:S(2)}) copy-start(s32[32]{0:T(128)} %param.21) | copy-start | bytes 388
  488.3 3.2 copy-start.2
  488.3 4.6 copy-start.1
Sparse Core Ops, SparseCore 0:
  11.8 104.7 all-reduce.1
  121.4 153.1 reduce-scatter.2
  278.5 78.2 reduce-scatter.4
  359.2 77.9 all-gather.1
where the time goes:
time: 501 us; the launch traced here: 499 us
  waiting for transfers between devices  354 us (71%)
  local copies, waits for them, and re-layouts  52.6 us (10%)
  blocking collectives  39.5 us (8%)
  matrix products  24.2 us (5%)
  between operations  16.8 us (3%)
  other arithmetic  12.5 us (2%)
    reduce_scatter x1, waiting for transfers between devices, reduce_terms(): lax.psum_scatter(first_term, 'tp', scatter_dimension=1, tiled=True)  155 us
    psum x1, waiting for transfers between devices, on_device(): rank_prefix, rank_new = lax.psum((part_prefix, part_new), 'tp')  90.8 us
    all_gather x1, waiting for transfers between devices, on_device(): all_prefix = lax.all_gather(prefix_local[None], 'rep', axis=0, tiled=True)  78.2 us
    gather x3, local copies, waits for them, and re-layouts, on_device(): jnp.take(all_prefix, parent, axis=0)  44.6 us
    psum x1, blocking collectives, on_device(): rank_prefix, rank_new = lax.psum((part_prefix, part_new), 'tp')  39.5 us
    reduce_scatter x1, waiting for transfers between devices, reduce_terms(): lax.psum_scatter(second_term, 'tp', scatter_dimension=1, tiled=True)  29.6 us
  transfers between devices with their start and end apart: 4, of which 4 were waited for; matrix products, arithmetic and copies ran while one was open for 6% of the time, Pallas kernels for 0%

commit v1 on v0

v1 whole, which is shorter than its diff:
```python
import jax
import jax.numpy as jnp
import numpy as np
from jax import lax
from jax.experimental import pallas as pl
from jax.experimental.pallas import tpu as pltpu
from jax.sharding import PartitionSpec as P

HW = 128
RANK = 32
ROPE_BASE = 1000000.0
NEG = -1e30
CHUNKS = 3
BLK = 32
SROWS = 16
QMAX = 32766.0
MAGIC = 12582912.0
F32 = jnp.float32
BF16 = jnp.bfloat16


def rope_tables(first, count):
    half = HW // 2
    freq = (ROPE_BASE ** (-(np.arange(half, dtype=np.float64) * 2.0) / HW)).astype(np.float32)
    angle = np.arange(first, first + count, dtype=np.float32)[:, None] * freq[None, :]
    cosine = np.cos(angle.astype(np.float64)).astype(np.float32)
    sine = np.sin(angle.astype(np.float64)).astype(np.float32)
    return np.concatenate([cosine, cosine], 1), np.concatenate([-sine, sine], 1)


def three_parts(table):
    parts = []
    rest = table.astype(np.float32)
    for _ in range(3):
        part = rest.astype(BF16)
        parts.append(part)
        rest = rest - part.astype(np.float32)
    return parts


def turn(values, cosine, sine):
    return values * cosine + pltpu.roll(values, HW // 2, 1) * sine


def nn(a, b):
    return lax.dot_general(a, b, (((1,), (0,)), ((), ())), preferred_element_type=F32)


def nt(a, b):
    return lax.dot_general(a, b, (((1,), (1,)), ((), ())), preferred_element_type=F32)


def encode(values, out_ref, peak_ref):
    rows, cols = values.shape
    blocks = rows // BLK
    peak_ref[...] = jnp.full(peak_ref.shape, 1e-30, F32)
    for b in range(blocks):
        peak_ref[b : b + 1, :] = jnp.max(jnp.abs(values[b * BLK : (b + 1) * BLK]), axis=0, keepdims=True)
    level = jnp.ceil(jnp.log2(jnp.maximum(peak_ref[...], 1e-30)) * 256.0) + 1.0
    inverse = jnp.exp2(level * (-1.0 / 256.0)) * QMAX
    for b in range(blocks):
        scaled = values[b * BLK : (b + 1) * BLK] * inverse[b : b + 1, :]
        code = (scaled + MAGIC) - MAGIC
        out_ref[b * BLK : (b + 1) * BLK, :] = code.astype(jnp.int32).astype(jnp.int16)
    out_ref[rows : rows + SROWS, :] = level.astype(jnp.int32).astype(jnp.int16)


def scales(ref, rows):
    level = ref[rows : rows + SROWS, :].astype(jnp.int32).astype(F32)
    return jnp.exp2(level * (1.0 / 256.0)) * (1.0 / QMAX)


def decode(ref, scale, b):
    return ref[b * BLK : (b + 1) * BLK, :].astype(jnp.int32).astype(F32) * scale[b : b + 1, :]


def split_ranks(ranks, keep, is_key, key_ref, value_ref):
    width = ranks.shape[1]
    for mask, ref in ((keep & is_key, key_ref), (keep & jnp.logical_not(is_key), value_ref)):
        part = jnp.where(mask, ranks, 0.0)
        high = part.astype(BF16)
        ref[:, :width] = high
        ref[:, width:] = (part - high.astype(F32)).astype(BF16)


def project_body(with_latest, pf, *refs):
    if with_latest:
        (h, w, down, up, latest, parents, adapters, down_all, up_all,
         q1, q3, q2, own, xk, xv, codes, peaks, xlk, xlv, tile) = refs
    else:
        h, w, down, up, q1, q3, q2, own, xk, xv, codes, peaks, tile = refs
    g = pl.program_id(0)
    rows = h.shape[0]

    @pl.when(g == 0)
    def _():
        ranks = nn(h[...], down[...])
        lane = lax.broadcasted_iota(jnp.int32, ranks.shape, 1)
        split_ranks(ranks, (lane // (2 * RANK)) == pf[3], (lane % (2 * RANK)) < RANK, xk, xv)
        if with_latest:
            ranks = nn(latest[...], down_all[...])
            spot = lax.broadcasted_iota(jnp.int32, (parents.shape[0], adapters.shape[1]), 1)
            mine = jnp.sum(jnp.where(parents[...] == spot, adapters[...], 0), axis=1, keepdims=True)
            lane = lax.broadcasted_iota(jnp.int32, ranks.shape, 1)
            split_ranks(ranks, (lane // (2 * RANK)) == mine, (lane % (2 * RANK)) < RANK, xlk, xlv)

    base = nn(h[...], w[...])
    up2 = jnp.concatenate([up[...], up[...]], axis=0)
    tile[:rows, :HW] = base[:, :HW] + nn(xk[...], up2)
    tile[:rows, HW:] = base[:, HW:] + nn(xv[...], up2)
    if with_latest:
        base = nn(latest[...], w[...])
        up2 = jnp.concatenate([up_all[...], up_all[...]], axis=0)
        tile[rows:, :HW] = base[:, :HW] + nn(xlk[...], up2)
        tile[rows:, HW:] = base[:, HW:] + nn(xlv[...], up2)

    j = g // 2
    cols = pl.ds(pl.multiple_of((g % 2) * 2 * HW, 2 * HW), 2 * HW)

    @pl.when(j == 3)
    def _():
        own[:, cols] = tile[...]

    @pl.when(j < 3)
    def _():
        encode(tile[...], codes, peaks)
        for k, ref in enumerate((q1, q3, q2)):
            @pl.when(j == k)
            def _():
                ref[:, cols] = codes[...]


def project(chunk, rows, pf, hidden, weight, down, up, extra):
    with_latest = extra is not None
    depth = hidden.shape[1]
    total = rows + (extra[0].shape[0] if with_latest else 0)

    def column(g, pf):
        j = g // 2
        off = jnp.where(j == 0, 1, jnp.where(j == 1, 3, jnp.where(j == 2, 2, 0)))
        return ((pf[0] + off) % 4) * 2 + jnp.where(g % 2 == 0, pf[1], 1 - pf[1])

    in_specs = [
        pl.BlockSpec((rows, depth), lambda g, pf: (chunk, 0)),
        pl.BlockSpec((depth, 2 * HW), lambda g, pf: (0, column(g, pf))),
        pl.BlockSpec((depth, 4 * RANK), lambda g, pf: (0, pf[2])),
        pl.BlockSpec((4 * RANK, HW), lambda g, pf: (pf[2], column(g, pf))),
    ]
    args = [hidden, weight, down, up]
    scratch = [
        pltpu.VMEM((rows, 8 * RANK), BF16),
        pltpu.VMEM((rows, 8 * RANK), BF16),
        pltpu.VMEM((total + SROWS, 2 * HW), jnp.int16),
        pltpu.VMEM((SROWS, 2 * HW), F32),
    ]
    if with_latest:
        latest, parents, adapters = extra
        width = down.shape[1]
        in_specs += [
            pl.BlockSpec(latest.shape, lambda g, pf: (0, 0)),
            pl.BlockSpec(parents.shape, lambda g, pf: (0, 0)),
            pl.BlockSpec(adapters.shape, lambda g, pf: (0, 0)),
            pl.BlockSpec((depth, width), lambda g, pf: (0, 0)),
            pl.BlockSpec((width, HW), lambda g, pf: (0, column(g, pf))),
        ]
        args += [latest, parents, adapters, down, up]
        scratch += [pltpu.VMEM((latest.shape[0], 2 * width), BF16)] * 2
    scratch += [pltpu.VMEM((total, 2 * HW), F32)]
    fixed = lambda g, pf: (0, 0)
    code_shape = jax.ShapeDtypeStruct((total + SROWS, 4 * HW), jnp.int16)
    return pl.pallas_call(
        lambda pf, *refs: project_body(with_latest, pf, *refs),
        grid_spec=pltpu.PrefetchScalarGridSpec(
            num_scalar_prefetch=1,
            grid=(8,),
            in_specs=in_specs,
            out_specs=[pl.BlockSpec(code_shape.shape, fixed)] * 3 + [pl.BlockSpec((total, 4 * HW), fixed)],
            scratch_shapes=scratch,
        ),
        out_shape=[code_shape] * 3 + [jax.ShapeDtypeStruct((total, 4 * HW), F32)],
        compiler_params=pltpu.CompilerParams(vmem_limit_bytes=24 * 2**20),
        cost_estimate=pl.CostEstimate(
            flops=2 * total * depth * 16 * HW, bytes_accessed=depth * 32 * HW + total * depth * 2, transcendentals=0
        ),
        name="project",
    )(pf, *args)


def fold_body(a, b, c, own, out, keep, peaks, other):
    rows = own.shape[0]
    sa, sb, sc = scales(a, rows), scales(b, rows), scales(c, rows)
    for k in range(rows // BLK):
        span = slice(k * BLK, (k + 1) * BLK)
        total = own[span, :] + decode(a, sa, k) + decode(b, sb, k) + decode(c, sc, k)
        keep[span, :] = total[:, : 2 * HW]
        other[span, :] = total[:, 2 * HW :]
    encode(other[...], out, peaks)


def fold(a, b, c, own):
    rows = own.shape[0]
    return pl.pallas_call(
        fold_body,
        out_shape=[
            jax.ShapeDtypeStruct((rows + SROWS, 2 * HW), jnp.int16),
            jax.ShapeDtypeStruct((rows, 2 * HW), F32),
        ],
        scratch_shapes=[pltpu.VMEM((SROWS, 2 * HW), F32), pltpu.VMEM((rows, 2 * HW), F32)],
        compiler_params=pltpu.CompilerParams(vmem_limit_bytes=16 * 2**20),
        cost_estimate=pl.CostEstimate(flops=rows * 4 * HW * 8, bytes_accessed=rows * HW * 48, transcendentals=0),
        name="fold",
    )(a, b, c, own)


def dispatch_body(parents, lengths, queries, table, send, turned, cos_out, sin_out, place, counts, spread):
    comps = queries.shape[0]
    group = queries.shape[1] // HW
    spot = lax.broadcasted_iota(jnp.int32, (comps, table.shape[0]), 1)
    pick = (lengths[...] == spot + 1).astype(F32).astype(BF16)
    got = nn(pick, table[...])
    cosine = got[:, :HW] + got[:, HW : 2 * HW] + got[:, 2 * HW : 3 * HW]
    sine = got[:, 3 * HW : 4 * HW] + got[:, 4 * HW : 5 * HW] + got[:, 5 * HW :]
    cos_out[...] = cosine
    sin_out[...] = sine
    for h in range(group):
        part = queries[:, h * HW : (h + 1) * HW].astype(F32)
        turned[pl.ds(h, comps, stride=group), :] = turn(part, cosine, sine).astype(BF16).astype(F32)
    spread[...] = jnp.zeros(spread.shape, F32)

    def clear(i, carry):
        counts[i] = 0
        return carry

    lax.fori_loop(0, counts.shape[0], clear, 0)

    def put(c, carry):
        p = parents[c]
        s = counts[p]
        counts[p] = s + 1
        at = 2 * p + s
        place[c] = at
        to = pl.multiple_of(at * group, group)
        spread[pl.ds(to, group), :] = turned[pl.ds(pl.multiple_of(c * group, group), group), :]
        return carry

    lax.fori_loop(0, comps, put, 0)
    send[...] = spread[...].astype(BF16).reshape(send.shape)


def dispatch(parents, lengths, queries, table, prompts):
    comps = queries.shape[0]
    group = queries.shape[1] // HW
    vmem = pl.BlockSpec(memory_space=pltpu.VMEM)
    smem = pl.BlockSpec(memory_space=pltpu.SMEM)
    return pl.pallas_call(
        dispatch_body,
        in_specs=[smem, vmem, vmem, vmem],
        out_specs=[vmem, vmem, vmem, vmem, smem],
        out_shape=[
            jax.ShapeDtypeStruct((prompts, 2 * group, HW), BF16),
            jax.ShapeDtypeStruct((comps * group, HW), F32),
            jax.ShapeDtypeStruct((comps, HW), F32),
            jax.ShapeDtypeStruct((comps, HW), F32),
            jax.ShapeDtypeStruct((comps,), jnp.int32),
        ],
        scratch_shapes=[pltpu.SMEM((prompts,), jnp.int32), pltpu.VMEM((prompts * 2 * group, HW), F32)],
        compiler_params=pltpu.CompilerParams(vmem_limit_bytes=8 * 2**20),
        cost_estimate=pl.CostEstimate(flops=10**6, bytes_accessed=10**6, transcendentals=0),
        name="dispatch",
    )(parents, lengths, queries, table)


def suffix_body(turned, cache, came, keep, bias, cosine, sine, lengths, latest, out, stats, scores, weights, whole):
    comps = cosine.shape[0]
    first = keep.shape[0] - comps
    group = turned.shape[0] // comps
    scale = HW ** -0.5
    whole[...] = keep[first:, :] + bias[...] + decode(came, scales(came, keep.shape[0]), first // BLK)
    key = turn(whole[:, :HW], cosine[...], sine[...]).astype(BF16)
    value = whole[:, HW:].astype(BF16)
    latest[:, :HW] = key
    latest[:, HW:] = value

    def wide(rows):
        return jnp.broadcast_to(rows[:, None, :], (comps, group, HW)).reshape(comps * group, HW)

    for c in range(comps):
        span = slice(c * group, (c + 1) * group)
        scores[span, :] = nt(turned[span, :].astype(BF16), cache[c, :, :HW])
    own_score = jnp.sum(turned[...] * wide(key.astype(F32)), axis=1, keepdims=True) * scale
    slot = lax.broadcasted_iota(jnp.int32, scores.shape, 1)
    masked = jnp.where(slot < lengths[...], scores[...] * scale, NEG)
    top = jnp.maximum(jnp.max(masked, axis=1, keepdims=True), own_score)
    weight = jnp.exp(masked - top)
    own_weight = jnp.exp(own_score - top)
    total = jnp.sum(weight, axis=1, keepdims=True) + own_weight
    weights[...] = weight
    for c in range(comps):
        span = slice(c * group, (c + 1) * group)
        out[span, :] = nn(weights[span, :].astype(BF16), cache[c, :, HW:])
    out[...] = out[...] + own_weight.astype(BF16).astype(F32) * wide(value.astype(F32))
    stats[...] = jnp.where(slot < HW // 2, top, total)


def suffix(turned, cache, came, keep, bias, cosine, sine, lengths):
    comps = cosine.shape[0]
    rows = turned.shape[0]
    return pl.pallas_call(
        suffix_body,
        out_shape=[
            jax.ShapeDtypeStruct((comps, 2 * HW), BF16),
            jax.ShapeDtypeStruct((rows, HW), F32),
            jax.ShapeDtypeStruct((rows, HW), F32),
        ],
        scratch_shapes=[pltpu.VMEM((rows, HW), F32), pltpu.VMEM((rows, HW), F32), pltpu.VMEM((comps, 2 * HW), F32)],
        compiler_params=pltpu.CompilerParams(vmem_limit_bytes=16 * 2**20),
        cost_estimate=pl.CostEstimate(flops=10**7, bytes_accessed=10**7, transcendentals=0),
        name="suffix",
    )(turned, cache, came, keep, bias, cosine, sine, lengths)


def prefix_body(chunks, queries, bias, cosine, sine, *refs):
    came, keep = refs[:chunks], refs[chunks : 2 * chunks]
    kv, out = refs[2 * chunks :]
    length = kv.shape[0]
    rows = length // chunks
    for i in range(chunks):
        scale = scales(came[i], keep[i].shape[0])
        for k in range(rows // BLK):
            span = slice(i * rows + k * BLK, i * rows + (k + 1) * BLK)
            total = keep[i][k * BLK : (k + 1) * BLK, :] + decode(came[i], scale, k) + bias[...]
            kv[span, :HW] = turn(total[:, :HW], cosine[span, :], sine[span, :]).astype(BF16)
            kv[span, HW:] = total[:, HW:].astype(BF16)
    prompts, per, _ = queries.shape
    step = 8
    for s in range(0, prompts, step):
        q = queries[s : s + step].reshape(step * per, HW)
        scores = nt(q, kv[:, :HW]) * (HW ** -0.5)
        top = jnp.max(scores, axis=1, keepdims=True)
        weight = jnp.exp(scores - top)
        total = jnp.sum(weight, axis=1, keepdims=True)
        part = nn(weight.astype(BF16), kv[:, HW:])
        out[s : s + step, :per, :] = part.reshape(step, per, HW)
        lane = lax.broadcasted_iota(jnp.int32, (step * per, HW), 1)
        row = lax.broadcasted_iota(jnp.int32, (step * per, HW), 0) % per
        stat = jnp.where(lane == row, top, 0.0) + jnp.where(lane == row + per, total, 0.0)
        stat = jnp.sum(stat.reshape(step, per, HW), axis=1, keepdims=True)
        out[s : s + step, per:, :] = jnp.broadcast_to(stat, (step, 8, HW))


def prefix(queries, bias, cosine, sine, came, keep, length):
    chunks = len(came)
    prompts, per, _ = queries.shape
    return pl.pallas_call(
        lambda *refs: prefix_body(chunks, *refs),
        out_shape=[
            jax.ShapeDtypeStruct((length, 2 * HW), BF16),
            jax.ShapeDtypeStruct((prompts, per + 8, HW), F32),
        ],
        compiler_params=pltpu.CompilerParams(vmem_limit_bytes=24 * 2**20),
        cost_estimate=pl.CostEstimate(flops=2 * 10**8, bytes_accessed=10**7, transcendentals=10**6),
        name="prefix",
    )(queries, bias, cosine, sine, *came, *keep)


def merge_body(place, back, out, stats, attn, top_all, total_all, joined):
    prompts, per, _ = back.shape
    per -= 8
    rows = out.shape[0]
    comps = attn.shape[0]
    group = rows // comps
    lane = lax.broadcasted_iota(jnp.int32, (prompts * per, HW), 1)
    row = lax.broadcasted_iota(jnp.int32, (prompts * per, HW), 0) % per
    wide = jnp.broadcast_to(back[:, per : per + 1, :], (prompts, per, HW)).reshape(prompts * per, HW)
    top_all[...] = jnp.broadcast_to(
        jnp.sum(jnp.where(lane == row, wide, 0.0), axis=1, keepdims=True), top_all.shape)
    total_all[...] = jnp.broadcast_to(
        jnp.sum(jnp.where(lane == row + per, wide, 0.0), axis=1, keepdims=True), total_all.shape)

    for c in range(comps):
        at = place[c]
        src = pl.ds(pl.multiple_of(at * group, group), group)
        top_p, total_p = top_all[src, :], total_all[src, :]
        out_p = back[at // 2, pl.ds(pl.multiple_of((at % 2) * group, group), group), :]
        span = slice(c * group, (c + 1) * group)
        stat = stats[span, :]
        top_s, total_s = stat[:, :1], stat[:, HW // 2 : HW // 2 + 1]
        top = jnp.maximum(top_p, top_s)
        alpha = jnp.exp(top_p - top)
        beta = jnp.exp(top_s - top)
        joined[span, :] = (alpha * out_p + beta * out[span, :]) / (alpha * total_p + beta * total_s)
    for h in range(group):
        attn[:, h * HW : (h + 1) * HW] = joined[pl.ds(h, comps, stride=group), :].astype(BF16)


def merge(place, back, out, stats, comps):
    rows = out.shape[0]
    slots = back.shape[0] * (back.shape[1] - 8)
    vmem = pl.BlockSpec(memory_space=pltpu.VMEM)
    smem = pl.BlockSpec(memory_space=pltpu.SMEM)
    return pl.pallas_call(
        merge_body,
        in_specs=[smem, vmem, vmem, vmem],
        out_specs=vmem,
        out_shape=jax.ShapeDtypeStruct((comps, rows // comps * HW), BF16),
        scratch_shapes=[pltpu.VMEM((slots, HW), F32), pltpu.VMEM((slots, HW), F32), pltpu.VMEM((rows, HW), F32)],
        compiler_params=pltpu.CompilerParams(vmem_limit_bytes=8 * 2**20),
        cost_estimate=pl.CostEstimate(flops=10**6, bytes_accessed=10**6, transcendentals=10**5),
        name="merge",
    )(place, back, out, stats)


def on_device(
    prefix_hidden_states, latest_hidden, queries, suffix_key_cache, key_value_weight, key_value_bias,
    adapter_down_weight, adapter_up_weight, parents, adapter_index, suffix_length_count,
):
    rep = lax.axis_index("rep")
    tp = lax.axis_index("tp")
    y, z = tp // 2, tp % 2
    length = prefix_hidden_states.shape[1]
    comps = latest_hidden.shape[0]
    prompts = adapter_index.shape[0]
    group = queries.shape[1] // HW
    rows = length // CHUNKS
    along_y = lambda d: [(a * 2 + b, ((a + d) % 4) * 2 + b) for a in range(4) for b in range(2)]
    along_z = [(a * 2 + b, a * 2 + 1 - b) for a in range(4) for b in range(2)]

    adapter = lax.dynamic_index_in_dim(adapter_index, rep, 0, keepdims=False)
    pf = jnp.stack([y, z, adapter // 2, adapter % 2]).astype(jnp.int32)
    hidden = prefix_hidden_states[0]
    sent, own = [], []
    for i in range(CHUNKS):
        extra = (latest_hidden, parents, adapter_index.reshape(1, -1)) if i == 0 else None
        q1, q3, q2, mine = project(i, rows, pf, hidden, key_value_weight, adapter_down_weight, adapter_up_weight, extra)
        sent.append([
            lax.ppermute(q1, "tp", along_y(1)),
            lax.ppermute(q3, "tp", along_y(3)),
            lax.ppermute(q2, "tp", along_y(2)),
        ])
        own.append(mine)

    cos_t, sin_t = rope_tables(length + 1, suffix_key_cache.shape[1])
    table = jnp.asarray(np.concatenate(three_parts(cos_t) + three_parts(sin_t), 1))
    to_prompts, turned, cos_new, sin_new, place = dispatch(
        parents[:, 0], suffix_length_count.reshape(comps, 1), queries, table, prompts)
    here = lax.all_to_all(to_prompts, "rep", 0, 0, tiled=True)

    came, keep = [], []
    for i in range(CHUNKS):
        code, kept = fold(*sent[i], own[i])
        came.append(lax.ppermute(code, "tp", along_z))
        keep.append(kept)

    bias = key_value_bias.astype(F32).reshape(1, 2 * HW)
    latest_key_value, out_s, stats = suffix(
        turned, suffix_key_cache, came[0], keep[0], bias, cos_new, sin_new,
        jnp.repeat(suffix_length_count, group).reshape(comps * group, 1))
    cos_p, sin_p = rope_tables(0, length)
    prefix_kv, part = prefix(here, bias, jnp.asarray(cos_p), jnp.asarray(sin_p), came, keep, length)
    back = lax.all_to_all(part, "rep", 0, 0, tiled=True)
    attn_out = merge(place, back, out_s, stats, comps)
    return prefix_kv[None], latest_key_value, attn_out


def solution(mesh):
    in_specs = (
        P("rep", None, "tp"), P("rep", "tp"), P("rep", "tp"), P("rep", None, "tp"), P("tp", None), P("tp"),
        P("tp", None), P(), P("rep", None), P(), P("rep"),
    )
    out_specs = (P("rep", None, "tp"), P("rep", "tp"), P("rep", "tp"))
    return jax.shard_map(on_device, mesh=mesh, in_specs=in_specs, out_specs=out_specs, check_vma=False)
```

time: 501 us -> 120 us (0.24)
  waiting for transfers between devices: 354 us -> 28.7 us
  blocking collectives: 39.5 us -> 0 us
  starting transfers between devices: 0.16 us -> 37.4 us
  local copies, waits for them, and re-layouts: 52.6 us -> 15.9 us
  Pallas kernels: 0 us -> 34.1 us
  matrix products: 24.2 us -> 0 us
  between operations: 16.8 us -> 3.39 us
  other arithmetic: 12.5 us -> 0.08 us
    reduce_scatter x2 -> x0, waiting for transfers between devices: 185 us -> none  [the longest x1 155 us: reduce_terms(): lax.psum_scatter(first_term, 'tp', scatter_dimension=1, tiled=True)]
    psum x1 -> x0, waiting for transfers between devices: 90.8 us -> none  [on_device(): rank_prefix, rank_new = lax.psum((part_prefix, part_new), 'tp')]
    all_gather x1 -> x0, waiting for transfers between devices: 78.2 us -> none  [on_device(): all_prefix = lax.all_gather(prefix_local[None], 'rep', axis=0, tiled=True)]
    gather x3 -> x0, local copies, waits for them, and re-layouts: 44.6 us -> none  [on_device(): jnp.take(all_prefix, parent, axis=0)]
    psum x1 -> x0, blocking collectives: 39.5 us -> none  [on_device(): rank_prefix, rank_new = lax.psum((part_prefix, part_new), 'tp')]
    pallas_call x0 -> x10, Pallas kernels: none -> 34.1 us  [the longest x3 20.8 us: project(): pl.pallas_call(lambda pf, *refs: project_body(with_latest, pf, *refs), gr...]
    dot_general x13 -> x0, matrix products: 24.2 us -> none  [the longest x1 7.5 us: on_device(): jnp.dot(rows_prefix, key_value_weight, preferred_element_type=jnp.float32)]
    ppermute x0 -> x12, starting transfers between devices: none -> 20.1 us  [the longest x3 9.59 us: on_device(): came.append(lax.ppermute(code, 'tp', along_z))]
  transfers between devices with their start and end apart: 4 -> 14, of which waited for: 4 -> 4; matrix products, arithmetic and copies ran while one was open for 6% -> 0% of each run, Pallas kernels for 0% -> 18%
where the time goes in v1:
time: 120 us
  starting transfers between devices  37.4 us (31%)
  Pallas kernels  34.1 us (28%)
  waiting for transfers between devices  28.7 us (24%)
  local copies, waits for them, and re-layouts  15.9 us (13%)
  between operations  3.39 us (3%)
    pallas_call x3, Pallas kernels, project(): pl.pallas_call(lambda pf, *refs: project_body(with_latest, pf, *refs), gr...  20.8 us
    unnamed x41, local copies, waits for them, and re-layouts  14.5 us
    ppermute x3, waiting for transfers between devices, on_device(): came.append(lax.ppermute(code, 'tp', along_z))  13 us
    all_to_all x1, waiting for transfers between devices, on_device(): back = lax.all_to_all(part, 'rep', 0, 0, tiled=True)  11.8 us
    all_to_all x1, starting transfers between devices, on_device(): here = lax.all_to_all(to_prompts, 'rep', 0, 0, tiled=True)  11.6 us
    ppermute x3, starting transfers between devices, on_device(): came.append(lax.ppermute(code, 'tp', along_z))  9.59 us
    all_to_all x1, starting transfers between devices, on_device(): back = lax.all_to_all(part, 'rep', 0, 0, tiled=True)  5.6 us
    pallas_call x3, Pallas kernels, fold(): pl.pallas_call(fold_body, out_shape=[jax.ShapeDtypeStruct((rows + SROWS,...  5.36 us
  transfers between devices with their start and end apart: 14, of which 4 were waited for; matrix products, arithmetic and copies ran while one was open for 0% of the time, Pallas kernels for 18%

profile of v1, /device:TPU:1, one launch (start us, length us, event | category | flops | bytes accessed | tf_op | source)
XLA Modules:
  0.0 119.5 jit_solution(10319740513038876138)
XLA Ops:
  0.6 1.2 %dynamic_slice.4 = s32[1]{0:T(128)} dynamic-slice(s32[32]{0:T(128)} %param.23, s32[]{:T(128)S(6)} %select_n.24), dynamic_slice_sizes={1} | dynamic-slice | bytes 12 | tf_op jit(solution)/shard_map/jit(dynamic_index_in_dim)/dynamic_slice | solution.py:428
  4.5 0.7 copy.20.refs_5_
  5.2 0.1 pad_add_fusion.pf
  5.3 2.2 %copy-done = bf16[1024,2048]{1,0:T(8,128)(2,1)S(1)} copy-done((bf16[1024,2048]{1,0:T(8,128)(2,1)S(1)}, bf16[1024,2048]{1,0:T(8,128)(2,1)}, u32[]{:S(2)}) %copy-start) | copy-done | bytes 4194328
  7.5 1.2 %copy-done.1 = bf16[1024,512]{1,0:T(8,128)(2,1)S(1)} copy-done((bf16[1024,512]{1,0:T(8,128)(2,1)S(1)}, bf16[1024,512]{1,0:T(8,128)(2,1)}, u32[]{:S(2)}) %copy-start.1) | copy-done | bytes 1048600
  8.7 1.2 %copy-done.2 = bf16[512,1024]{1,0:T(8,128)(2,1)S(1)} copy-done((bf16[512,1024]{1,0:T(8,128)(2,1)S(1)}, bf16[512,1024]{1,0:T(8,128)(2,1)}, u32[]{:S(2)}) %copy-start.2) | copy-done | bytes 1048600
  10.0 1.4 %copy-done.3 = bf16[1,768,1024]{2,1,0:T(8,128)(2,1)S(1)} copy-done((bf16[1,768,1024]{2,1,0:T(8,128)(2,1)S(1)}, bf16[1,768,1024]{2,1,0:T(8,128)(2,1)}, u32[]{:S(2)}) %copy-start.3) | copy-done | bytes 1572888
  11.4 0.8 copy-done.15
  12.2 0.7 copy-done.17
  12.9 7.3 %project.3 = (s16[304,512]{1,0:T(8,128)(2,1)S(1)}, s16[304,512]{1,0:T(8,128)(2,1)S(1)}, s16[304,512]{1,0:T(8,128)(2,1)S(1)}, f32[288,512]{1,0:T(8,128)S(1)}) custom-call(s32[4]{0:T(128)S(1)} %pad_add_fusion.pf, bf16[768,1024]{1,0:T(8,128)(2,1)S(1)} %bitcast.11, bf16[1024,2048]{1,0:T(8,128)(2,1)S(1)} %copy-done, bf16[1024,512]{1,0:T(8,128)(2,1)S(1)} %copy-done.1, ...), custom_call_target="tpu_custom_call" | custom-call | flops 1207959552 | bytes 4784128 | tf_op jit(solution)/shard_map/project/pallas_call | solution.py:171
  20.2 2.2 %collective-permute-start = (s16[304,512]{1,0:T(8,128)(2,1)S(1)}, s16[304,512]{1,0:T(8,128)(2,1)S(1)}, u32[]{:S(2)}, u32[]{:S(2)}) collective-permute-start(s16[304,512]{1,0:T(8,128)(2,1)S(1)} %get-tuple-element.32), channel_id=1, source_target_pairs={{0,2},{1,3},{2,4},{3,5},{4,6},{5,7},{6,0},{7,1},{8,10},{9,11},{10,... | collective-permute-start | bytes 933896 | tf_op jit(solution)/shard_map/ppermute | solution.py:436
  22.4 1.5 %collective-permute-start.1 = (s16[304,512]{1,0:T(8,128)(2,1)S(1)}, s16[304,512]{1,0:T(8,128)(2,1)S(1)}, u32[]{:S(2)}, u32[]{:S(2)}) collective-permute-start(s16[304,512]{1,0:T(8,128)(2,1)S(1)} %get-tuple-element.33), channel_id=1, source_target_pairs={{0,6},{1,7},{2,0},{3,1},{4,2},{5,3},{6,4},{7,5},{8,14},{9,15},{10,... | collective-permute-start | bytes 933896 | tf_op jit(solution)/shard_map/ppermute | solution.py:437
  23.9 1.6 %collective-permute-start.2 = (s16[304,512]{1,0:T(8,128)(2,1)S(1)}, s16[304,512]{1,0:T(8,128)(2,1)S(1)}, u32[]{:S(2)}, u32[]{:S(2)}) collective-permute-start(s16[304,512]{1,0:T(8,128)(2,1)S(1)} %get-tuple-element.34), channel_id=1, source_target_pairs={{0,4},{1,5},{2,6},{3,7},{4,0},{5,1},{6,2},{7,3},{8,12},{9,13},{10,... | collective-permute-start | bytes 933896 | tf_op jit(solution)/shard_map/ppermute | solution.py:438
  25.4 6.7 %project.5 = (s16[272,512]{1,0:T(8,128)(2,1)}, s16[272,512]{1,0:T(8,128)(2,1)}, s16[272,512]{1,0:T(8,128)(2,1)S(1)}, f32[256,512]{1,0:T(8,128)S(1)}) custom-call(s32[4]{0:T(128)S(1)} %pad_add_fusion.pf, bf16[768,1024]{1,0:T(8,128)(2,1)S(1)} %bitcast.12, bf16[1024,2048]{1,0:T(8,128)(2,1)S(1)} %copy-done, bf16[1024,512]{1,0:T(8,128)(2,1)S(1)} %copy-done.1, ...), custom_call_target="tpu_custom_call" | custom-call | flops 1073741824 | bytes 4718592 | tf_op jit(solution)/shard_map/project/pallas_call | solution.py:171
  32.2 1.4 %collective-permute-start.10 = (s16[272,512]{1,0:T(8,128)(2,1)S(1)}, s16[272,512]{1,0:T(8,128)(2,1)S(1)}, u32[]{:S(2)}, u32[]{:S(2)}) collective-permute-start(s16[272,512]{1,0:T(8,128)(2,1)S(1)} %get-tuple-element.44), channel_id=1, source_target_pairs={{0,4},{1,5},{2,6},{3,7},{4,0},{5,1},{6,2},{7,3},{8,12},{9,13},{10,... | collective-permute-start | bytes 835592 | tf_op jit(solution)/shard_map/ppermute | solution.py:438
  33.6 0.1 collective-permute-start.8
  33.7 6.8 %project.4 = (s16[272,512]{1,0:T(8,128)(2,1)}, s16[272,512]{1,0:T(8,128)(2,1)}, s16[272,512]{1,0:T(8,128)(2,1)}, f32[256,512]{1,0:T(8,128)S(1)}) custom-call(s32[4]{0:T(128)S(1)} %pad_add_fusion.pf, bf16[768,1024]{1,0:T(8,128)(2,1)S(1)} %bitcast.13, bf16[1024,2048]{1,0:T(8,128)(2,1)S(1)} %copy-done, bf16[1024,512]{1,0:T(8,128)(2,1)S(1)} %copy-done.1, ...), custom_call_target="tpu_custom_call" | custom-call | flops 1073741824 | bytes 4718592 | tf_op jit(solution)/shard_map/project/pallas_call | solution.py:171
  40.5 3.9 %collective-permute-done.10.c = s16[272,512]{1,0:T(8,128)(2,1)S(1)} collective-permute-done((s16[272,512]{1,0:T(8,128)(2,1)S(1)}, s16[272,512]{1,0:T(8,128)(2,1)S(1)}, u32[]{:S(2)}, u32[]{:S(2)}) %collective-permute-start.10) | collective-permute-done | bytes 278560 | tf_op jit(solution)/shard_map/ppermute | solution.py:438
  44.4 0.7 collective-permute-start.9
  45.1 0.0 collective-permute-done.a
  45.1 0.8 collective-permute-start.4
  45.9 0.0 collective-permute-done.1.b
  45.9 1.9 %collective-permute-start.5 = (s16[272,512]{1,0:T(8,128)(2,1)}, s16[272,512]{1,0:T(8,128)(2,1)}, u32[]{:S(2)}, u32[]{:S(2)}) collective-permute-start(s16[272,512]{1,0:T(8,128)(2,1)} %get-tuple-element.38), channel_id=1, source_target_pairs={{0,6},{1,7},{2,0},{3,1},{4,2},{5,3},{6,4},{7,5},{8,14},{9,15},{10,... | collective-permute-start | bytes 835592 | tf_op jit(solution)/shard_map/ppermute | solution.py:437
  47.8 0.0 collective-permute-done.2.c
  47.8 0.4 collective-permute-start.6
  48.2 0.0 copy-done.18
  48.2 0.1 copy.19.lengths
  48.3 0.0 copy-done.11
  48.3 0.0 copy-done.14
  48.3 1.9 %dispatch.1 = (bf16[32,16,128]{2,1,0:T(8,128)(2,1)}, f32[256,128]{1,0:T(8,128)S(1)}, f32[32,128]{1,0:T(8,128)S(1)}, f32[32,128]{1,0:T(8,128)S(1)}, s32[32]{0:T(128)S(1)}) custom-call(s32[32]{0:T(128)S(1)} %bitcast.16, s32[32,1]{1,0:T(8,128)S(1)} %copy.19.lengths, bf16[32,1024]{1,0:T(8,128)(2,1)S(1)} %copy-done.14, bf16[128,768]{1,0:T(8,128)(2,1)S(1)} %copy-done.11), custom_call_target="tpu_custom_call" | custom-call | flops 1000000 | bytes 1000000 | tf_op jit(solution)/shard_map/dispatch/pallas_call | solution.py:255
  50.2 0.0 copy-start.12
  50.3 0.6 copy-done.12
  50.9 0.0 copy-done.7
  50.9 11.6 %all-to-all-start = ((bf16[32,16,128]{2,1,0:T(8,128)(2,1)}), bf16[32,16,128]{2,1,0:T(8,128)(2,1)S(1)}, u32[]{:S(2)}, u32[]{:S(2)}) async-start(bf16[32,16,128]{2,1,0:T(8,128)(2,1)} %get-tuple-element.31), calls=%async_computation | async-start | bytes 262144 | tf_op jit(solution)/shard_map/all_to_all | solution.py:446
  62.5 0.0 copy-start.19
  62.6 1.0 fold.3
  63.6 0.0 collective-permute-done.8.a
  63.6 4.2 %collective-permute-start.3 = (s16[304,256]{1,0:T(8,128)(2,1)}, s16[304,256]{1,0:T(8,128)(2,1)S(1)}, u32[]{:S(2)}, u32[]{:S(2)}) collective-permute-start(s16[304,256]{1,0:T(8,128)(2,1)} %get-tuple-element.36), channel_id=1, source_target_pairs={{0,1},{1,0},{2,3},{3,2},{4,5},{5,4},{6,7},{7,6},{8,9},{9,8},{10,11... | collective-permute-start | bytes 466952 | tf_op jit(solution)/shard_map/ppermute | solution.py:451
  67.8 0.0 collective-permute-done.9.b
  67.8 1.0 copy-done.8
  68.8 2.0 %fold.5 = (s16[272,256]{1,0:T(8,128)(2,1)}, f32[256,256]{1,0:T(8,128)S(1)}) custom-call(s16[272,512]{1,0:T(8,128)(2,1)} %collective-permute-done.8.a, s16[272,512]{1,0:T(8,128)(2,1)} %collective-permute-done.9.b, s16[272,512]{1,0:T(8,128)(2,1)S(1)} %copy-done.8, f32[256,512]{1,0:T(8,128)S(1)} %get-tuple-element.45.own), custom_call_target="tpu_custom_call" | custom-call | flops 1048576 | bytes 1572864 | tf_op jit(solution)/shard_map/fold/pallas_call | solution.py:202
  70.8 1.2 collective-permute-start.11
  72.0 0.0 collective-permute-done.4.a
  72.0 0.0 collective-permute-done.5.b
  72.0 0.0 collective-permute-done.6.c
  72.0 0.0 copy-start.4
  72.0 2.3 %fold.4 = (s16[272,256]{1,0:T(8,128)(2,1)}, f32[256,256]{1,0:T(8,128)S(1)}) custom-call(s16[272,512]{1,0:T(8,128)(2,1)} %collective-permute-done.4.a, s16[272,512]{1,0:T(8,128)(2,1)} %collective-permute-done.5.b, s16[272,512]{1,0:T(8,128)(2,1)} %collective-permute-done.6.c, f32[256,512]{1,0:T(8,128)S(1)} %get-tuple-element.40.own), custom_call_target="tpu_custom_call" | custom-call | flops 1048576 | bytes 1572864 | tf_op jit(solution)/shard_map/fold/pallas_call | solution.py:202
  74.3 0.7 copy-done.9
  75.0 4.2 %collective-permute-start.7 = (s16[272,256]{1,0:T(8,128)(2,1)}, s16[272,256]{1,0:T(8,128)(2,1)S(1)}, u32[]{:S(2)}, u32[]{:S(2)}) collective-permute-start(s16[272,256]{1,0:T(8,128)(2,1)} %get-tuple-element.41), channel_id=1, source_target_pairs={{0,1},{1,0},{2,3},{3,2},{4,5},{5,4},{6,7},{7,6},{8,9},{9,8},{10,11... | collective-permute-start | bytes 417800 | tf_op jit(solution)/shard_map/ppermute | solution.py:451
  79.2 0.0 all-to-all-done.refs_0_
  79.2 7.6 %collective-permute-done.11.refs_6_ = s16[272,256]{1,0:T(8,128)(2,1)} collective-permute-done((s16[272,256]{1,0:T(8,128)(2,1)}, s16[272,256]{1,0:T(8,128)(2,1)}, u32[]{:S(2)}, u32[]{:S(2)}) %collective-permute-start.11) | collective-permute-done | bytes 139296 | tf_op jit(solution)/shard_map/ppermute | solution.py:451
  86.8 5.5 %collective-permute-done.7.refs_5_ = s16[272,256]{1,0:T(8,128)(2,1)S(1)} collective-permute-done((s16[272,256]{1,0:T(8,128)(2,1)}, s16[272,256]{1,0:T(8,128)(2,1)S(1)}, u32[]{:S(2)}, u32[]{:S(2)}) %collective-permute-start.7) | collective-permute-done | bytes 139296 | tf_op jit(solution)/shard_map/ppermute | solution.py:451
  92.2 0.0 collective-permute-done.3.refs_4_.came
  92.2 1.0 copy-done.5
  93.2 1.0 copy-done.6
  94.2 0.9 copy-done.10
  95.2 3.3 %prefix.1 = (bf16[768,256]{1,0:T(8,128)(2,1)}, f32[32,24,128]{2,1,0:T(8,128)}) custom-call(bf16[32,16,128]{2,1,0:T(8,128)(2,1)S(1)} %all-to-all-done.refs_0_, f32[1,256]{1,0:T(1,128)S(1)} %bitcast.14, f32[768,128]{1,0:T(8,128)S(1)} %copy-done.5, f32[768,128]{1,0:T(8,128)S(1)} %copy-done.6, s16[304,256]{1,0:T(8,128)(2,1)S(1)} %collective-permute-done.3.refs_4_.came, ...), custom_call_target="tpu_custom_call" | custom-call | flops 200000000 | bytes 10000000 | tf_op jit(solution)/shard_map/prefix/pallas_call | solution.py:354
  98.5 5.6 %all-to-all-start.1 = ((f32[32,24,128]{2,1,0:T(8,128)}), f32[32,24,128]{2,1,0:T(8,128)S(1)}, u32[]{:S(2)}, u32[]{:S(2)}) async-start(f32[32,24,128]{2,1,0:T(8,128)} %get-tuple-element.56), calls=%async_computation.1 | async-start | bytes 786432 | tf_op jit(solution)/shard_map/all_to_all | solution.py:460
  104.1 0.1 broadcast_in_dim.7
  104.2 0.1 reshape_reshape.4.lengths
  104.3 0.9 copy-done.13
  105.2 0.9 suffix.1
  106.1 11.8 %all-to-all-done.1.back = f32[32,24,128]{2,1,0:T(8,128)S(1)} async-done(((f32[32,24,128]{2,1,0:T(8,128)}), f32[32,24,128]{2,1,0:T(8,128)S(1)}, u32[]{:S(2)}, u32[]{:S(2)}) %all-to-all-start.1) | async-done | bytes 393248 | tf_op jit(solution)/shard_map/all_to_all | solution.py:460
  117.9 1.6 %merge.1 = bf16[32,1024]{1,0:T(8,128)(2,1)} custom-call(s32[32]{0:T(128)S(1)} %get-tuple-element.55.place, f32[32,24,128]{2,1,0:T(8,128)S(1)} %all-to-all-done.1.back, f32[256,128]{1,0:T(8,128)S(1)} %get-tuple-element.57.out, f32[256,128]{1,0:T(8,128)S(1)} %get-tuple-element.58.stats), custom_call_target="tpu_custom_call" | custom-call | flops 1000000 | bytes 1000000 | tf_op jit(solution)/shard_map/merge/pallas_call | solution.py:401
  (21 shorter events, 0.0 us)
Async XLA Ops:
  5.3 2.2 %copy-start = (bf16[1024,2048]{1,0:T(8,128)(2,1)S(1)}, bf16[1024,2048]{1,0:T(8,128)(2,1)}, u32[]{:S(2)}) copy-start(bf16[1024,2048]{1,0:T(8,128)(2,1)} %refs_1_.5) | copy-start | bytes 12582916
  7.5 1.2 %copy-start.1 = (bf16[1024,512]{1,0:T(8,128)(2,1)S(1)}, bf16[1024,512]{1,0:T(8,128)(2,1)}, u32[]{:S(2)}) copy-start(bf16[1024,512]{1,0:T(8,128)(2,1)} %refs_2_.6) | copy-start | bytes 3145732
  8.7 1.2 %copy-start.2 = (bf16[512,1024]{1,0:T(8,128)(2,1)S(1)}, bf16[512,1024]{1,0:T(8,128)(2,1)}, u32[]{:S(2)}) copy-start(bf16[512,1024]{1,0:T(8,128)(2,1)} %refs_3_.6) | copy-start | bytes 3145732
  10.0 1.4 %copy-start.3 = (bf16[1,768,1024]{2,1,0:T(8,128)(2,1)S(1)}, bf16[1,768,1024]{2,1,0:T(8,128)(2,1)}, u32[]{:S(2)}) copy-start(bf16[1,768,1024]{2,1,0:T(8,128)(2,1)} %param.14) | copy-start | bytes 4718596
  11.4 0.8 copy-start.15
  12.2 0.7 copy-start.17
  20.2 24.9 %collective-permute-start = (s16[304,512]{1,0:T(8,128)(2,1)S(1)}, s16[304,512]{1,0:T(8,128)(2,1)S(1)}, u32[]{:S(2)}, u32[]{:S(2)}) collective-permute-start(s16[304,512]{1,0:T(8,128)(2,1)S(1)} %get-tuple-element.32), channel_id=1, source_target_pairs={{0,2},{1,3},{2,4},{3,5},{4,6},{5,7},{6,0},{7,1},{8,10},{9,11},{10,... | collective-permute-start | bytes 933896 | tf_op jit(solution)/shard_map/ppermute | solution.py:436
  22.4 23.5 %collective-permute-start.1 = (s16[304,512]{1,0:T(8,128)(2,1)S(1)}, s16[304,512]{1,0:T(8,128)(2,1)S(1)}, u32[]{:S(2)}, u32[]{:S(2)}) collective-permute-start(s16[304,512]{1,0:T(8,128)(2,1)S(1)} %get-tuple-element.33), channel_id=1, source_target_pairs={{0,6},{1,7},{2,0},{3,1},{4,2},{5,3},{6,4},{7,5},{8,14},{9,15},{10,... | collective-permute-start | bytes 933896 | tf_op jit(solution)/shard_map/ppermute | solution.py:437
  23.9 23.9 %collective-permute-start.2 = (s16[304,512]{1,0:T(8,128)(2,1)S(1)}, s16[304,512]{1,0:T(8,128)(2,1)S(1)}, u32[]{:S(2)}, u32[]{:S(2)}) collective-permute-start(s16[304,512]{1,0:T(8,128)(2,1)S(1)} %get-tuple-element.34), channel_id=1, source_target_pairs={{0,4},{1,5},{2,6},{3,7},{4,0},{5,1},{6,2},{7,3},{8,12},{9,13},{10,... | collective-permute-start | bytes 933896 | tf_op jit(solution)/shard_map/ppermute | solution.py:438
  32.2 12.3 %collective-permute-start.10 = (s16[272,512]{1,0:T(8,128)(2,1)S(1)}, s16[272,512]{1,0:T(8,128)(2,1)S(1)}, u32[]{:S(2)}, u32[]{:S(2)}) collective-permute-start(s16[272,512]{1,0:T(8,128)(2,1)S(1)} %get-tuple-element.44), channel_id=1, source_target_pairs={{0,4},{1,5},{2,6},{3,7},{4,0},{5,1},{6,2},{7,3},{8,12},{9,13},{10,... | collective-permute-start | bytes 835592 | tf_op jit(solution)/shard_map/ppermute | solution.py:438
  33.6 14.6 %copy-start.18 = (s32[32]{0:T(128)S(1)}, s32[32]{0:T(128)}, u32[]{:S(2)}) copy-start(s32[32]{0:T(128)} %param.24) | copy-start | bytes 388
  33.6 14.7 %copy-start.11 = (bf16[128,768]{1,0:T(8,128)(2,1)S(1)}, bf16[128,768]{1,0:T(8,128)(2,1)}, u32[]{:S(2)}) copy-start(bf16[128,768]{1,0:T(8,128)(2,1)} %constant.55.clone.table) | copy-start | bytes 589828
  33.6 14.7 %copy-start.14 = (bf16[32,1024]{1,0:T(8,128)(2,1)S(1)}, bf16[32,1024]{1,0:T(8,128)(2,1)}, u32[]{:S(2)}) copy-start(bf16[32,1024]{1,0:T(8,128)(2,1)} %queries.1) | copy-start | bytes 196612
  33.6 14.7 %copy-start.16 = (s32[32,1]{0,1:T(1,128)S(1)}, s32[32,1]{0,1:T(1,128)}, u32[]{:S(2)}) copy-start(s32[32,1]{0,1:T(1,128)} %param.22) | copy-start | bytes 388
  33.6 30.0 %collective-permute-start.8 = (s16[272,512]{1,0:T(8,128)(2,1)}, s16[272,512]{1,0:T(8,128)(2,1)}, u32[]{:S(2)}, u32[]{:S(2)}) collective-permute-start(s16[272,512]{1,0:T(8,128)(2,1)} %get-tuple-element.42), channel_id=1, source_target_pairs={{0,2},{1,3},{2,4},{3,5},{4,6},{5,7},{6,0},{7,1},{8,10},{9,11},{10,... | collective-permute-start | bytes 835592 | tf_op jit(solution)/shard_map/ppermute | solution.py:436
  44.4 6.5 %copy-start.7 = (s16[272,512]{1,0:T(8,128)(2,1)}, s16[272,512]{1,0:T(8,128)(2,1)S(1)}, u32[]{:S(2)}) copy-start(s16[272,512]{1,0:T(8,128)(2,1)S(1)} %collective-permute-done.10.c) | copy-start | bytes 835588
  44.4 23.4 %collective-permute-start.9 = (s16[272,512]{1,0:T(8,128)(2,1)}, s16[272,512]{1,0:T(8,128)(2,1)}, u32[]{:S(2)}, u32[]{:S(2)}) collective-permute-start(s16[272,512]{1,0:T(8,128)(2,1)} %get-tuple-element.43), channel_id=1, source_target_pairs={{0,6},{1,7},{2,0},{3,1},{4,2},{5,3},{6,4},{7,5},{8,14},{9,15},{10,... | collective-permute-start | bytes 835592 | tf_op jit(solution)/shard_map/ppermute | solution.py:437
  45.1 26.9 %collective-permute-start.4 = (s16[272,512]{1,0:T(8,128)(2,1)}, s16[272,512]{1,0:T(8,128)(2,1)}, u32[]{:S(2)}, u32[]{:S(2)}) collective-permute-start(s16[272,512]{1,0:T(8,128)(2,1)} %get-tuple-element.37), channel_id=1, source_target_pairs={{0,2},{1,3},{2,4},{3,5},{4,6},{5,7},{6,0},{7,1},{8,10},{9,11},{10,... | collective-permute-start | bytes 835592 | tf_op jit(solution)/shard_map/ppermute | solution.py:436
  45.9 26.1 %collective-permute-start.5 = (s16[272,512]{1,0:T(8,128)(2,1)}, s16[272,512]{1,0:T(8,128)(2,1)}, u32[]{:S(2)}, u32[]{:S(2)}) collective-permute-start(s16[272,512]{1,0:T(8,128)(2,1)} %get-tuple-element.38), channel_id=1, source_target_pairs={{0,6},{1,7},{2,0},{3,1},{4,2},{5,3},{6,4},{7,5},{8,14},{9,15},{10,... | collective-permute-start | bytes 835592 | tf_op jit(solution)/shard_map/ppermute | solution.py:437
  47.8 24.2 %collective-permute-start.6 = (s16[272,512]{1,0:T(8,128)(2,1)}, s16[272,512]{1,0:T(8,128)(2,1)}, u32[]{:S(2)}, u32[]{:S(2)}) collective-permute-start(s16[272,512]{1,0:T(8,128)(2,1)} %get-tuple-element.39), channel_id=1, source_target_pairs={{0,4},{1,5},{2,6},{3,7},{4,0},{5,1},{6,2},{7,3},{8,12},{9,13},{10,... | collective-permute-start | bytes 835592 | tf_op jit(solution)/shard_map/ppermute | solution.py:438
  50.2 0.7 copy-start.12
  50.9 28.3 %all-to-all-start = ((bf16[32,16,128]{2,1,0:T(8,128)(2,1)}), bf16[32,16,128]{2,1,0:T(8,128)(2,1)S(1)}, u32[]{:S(2)}, u32[]{:S(2)}) async-start(bf16[32,16,128]{2,1,0:T(8,128)(2,1)} %get-tuple-element.31), calls=%async_computation | async-start | bytes 262144 | tf_op jit(solution)/shard_map/all_to_all | solution.py:446
  62.5 16.7 %copy-start.19 = (bf16[256]{0:T(256)(128)(2,1)S(1)}, bf16[256]{0:T(256)(128)(2,1)}, u32[]{:S(2)}) copy-start(bf16[256]{0:T(256)(128)(2,1)} %param.19) | copy-start | bytes 1540
  63.6 28.6 %collective-permute-start.3 = (s16[304,256]{1,0:T(8,128)(2,1)}, s16[304,256]{1,0:T(8,128)(2,1)S(1)}, u32[]{:S(2)}, u32[]{:S(2)}) collective-permute-start(s16[304,256]{1,0:T(8,128)(2,1)} %get-tuple-element.36), channel_id=1, source_target_pairs={{0,1},{1,0},{2,3},{3,2},{4,5},{5,4},{6,7},{7,6},{8,9},{9,8},{10,11... | collective-permute-start | bytes 466952 | tf_op jit(solution)/shard_map/ppermute | solution.py:451
  67.8 1.0 copy-start.8
  70.8 16.0 %collective-permute-start.11 = (s16[272,256]{1,0:T(8,128)(2,1)}, s16[272,256]{1,0:T(8,128)(2,1)}, u32[]{:S(2)}, u32[]{:S(2)}) collective-permute-start(s16[272,256]{1,0:T(8,128)(2,1)} %get-tuple-element.46), channel_id=1, source_target_pairs={{0,1},{1,0},{2,3},{3,2},{4,5},{5,4},{6,7},{7,6},{8,9},{9,8},{10,11... | collective-permute-start | bytes 417800 | tf_op jit(solution)/shard_map/ppermute | solution.py:451
  72.0 32.3 %copy-start.4 = (bf16[32,128,256]{2,1,0:T(8,128)(2,1)S(1)}, bf16[32,128,256]{2,1,0:T(8,128)(2,1)}, u32[]{:S(2)}) copy-start(bf16[32,128,256]{2,1,0:T(8,128)(2,1)} %cache.1) | copy-start | bytes 6291460
  74.3 0.7 copy-start.9
  75.0 17.2 %collective-permute-start.7 = (s16[272,256]{1,0:T(8,128)(2,1)}, s16[272,256]{1,0:T(8,128)(2,1)S(1)}, u32[]{:S(2)}, u32[]{:S(2)}) collective-permute-start(s16[272,256]{1,0:T(8,128)(2,1)} %get-tuple-element.41), channel_id=1, source_target_pairs={{0,1},{1,0},{2,3},{3,2},{4,5},{5,4},{6,7},{7,6},{8,9},{9,8},{10,11... | collective-permute-start | bytes 417800 | tf_op jit(solution)/shard_map/ppermute | solution.py:451
  92.2 1.0 copy-start.5
  93.2 1.0 copy-start.6
  94.2 0.9 copy-start.10
  98.5 19.4 %all-to-all-start.1 = ((f32[32,24,128]{2,1,0:T(8,128)}), f32[32,24,128]{2,1,0:T(8,128)S(1)}, u32[]{:S(2)}, u32[]{:S(2)}) async-start(f32[32,24,128]{2,1,0:T(8,128)} %get-tuple-element.56), calls=%async_computation.1 | async-start | bytes 786432 | tf_op jit(solution)/shard_map/all_to_all | solution.py:460
  104.3 0.9 copy-start.13

commit v2 on v1

v2 whole, which is shorter than its diff:
```python
import jax
import jax.numpy as jnp
import numpy as np
from jax import lax
from jax.experimental import pallas as pl
from jax.experimental.pallas import tpu as pltpu
from jax.sharding import PartitionSpec as P

HW = 128
RANK = 32
ROPE_BASE = 1000000.0
NEG = -1e30
PARTS = ((0, 384), (384, 384))
LIMIT = 52 * 2**20
BLK = 32
SROWS = 16
QMAX = 32766.0
MAGIC = 12582912.0
F32 = jnp.float32
BF16 = jnp.bfloat16


def rope_tables(first, count, step=1):
    half = HW // 2
    freq = (ROPE_BASE ** (-(np.arange(half, dtype=np.float64) * 2.0) / HW)).astype(np.float32)
    angle = np.arange(first, first + count, step, dtype=np.float32)[:, None] * freq[None, :]
    cosine = np.cos(angle.astype(np.float64)).astype(np.float32)
    sine = np.sin(angle.astype(np.float64)).astype(np.float32)
    return np.concatenate([cosine, cosine], 1), np.concatenate([-sine, sine], 1)


def turn(values, cosine, sine):
    return values * cosine + pltpu.roll(values, HW // 2, 1) * sine


def nn(a, b):
    return lax.dot_general(a, b, (((1,), (0,)), ((), ())), preferred_element_type=F32)


def nt(a, b):
    return lax.dot_general(a, b, (((1,), (1,)), ((), ())), preferred_element_type=F32)


def encode(values, out_ref, peak_ref):
    rows, cols = values.shape
    blocks = rows // BLK
    peak_ref[...] = jnp.full(peak_ref.shape, 1e-30, F32)
    for b in range(blocks):
        peak_ref[b : b + 1, :] = jnp.max(jnp.abs(values[b * BLK : (b + 1) * BLK]), axis=0, keepdims=True)
    level = jnp.ceil(jnp.log2(jnp.maximum(peak_ref[...], 1e-30)) * 256.0) + 1.0
    inverse = jnp.exp2(level * (-1.0 / 256.0)) * QMAX
    for b in range(blocks):
        scaled = values[b * BLK : (b + 1) * BLK] * inverse[b : b + 1, :]
        code = (scaled + MAGIC) - MAGIC
        out_ref[b * BLK : (b + 1) * BLK, :] = code.astype(jnp.int32).astype(jnp.int16)
    out_ref[rows : rows + SROWS, :] = level.astype(jnp.int32).astype(jnp.int16)


def scales(ref, rows):
    level = ref[rows : rows + SROWS, :].astype(jnp.int32).astype(F32)
    return jnp.exp2(level * (1.0 / 256.0)) * (1.0 / QMAX)


def decode(ref, scale, b):
    return ref[b * BLK : (b + 1) * BLK, :].astype(jnp.int32).astype(F32) * scale[b : b + 1, :]


def spread_up(up, span, heads, rows):
    key_row = (lax.broadcasted_iota(jnp.int32, (rows, HW), 0) % (2 * RANK)) < RANK
    zero = jnp.zeros((rows, HW), BF16)
    parts = []
    for head in heads:
        part = up[span, pl.ds(pl.multiple_of(head * HW, HW), HW)]
        parts += [jnp.where(key_row, part, zero), jnp.where(key_row, zero, part)]
    return jnp.concatenate(parts, axis=1)


def two_parts(values):
    high = values.astype(BF16)
    return high, (values - high.astype(F32)).astype(BF16)


class Loader:
    def __init__(self, adapter_of, hidden, weight, down, up, hx, wx, d, u, sems, whole):
        self.sems, self.hx, self.wx, self.d, self.u = sems, hx, wx, d, u
        self.depth = hidden.shape[1]
        tp = lax.axis_index("tp")
        self.y, self.z = tp // 2, tp % 2
        adapter = adapter_of[lax.axis_index("rep")]
        self.odd = adapter % 2
        spot = pl.ds(pl.multiple_of((adapter // 2) * (4 * RANK), 4 * RANK), 4 * RANK)
        self.pair = spot if whole else pl.ds(0, 4 * RANK)
        self.copies = [
            pltpu.make_async_copy(down if whole else down.at[:, spot], d, sems.at[0]),
            pltpu.make_async_copy(up if whole else up.at[spot, :], u, sems.at[1]),
        ]
        for first, rows in PARTS:
            span = pl.ds(first, rows)
            self.copies.append(
                pltpu.make_async_copy(hidden.at[span, :], hx.at[span, pl.ds(0, self.depth)], sems.at[len(self.copies)]))
        self.weight = weight

    def head(self, off, other):
        return ((self.y + off) % 4) * 2 + (1 - self.z if other else self.z)

    def weights(self, slot, off):
        made = []
        for other in range(2):
            at = pl.ds(pl.multiple_of(self.head(off, other) * (2 * HW), 2 * HW), 2 * HW)
            to = self.wx.at[slot, pl.ds(0, self.depth), pl.ds(other * 2 * HW, 2 * HW)]
            made.append(pltpu.make_async_copy(self.weight.at[:, at], to, self.sems.at[4 + 2 * slot + other]))
        return made

    def ranks(self, first, rows):
        span = slice(first, first + rows)
        got = nn(self.hx[span, : self.depth], self.d[:, self.pair])
        lane = lax.broadcasted_iota(jnp.int32, got.shape, 1)
        high, low = two_parts(jnp.where((lane // (2 * RANK)) == self.odd, got, 0.0))
        self.hx[span, self.depth : self.depth + 4 * RANK] = high
        self.hx[span, self.depth + 4 * RANK :] = low

    def extend(self, slot, off):
        ups = spread_up(self.u, self.pair, [self.head(off, 0), self.head(off, 1)], 4 * RANK)
        self.wx[slot, self.depth : self.depth + 4 * RANK, :] = ups
        self.wx[slot, self.depth + 4 * RANK :, :] = ups


def far_body(adapter_of, hidden, weight, down, up, out0, out1, hx, wx, d, u, tile, peaks, sems):
    load = Loader(adapter_of, hidden, weight, down, up, hx, wx, d, u, sems, False)
    blocks = load.weights(0, 2)
    for copy in load.copies[:3] + blocks + load.copies[3:]:
        copy.start()
    for copy in load.copies[:3]:
        copy.wait()
    load.ranks(*PARTS[0])
    load.extend(0, 2)
    for copy in blocks:
        copy.wait()
    for i, out in enumerate((out0, out1)):
        first, rows = PARTS[i]
        if i:
            load.copies[3].wait()
            load.ranks(first, rows)
        tile[...] = nn(hx[first : first + rows, :], wx[0])
        encode(tile[...], out, peaks)


def near_body(adapter_of, hidden, weight, down, up, latest, parents, adapters,
              direct0, direct1, near0, near1, own0, own1, last, hx, wx, d, u, tile, peaks, xl, sems):
    load = Loader(adapter_of, hidden, weight, down, up, hx, wx, d, u, sems, True)
    offs = (1, 3, 0, 2)
    blocks = [load.weights(k, off) for k, off in enumerate(offs)]
    for copy in load.copies + [copy for block in blocks for copy in block]:
        copy.start()
    for copy in load.copies:
        copy.wait()
    for part in PARTS:
        load.ranks(*part)
    ranks = nn(latest[...], d[...])
    names = lax.broadcasted_iota(jnp.int32, (parents.shape[0], adapters.shape[1]), 1)
    mine = jnp.sum(jnp.where(parents[...] == names, adapters[...], 0), axis=1, keepdims=True)
    lane = lax.broadcasted_iota(jnp.int32, ranks.shape, 1)
    high, low = two_parts(jnp.where((lane // (2 * RANK)) == mine, ranks, 0.0))
    xl[:, : ranks.shape[1]] = high
    xl[:, ranks.shape[1] :] = low
    first, rows = PARTS[1]

    def new_rows(k, off):
        ups = spread_up(u, slice(None), [load.head(off, 0), load.head(off, 1)], u.shape[0])
        return (nn(latest[...], wx[k, : load.depth, :]) + nn(xl[:, : ranks.shape[1]], ups)
                + nn(xl[:, ranks.shape[1] :], ups))

    for k, off in enumerate(offs):
        for copy in blocks[k]:
            copy.wait()
        if off == 2:
            encode(new_rows(k, off), last, peaks)
            continue
        load.extend(k, off)
        top = nn(hx[: PARTS[0][1], :], wx[k])
        if off == 3:
            tile[: PARTS[0][1], :] = top
            encode(tile[: PARTS[0][1], :], direct0, peaks)
        else:
            (near0 if off == 1 else own0)[...] = top
        to = {1: tile, 3: near1, 0: own1}[off]
        to[:rows, :] = nn(hx[first:, :], wx[k])
        to[rows:, :] = new_rows(k, off)
        if off == 1:
            encode(tile[...], direct1, peaks)


def project(adapter_index, hidden, weight, down, up, extra):
    depth = hidden.shape[1]
    news = extra[0].shape[0] if extra else 0
    length = hidden.shape[0]
    vmem = pl.BlockSpec(memory_space=pltpu.VMEM)
    hbm = pl.BlockSpec(memory_space=pltpu.HBM)
    smem = pl.BlockSpec(memory_space=pltpu.SMEM)
    code = lambda rows: jax.ShapeDtypeStruct((rows + SROWS, 4 * HW), jnp.int16)
    sums = lambda rows: jax.ShapeDtypeStruct((rows, 4 * HW), F32)
    r0, r1 = PARTS[0][1], PARTS[1][1] + news
    wide, tall, slots = (down.shape[1], up.shape[0], 4) if extra else (4 * RANK, 4 * RANK, 1)
    out_shape = [code(r0), code(r1), sums(r0), sums(r1), sums(r0), sums(r1), code(news)] if extra else [code(r0), code(r1)]
    scratch = [
        pltpu.VMEM((length, depth + 8 * RANK), BF16),
        pltpu.VMEM((slots, depth + 8 * RANK, 4 * HW), BF16),
        pltpu.VMEM((depth, wide), BF16),
        pltpu.VMEM((tall, up.shape[1]), BF16),
        pltpu.VMEM((r1, 4 * HW), F32),
        pltpu.VMEM((SROWS, 4 * HW), F32),
    ]
    if extra:
        scratch.append(pltpu.VMEM((news, 2 * wide), BF16))
    scratch.append(pltpu.SemaphoreType.DMA((4 + 2 * slots,)))
    return pl.pallas_call(
        near_body if extra else far_body,
        in_specs=[smem, hbm, hbm, hbm, hbm] + [vmem] * (3 if extra else 0),
        out_specs=[vmem] * len(out_shape),
        out_shape=out_shape,
        scratch_shapes=scratch,
        compiler_params=pltpu.CompilerParams(vmem_limit_bytes=LIMIT),
        cost_estimate=pl.CostEstimate(
            flops=2 * length * depth * (12 if extra else 4) * HW, bytes_accessed=8 * 10**6, transcendentals=0),
        name="project_near" if extra else "project_far",
    )(adapter_index, hidden, weight, down, up, *(extra or ()))


def relay_body(came, near, out, peaks, whole):
    sent = came.shape[0] - SROWS
    scale = scales(came, sent)
    for k in range(sent // BLK):
        span = slice(k * BLK, (k + 1) * BLK)
        whole[span, :] = near[span, :] + decode(came, scale, k)
    if sent < near.shape[0]:
        whole[sent:, :] = near[sent:, :]
    encode(whole[...], out, peaks)


def relay(came, near):
    rows, cols = near.shape
    return pl.pallas_call(
        relay_body,
        out_shape=jax.ShapeDtypeStruct((rows + SROWS, cols), jnp.int16),
        scratch_shapes=[pltpu.VMEM((SROWS, cols), F32), pltpu.VMEM((rows, cols), F32)],
        compiler_params=pltpu.CompilerParams(vmem_limit_bytes=LIMIT),
        cost_estimate=pl.CostEstimate(flops=rows * cols * 8, bytes_accessed=rows * cols * 8, transcendentals=0),
        name="relay",
    )(came, near)


def fold_body(a, b, own, *refs):
    last = refs[0] if len(refs) == 5 else None
    out, keep, peaks, other = refs[-4:]
    rows = own.shape[0]
    sa, sb = scales(a, rows), scales(b, rows)
    for k in range(rows // BLK):
        span = slice(k * BLK, (k + 1) * BLK)
        total = own[span, :] + decode(a, sa, k) + decode(b, sb, k)
        if last is not None and k == rows // BLK - 1:
            total = total + decode(last, scales(last, BLK), 0)
        keep[span, :] = total[:, : 2 * HW]
        other[span, :] = total[:, 2 * HW :]
    encode(other[...], out, peaks)


def fold(a, b, own, *last):
    rows = own.shape[0]
    return pl.pallas_call(
        fold_body,
        out_shape=[
            jax.ShapeDtypeStruct((rows + SROWS, 2 * HW), jnp.int16),
            jax.ShapeDtypeStruct((rows, 2 * HW), F32),
        ],
        scratch_shapes=[pltpu.VMEM((SROWS, 2 * HW), F32), pltpu.VMEM((rows, 2 * HW), F32)],
        compiler_params=pltpu.CompilerParams(vmem_limit_bytes=LIMIT),
        cost_estimate=pl.CostEstimate(flops=rows * 4 * HW * 8, bytes_accessed=rows * HW * 48, transcendentals=0),
        name="fold",
    )(a, b, own, *last)


def dispatch_body(parents, lengths, queries, table, send, turned, ropes, place, counts, spread):
    comps = queries.shape[0]
    group = queries.shape[1] // HW

    def look(c, carry):
        ropes[pl.ds(c, 1), :] = table[pl.ds(lengths[c] - 1, 1), :]
        return carry

    lax.fori_loop(0, comps, look, 0)
    for h in range(group):
        part = queries[:, h * HW : (h + 1) * HW].astype(F32)
        part = turn(part, ropes[:, :HW], ropes[:, HW:])
        turned[pl.ds(h, comps, stride=group), :] = part.astype(BF16).astype(F32)
    spread[...] = jnp.zeros(spread.shape, F32)

    def clear(i, carry):
        counts[i] = 0
        return carry

    lax.fori_loop(0, counts.shape[0], clear, 0)

    def put(c, carry):
        p = parents[c]
        s = counts[p]
        counts[p] = s + 1
        at = 2 * p + s
        place[c] = at
        to = pl.multiple_of(at * group, group)
        spread[pl.ds(to, group), :] = turned[pl.ds(pl.multiple_of(c * group, group), group), :]
        return carry

    lax.fori_loop(0, comps, put, 0)
    send[...] = spread[...].astype(BF16).reshape(send.shape)


def dispatch(parents, lengths, queries, table, prompts):
    comps = queries.shape[0]
    group = queries.shape[1] // HW
    vmem = pl.BlockSpec(memory_space=pltpu.VMEM)
    smem = pl.BlockSpec(memory_space=pltpu.SMEM)
    return pl.pallas_call(
        dispatch_body,
        in_specs=[smem, smem, vmem, vmem],
        out_specs=[vmem, vmem, vmem, smem],
        out_shape=[
            jax.ShapeDtypeStruct((prompts, 2 * group, HW), BF16),
            jax.ShapeDtypeStruct((comps * group, HW), F32),
            jax.ShapeDtypeStruct((comps, 2 * HW), F32),
            jax.ShapeDtypeStruct((comps,), jnp.int32),
        ],
        scratch_shapes=[pltpu.SMEM((prompts,), jnp.int32), pltpu.VMEM((prompts * 2 * group, HW), F32)],
        compiler_params=pltpu.CompilerParams(vmem_limit_bytes=LIMIT),
        cost_estimate=pl.CostEstimate(flops=10**6, bytes_accessed=10**6, transcendentals=0),
        name="dispatch",
    )(parents, lengths, queries, table)


def suffix_body(lengths, turned, cache, came, keep, bias, ropes, latest, out, stats, scores, weights, whole):
    comps = ropes.shape[0]
    first = keep.shape[0] - comps
    group = turned.shape[0] // comps
    scale = HW ** -0.5
    whole[...] = keep[first:, :] + bias[...] + decode(came, scales(came, keep.shape[0]), first // BLK)
    key = turn(whole[:, :HW], ropes[:, :HW], ropes[:, HW:]).astype(BF16)
    value = whole[:, HW:].astype(BF16)
    latest[:, :HW] = key
    latest[:, HW:] = value

    def wide(rows):
        return jnp.broadcast_to(rows[:, None, :], (comps, group, HW)).reshape(comps * group, HW)

    slot = lax.broadcasted_iota(jnp.int32, (group, HW), 1)
    for c in range(comps):
        span = slice(c * group, (c + 1) * group)
        score = nt(turned[span, :].astype(BF16), cache[c, :, :HW]) * scale
        scores[span, :] = jnp.where(slot < lengths[c], score, NEG)
    own_score = jnp.sum(turned[...] * wide(key.astype(F32)), axis=1, keepdims=True) * scale
    masked = scores[...]
    top = jnp.maximum(jnp.max(masked, axis=1, keepdims=True), own_score)
    weight = jnp.exp(masked - top)
    own_weight = jnp.exp(own_score - top)
    total = jnp.sum(weight, axis=1, keepdims=True) + own_weight
    weights[...] = weight
    for c in range(comps):
        span = slice(c * group, (c + 1) * group)
        out[span, :] = nn(weights[span, :].astype(BF16), cache[c, :, HW:])
    out[...] = out[...] + own_weight.astype(BF16).astype(F32) * wide(value.astype(F32))
    lane = lax.broadcasted_iota(jnp.int32, stats.shape, 1)
    stats[...] = jnp.where(lane < HW // 2, top, total)


def suffix(lengths, turned, cache, came, keep, bias, ropes):
    comps = ropes.shape[0]
    rows = turned.shape[0]
    vmem = pl.BlockSpec(memory_space=pltpu.VMEM)
    return pl.pallas_call(
        suffix_body,
        in_specs=[pl.BlockSpec(memory_space=pltpu.SMEM)] + [vmem] * 6,
        out_shape=[
            jax.ShapeDtypeStruct((comps, 2 * HW), BF16),
            jax.ShapeDtypeStruct((rows, HW), F32),
            jax.ShapeDtypeStruct((rows, HW), F32),
        ],
        scratch_shapes=[pltpu.VMEM((rows, HW), F32), pltpu.VMEM((rows, HW), F32), pltpu.VMEM((comps, 2 * HW), F32)],
        compiler_params=pltpu.CompilerParams(vmem_limit_bytes=LIMIT),
        cost_estimate=pl.CostEstimate(flops=10**7, bytes_accessed=10**7, transcendentals=0),
        name="suffix",
    )(lengths, turned, cache, came, keep, bias, ropes)


def prefix_body(queries, bias, turns, *refs):
    chunks = len(PARTS)
    came, keep = refs[:chunks], refs[chunks : 2 * chunks]
    kv, out = refs[2 * chunks :]
    blocks = kv.shape[0] // BLK
    cos_in, sin_in = turns[blocks:, :HW], turns[blocks:, HW:]
    for i, (first, rows) in enumerate(PARTS):
        scale = scales(came[i], keep[i].shape[0])
        for k in range(rows // BLK):
            span = slice(first + k * BLK, first + (k + 1) * BLK)
            total = keep[i][k * BLK : (k + 1) * BLK, :] + decode(came[i], scale, k) + bias[...]
            at = first // BLK + k
            cos_at, sin_at = turns[at : at + 1, :HW], turns[at : at + 1, HW:]
            cosine, sine = cos_at * cos_in - sin_at * sin_in, sin_at * cos_in + cos_at * sin_in
            kv[span, :HW] = turn(total[:, :HW], cosine, sine).astype(BF16)
            kv[span, HW:] = total[:, HW:].astype(BF16)
    prompts, per, _ = queries.shape
    step = 8
    for s in range(0, prompts, step):
        q = queries[s : s + step].reshape(step * per, HW)
        scores = nt(q, kv[:, :HW]) * (HW ** -0.5)
        top = jnp.max(scores, axis=1, keepdims=True)
        weight = jnp.exp(scores - top)
        total = jnp.sum(weight, axis=1, keepdims=True)
        part = nn(weight.astype(BF16), kv[:, HW:])
        out[s : s + step, :per, :] = part.reshape(step, per, HW)
        lane = lax.broadcasted_iota(jnp.int32, (step * per, HW), 1)
        row = lax.broadcasted_iota(jnp.int32, (step * per, HW), 0) % per
        stat = jnp.where(lane == row, top, 0.0) + jnp.where(lane == row + per, total, 0.0)
        stat = jnp.sum(stat.reshape(step, per, HW), axis=1, keepdims=True)
        out[s : s + step, per:, :] = jnp.broadcast_to(stat, (step, 8, HW))


def prefix(queries, bias, turns, came, keep, length):
    prompts, per, _ = queries.shape
    return pl.pallas_call(
        prefix_body,
        out_shape=[
            jax.ShapeDtypeStruct((length, 2 * HW), BF16),
            jax.ShapeDtypeStruct((prompts, per + 8, HW), F32),
        ],
        compiler_params=pltpu.CompilerParams(vmem_limit_bytes=LIMIT),
        cost_estimate=pl.CostEstimate(flops=2 * 10**8, bytes_accessed=10**7, transcendentals=10**6),
        name="prefix",
    )(queries, bias, turns, *came, *keep)


def merge_body(place, back, out, stats, attn, top_all, total_all, joined):
    prompts, per, _ = back.shape
    per -= 8
    rows = out.shape[0]
    comps = attn.shape[0]
    group = rows // comps
    lane = lax.broadcasted_iota(jnp.int32, (prompts * per, HW), 1)
    row = lax.broadcasted_iota(jnp.int32, (prompts * per, HW), 0) % per
    wide = jnp.broadcast_to(back[:, per : per + 1, :], (prompts, per, HW)).reshape(prompts * per, HW)
    top_all[...] = jnp.broadcast_to(
        jnp.sum(jnp.where(lane == row, wide, 0.0), axis=1, keepdims=True), top_all.shape)
    total_all[...] = jnp.broadcast_to(
        jnp.sum(jnp.where(lane == row + per, wide, 0.0), axis=1, keepdims=True), total_all.shape)

    for c in range(comps):
        at = place[c]
        src = pl.ds(pl.multiple_of(at * group, group), group)
        top_p, total_p = top_all[src, :], total_all[src, :]
        out_p = back[at // 2, pl.ds(pl.multiple_of((at % 2) * group, group), group), :]
        span = slice(c * group, (c + 1) * group)
        stat = stats[span, :]
        top_s, total_s = stat[:, :1], stat[:, HW // 2 : HW // 2 + 1]
        top = jnp.maximum(top_p, top_s)
        alpha = jnp.exp(top_p - top)
        beta = jnp.exp(top_s - top)
        joined[span, :] = (alpha * out_p + beta * out[span, :]) / (alpha * total_p + beta * total_s)
    for h in range(group):
        attn[:, h * HW : (h + 1) * HW] = joined[pl.ds(h, comps, stride=group), :].astype(BF16)


def merge(place, back, out, stats, comps):
    rows = out.shape[0]
    slots = back.shape[0] * (back.shape[1] - 8)
    vmem = pl.BlockSpec(memory_space=pltpu.VMEM)
    smem = pl.BlockSpec(memory_space=pltpu.SMEM)
    return pl.pallas_call(
        merge_body,
        in_specs=[smem, vmem, vmem, vmem],
        out_specs=vmem,
        out_shape=jax.ShapeDtypeStruct((comps, rows // comps * HW), BF16),
        scratch_shapes=[pltpu.VMEM((slots, HW), F32), pltpu.VMEM((slots, HW), F32), pltpu.VMEM((rows, HW), F32)],
        compiler_params=pltpu.CompilerParams(vmem_limit_bytes=LIMIT),
        cost_estimate=pl.CostEstimate(flops=10**6, bytes_accessed=10**6, transcendentals=10**5),
        name="merge",
    )(place, back, out, stats)


def on_device(
    prefix_hidden_states, latest_hidden, queries, suffix_key_cache, key_value_weight, key_value_bias,
    adapter_down_weight, adapter_up_weight, parents, adapter_index, suffix_length_count,
):
    length = prefix_hidden_states.shape[1]
    comps = latest_hidden.shape[0]
    prompts = adapter_index.shape[0]
    along_y = lambda d: [(a * 2 + b, ((a + d) % 4) * 2 + b) for a in range(4) for b in range(2)]
    along_z = [(a * 2 + b, a * 2 + 1 - b) for a in range(4) for b in range(2)]

    hidden = prefix_hidden_states[0]
    y_step = lambda value, d: lax.ppermute(value, "tp", along_y(d))
    weights = (key_value_weight, adapter_down_weight, adapter_up_weight)
    far0, far1 = project(adapter_index, hidden, *weights, None)
    far0, far1 = y_step(far0, 1), y_step(far1, -1)
    direct0, direct1, near0, near1, own0, own1, last = project(
        adapter_index, hidden, *weights, (latest_hidden, parents, adapter_index.reshape(1, -1)))
    direct0 = y_step(direct0, -1)
    joined0 = relay(far0, near0)
    joined0, direct1, last = lax.optimization_barrier((joined0, direct1, last))
    joined0 = y_step(joined0, 1)
    joined1 = relay(far1, near1)
    direct1, joined1, last = y_step(direct1, 1), y_step(joined1, -1), y_step(last, 2)

    cos_t, sin_t = rope_tables(length + 1, suffix_key_cache.shape[1])
    table = jnp.asarray(np.concatenate([cos_t, sin_t], 1))
    to_prompts, turned, ropes, place = dispatch(parents[:, 0], suffix_length_count, queries, table, prompts)
    here = lax.all_to_all(to_prompts, "rep", 0, 0, tiled=True)

    came, keep = [], []
    for args in ((joined0, direct0, own0), (joined1, direct1, own1, last)):
        code, kept = fold(*args)
        came.append(lax.ppermute(code, "tp", along_z))
        keep.append(kept)

    bias = key_value_bias.astype(F32).reshape(1, 2 * HW)
    latest_key_value, out_s, stats = suffix(
        suffix_length_count, turned, suffix_key_cache, came[1], keep[1], bias, ropes)
    blocks, within = rope_tables(0, length, BLK), rope_tables(0, BLK)
    turns = jnp.asarray(np.concatenate([np.concatenate(blocks, 1), np.concatenate(within, 1)], 0))
    prefix_kv, part = prefix(here, bias, turns, came, keep, length)
    back = lax.all_to_all(part, "rep", 0, 0, tiled=True)
    attn_out = merge(place, back, out_s, stats, comps)
    return prefix_kv[None], latest_key_value, attn_out


def solution(mesh):
    in_specs = (
        P("rep", None, "tp"), P("rep", "tp"), P("rep", "tp"), P("rep", None, "tp"), P("tp", None), P("tp"),
        P("tp", None), P(), P("rep", None), P(), P("rep"),
    )
    out_specs = (P("rep", None, "tp"), P("rep", "tp"), P("rep", "tp"))
    return jax.shard_map(on_device, mesh=mesh, in_specs=in_specs, out_specs=out_specs, check_vma=False)
```

time: 120 us -> 95.3 us (0.79)
  local copies, waits for them, and re-layouts: 15.9 us -> 2.6 us
  Pallas kernels: 34.1 us -> 27.3 us
  waiting for transfers between devices: 28.7 us -> 22.5 us
  starting transfers between devices: 37.4 us -> 41.6 us
  between operations: 3.39 us -> 0.8 us
    unnamed x41 -> x23, local copies, waits for them, and re-layouts: 14.5 us -> 2.6 us
    all_to_all x1, starting transfers between devices: 5.6 us -> 15.3 us  [on_device(): back = lax.all_to_all(part, 'rep', 0, 0, tiled=True)]
    ppermute x3 -> x2, waiting for transfers between devices: 13 us -> 8.57 us  [on_device(): came.append(lax.ppermute(code, 'tp', along_z))]
    pallas_call x6 -> x7, Pallas kernels: 27.1 us -> 22.6 us  [the longest x2 14.5 us: project(): pl.pallas_call(near_body if extra else far_body, in_specs=[smem, hbm, hbm...]
    ppermute x9 -> x7, starting transfers between devices: 10.5 us -> 7.77 us  [on_device(): y_step = lambda value, d: lax.ppermute(value, 'tp', along_y(d))]
    pallas_call x3 -> x2, Pallas kernels: 5.36 us -> 3.09 us  [fold(): pl.pallas_call(fold_body, out_shape=[jax.ShapeDtypeStruct((rows + SROWS,...]
    ppermute x3 -> x2, starting transfers between devices: 9.59 us -> 7.4 us  [on_device(): came.append(lax.ppermute(code, 'tp', along_z))]
    dynamic_slice x1 -> x0, local copies, waits for them, and re-layouts: 1.24 us -> none  [on_device(): adapter = lax.dynamic_index_in_dim(adapter_index, rep, 0, keepdims=False)]
  transfers between devices with their start and end apart: 14 -> 11, of which waited for: 4 -> 3; matrix products, arithmetic and copies ran while one was open for 0% -> 0% of each run, Pallas kernels for 18% -> 20%
where the time goes in v2:
time: 95.3 us; the launch traced here: 94.8 us
  starting transfers between devices  41.6 us (44%)
  Pallas kernels  27.3 us (29%)
  waiting for transfers between devices  22.5 us (24%)
  local copies, waits for them, and re-layouts  2.6 us (3%)
    all_to_all x1, starting transfers between devices, on_device(): back = lax.all_to_all(part, 'rep', 0, 0, tiled=True)  15.3 us
    pallas_call x2, Pallas kernels, project(): pl.pallas_call(near_body if extra else far_body, in_specs=[smem, hbm, hbm...  14.5 us
    all_to_all x1, starting transfers between devices, on_device(): here = lax.all_to_all(to_prompts, 'rep', 0, 0, tiled=True)  11.1 us
    all_to_all x1, waiting for transfers between devices, on_device(): back = lax.all_to_all(part, 'rep', 0, 0, tiled=True)  11 us
    ppermute x2, waiting for transfers between devices, on_device(): came.append(lax.ppermute(code, 'tp', along_z))  8.57 us
    ppermute x7, starting transfers between devices, on_device(): y_step = lambda value, d: lax.ppermute(value, 'tp', along_y(d))  7.77 us
    ppermute x2, starting transfers between devices, on_device(): came.append(lax.ppermute(code, 'tp', along_z))  7.4 us
    pallas_call x2, Pallas kernels, fold(): pl.pallas_call(fold_body, out_shape=[jax.ShapeDtypeStruct((rows + SROWS,...  3.09 us
  transfers between devices with their start and end apart: 11, of which 3 were waited for; matrix products, arithmetic and copies ran while one was open for 0% of the time, Pallas kernels for 20%

profile of v2, /device:TPU:1, one launch (start us, length us, event | category | flops | bytes accessed | tf_op | source)
XLA Modules:
  0.0 94.8 jit_solution(12901803953743170795)
XLA Ops:
  0.6 0.0 copy-start
  0.6 1.2 %copy-done = bf16[1024,512]{1,0:T(8,128)(2,1)S(1)} copy-done((bf16[1024,512]{1,0:T(8,128)(2,1)S(1)}, bf16[1024,512]{1,0:T(8,128)(2,1)}, u32[]{:S(2)}) %copy-start) | copy-done | bytes 1048600
  1.9 0.0 copy-start.6
  1.9 0.7 copy-done.6
  2.5 0.0 copy-start.5
  2.5 0.0 copy-start.7
  2.5 0.0 copy-start.8
  2.5 4.7 %project_far.1 = (s16[400,512]{1,0:T(8,128)(2,1)S(1)}, s16[400,512]{1,0:T(8,128)(2,1)S(1)}) custom-call(s32[32]{0:T(128)S(1)} %copy-done.6, bf16[768,1024]{1,0:T(8,128)(2,1)} %bitcast.9, bf16[1024,2048]{1,0:T(8,128)(2,1)} %weight.3, bf16[1024,512]{1,0:T(8,128)(2,1)S(1)} %copy-done, bf16[512,1024]{1,0:T(8,128)(2,1)} %up.3), custom_call_target="tpu_custom_call" | custom-call | flops 805306368 | bytes 8000000 | tf_op jit(solution)/shard_map/project_far/pallas_call | solution.py:216
  7.2 2.2 %collective-permute-start = (s16[400,512]{1,0:T(8,128)(2,1)S(1)}, s16[400,512]{1,0:T(8,128)(2,1)S(1)}, u32[]{:S(2)}, u32[]{:S(2)}) collective-permute-start(s16[400,512]{1,0:T(8,128)(2,1)S(1)} %get-tuple-element.29), channel_id=1, source_target_pairs={{0,2},{1,3},{2,4},{3,5},{4,6},{5,7},{6,0},{7,1},{8,10},{9,11},{10,... | collective-permute-start | bytes 1228808 | tf_op jit(solution)/shard_map/ppermute | solution.py:497
  9.4 1.5 %collective-permute-start.4 = (s16[400,512]{1,0:T(8,128)(2,1)S(1)}, s16[400,512]{1,0:T(8,128)(2,1)S(1)}, u32[]{:S(2)}, u32[]{:S(2)}) collective-permute-start(s16[400,512]{1,0:T(8,128)(2,1)S(1)} %get-tuple-element.37), channel_id=1, source_target_pairs={{0,6},{1,7},{2,0},{3,1},{4,2},{5,3},{6,4},{7,5},{8,14},{9,15},{10,... | collective-permute-start | bytes 1228808 | tf_op jit(solution)/shard_map/ppermute | solution.py:497
  10.9 0.0 copy-done.5
  10.9 0.1 copy.16.parents
  11.0 0.0 copy-done.7
  11.0 0.0 copy-done.8
  11.0 9.9 %project_near.1 = (s16[400,512]{1,0:T(8,128)(2,1)}, s16[432,512]{1,0:T(8,128)(2,1)S(1)}, f32[384,512]{1,0:T(8,128)S(1)}, f32[416,512]{1,0:T(8,128)}, f32[384,512...) custom-call(s32[32]{0:T(128)S(1)} %copy-done.7, bf16[768,1024]{1,0:T(8,128)(2,1)} %bitcast.10, ...), custom_call_target="tpu_custom_call" | custom-call | flops 2415919104 | bytes 8000000 | tf_op jit(solution)/shard_map/project_near/pallas_call | solution.py:216
  20.9 0.0 copy-start.1
  20.9 0.0 copy-start.2
  20.9 0.0 copy-start.3
  20.9 0.0 copy-start.4
  21.0 0.0 collective-permute-done.came
  21.0 0.4 relay.2
  21.4 0.1 collective-permute-start.6
  21.5 0.0 collective-permute-done.4.came
  21.5 0.6 copy-done.1
  22.1 0.4 relay.3
  22.5 0.0 copy-start.10
  22.5 0.0 copy-start.9
  22.5 2.1 %collective-permute-start.5 = (s16[432,512]{1,0:T(8,128)(2,1)S(1)}, s16[432,512]{1,0:T(8,128)(2,1)S(1)}, u32[]{:S(2)}, u32[]{:S(2)}) collective-permute-start(s16[432,512]{1,0:T(8,128)(2,1)S(1)} %relay.3), channel_id=1, source_target_pairs={{0,6},{1,7},{2,0},{3,1},{4,2},{5,3},{6,4},{7,5},{8,14},{9,15},{10,... | collective-permute-start | bytes 1327112 | tf_op jit(solution)/shard_map/ppermute | solution.py:497
  24.7 0.2 collective-permute-start.2
  24.8 1.3 %collective-permute-start.1 = (s16[400,512]{1,0:T(8,128)(2,1)S(1)}, s16[400,512]{1,0:T(8,128)(2,1)S(1)}, u32[]{:S(2)}, u32[]{:S(2)}) collective-permute-start(s16[400,512]{1,0:T(8,128)(2,1)S(1)} %relay.2), channel_id=1, source_target_pairs={{0,2},{1,3},{2,4},{3,5},{4,6},{5,7},{6,0},{7,1},{8,10},{9,11},{10,... | collective-permute-start | bytes 1228808 | tf_op jit(solution)/shard_map/ppermute | solution.py:497
  26.1 0.3 collective-permute-start.7
  26.5 0.0 copy-done.2
  26.5 0.0 copy-done.3
  26.5 0.0 copy-done.4
  26.5 2.0 %dispatch.1 = (bf16[32,16,128]{2,1,0:T(8,128)(2,1)}, f32[256,128]{1,0:T(8,128)S(1)}, f32[32,256]{1,0:T(8,128)S(1)}, s32[32]{0:T(128)S(1)}) custom-call(s32[32]{0:T(128)S(1)} %bitcast.5, s32[32]{0:T(128)S(1)} %copy-done.4, bf16[32,1024]{1,0:T(8,128)(2,1)S(1)} %copy-done.3, f32[128,256]{1,0:T(8,128)S(1)} %copy-done.2), custom_call_target="tpu_custom_call" | custom-call | flops 1000000 | bytes 1000000 | tf_op jit(solution)/shard_map/dispatch/pallas_call | solution.py:322
  28.5 11.1 %all-to-all-start = ((bf16[32,16,128]{2,1,0:T(8,128)(2,1)}), bf16[32,16,128]{2,1,0:T(8,128)(2,1)S(1)}, u32[]{:S(2)}, u32[]{:S(2)}) async-start(bf16[32,16,128]{2,1,0:T(8,128)(2,1)} %get-tuple-element.28), calls=%async_computation | async-start | bytes 262144 | tf_op jit(solution)/shard_map/all_to_all | solution.py:513
  39.7 2.9 %collective-permute-done.7.refs_0_ = s16[48,512]{1,0:T(8,128)(2,1)S(1)} collective-permute-done((s16[48,512]{1,0:T(8,128)(2,1)S(1)}, s16[48,512]{1,0:T(8,128)(2,1)S(1)}, u32[]{:S(2)}, u32[]{:S(2)}) %collective-permute-start.7) | collective-permute-done | bytes 49184 | tf_op jit(solution)/shard_map/ppermute | solution.py:497
  42.5 0.0 collective-permute-done.6.b
  42.5 0.0 collective-permute-done.5.a
  42.5 1.6 %fold.3 = (s16[432,256]{1,0:T(8,128)(2,1)S(1)}, f32[416,256]{1,0:T(8,128)S(1)}) custom-call(s16[432,512]{1,0:T(8,128)(2,1)S(1)} %collective-permute-done.5.a, s16[432,512]{1,0:T(8,128)(2,1)S(1)} %collective-permute-done.6.b, f32[416,512]{1,0:T(8,128)} %get-tuple-element.40.own, s16[48,512]{1,0:T(8,128)(2,1)S(1)} %collective-permute-done.7.refs_0_), custom_call_target="tpu_custom_call" | custom-call | flops 1703936 | bytes 2555904 | tf_op jit(solution)/shard_map/fold/pallas_call | solution.py:269
  44.1 7.3 %collective-permute-start.8 = (s16[432,256]{1,0:T(8,128)(2,1)S(1)}, s16[432,256]{1,0:T(8,128)(2,1)S(1)}, u32[]{:S(2)}, u32[]{:S(2)}) collective-permute-start(s16[432,256]{1,0:T(8,128)(2,1)S(1)} %get-tuple-element.42), channel_id=1, source_target_pairs={{0,1},{1,0},{2,3},{3,2},{4,5},{5,4},{6,7},{7,6},{8,9},{9,8},{10,11... | collective-permute-start | bytes 663560 | tf_op jit(solution)/shard_map/ppermute | solution.py:518
  51.4 0.0 collective-permute-done.2.b
  51.4 0.0 collective-permute-done.1.a
  51.4 1.5 %fold.2 = (s16[400,256]{1,0:T(8,128)(2,1)S(1)}, f32[384,256]{1,0:T(8,128)S(1)}) custom-call(s16[400,512]{1,0:T(8,128)(2,1)S(1)} %collective-permute-done.1.a, s16[400,512]{1,0:T(8,128)(2,1)S(1)} %collective-permute-done.2.b, f32[384,512]{1,0:T(8,128)} %get-tuple-element.35.own), custom_call_target="tpu_custom_call" | custom-call | flops 1572864 | bytes 2359296 | tf_op jit(solution)/shard_map/fold/pallas_call | solution.py:269
  52.9 0.1 collective-permute-start.3
  53.0 0.0 copy-done.10
  53.0 0.0 all-to-all-done.queries
  53.0 8.6 %collective-permute-done.3.refs_0_ = s16[400,256]{1,0:T(8,128)(2,1)S(1)} collective-permute-done((s16[400,256]{1,0:T(8,128)(2,1)S(1)}, s16[400,256]{1,0:T(8,128)(2,1)S(1)}, u32[]{:S(2)}, u32[]{:S(2)}) %collective-permute-start.3) | collective-permute-done | bytes 204832 | tf_op jit(solution)/shard_map/ppermute | solution.py:518
  61.6 0.0 collective-permute-done.8.refs_1_.came
  61.6 0.0 copy-done.9
  61.6 2.5 %prefix.1 = (bf16[768,256]{1,0:T(8,128)(2,1)}, f32[32,24,128]{2,1,0:T(8,128)}) custom-call(bf16[32,16,128]{2,1,0:T(8,128)(2,1)S(1)} %all-to-all-done.queries, f32[1,256]{1,0:T(1,128)S(1)} %bitcast.6, f32[56,256]{1,0:T(8,128)S(1)} %copy-done.9, s16[400,256]{1,0:T(8,128)(2,1)S(1)} %collective-permute-done.3.refs_0_, ...), custom_call_target="tpu_custom_call" | custom-call | flops 200000000 | bytes 10000000 | tf_op jit(solution)/shard_map/prefix/pallas_call | solution.py:427
  64.1 15.3 %all-to-all-start.1 = ((f32[32,24,128]{2,1,0:T(8,128)}), f32[32,24,128]{2,1,0:T(8,128)S(1)}, u32[]{:S(2)}, u32[]{:S(2)}) async-start(f32[32,24,128]{2,1,0:T(8,128)} %get-tuple-element.50), calls=%async_computation.1 | async-start | bytes 786432 | tf_op jit(solution)/shard_map/all_to_all | solution.py:527
  79.4 2.8 %suffix.1 = (bf16[32,256]{1,0:T(8,128)(2,1)}, f32[256,128]{1,0:T(8,128)S(1)}, f32[256,128]{1,0:T(8,128)S(1)}) custom-call(s32[32]{0:T(128)S(1)} %copy-done.4, f32[256,128]{1,0:T(8,128)S(1)} %get-tuple-element.46.turned, bf16[32,128,256]{2,1,0:T(8,128)(2,1)} %cache.1, s16[432,256]{1,0:T(8,128)(2,1)S(1)} %collective-permute-done.8.refs_1_.came, ...), custom_call_target="tpu_custom_call" | custom-call | flops 10000000 | bytes 10000000 | tf_op jit(solution)/shard_map/suffix/pallas_call | solution.py:377
  82.2 11.0 %all-to-all-done.1.back = f32[32,24,128]{2,1,0:T(8,128)S(1)} async-done(((f32[32,24,128]{2,1,0:T(8,128)}), f32[32,24,128]{2,1,0:T(8,128)S(1)}, u32[]{:S(2)}, u32[]{:S(2)}) %all-to-all-start.1) | async-done | bytes 393248 | tf_op jit(solution)/shard_map/all_to_all | solution.py:527
  93.2 1.6 %merge.1 = bf16[32,1024]{1,0:T(8,128)(2,1)} custom-call(s32[32]{0:T(128)S(1)} %get-tuple-element.49.place, f32[32,24,128]{2,1,0:T(8,128)S(1)} %all-to-all-done.1.back, f32[256,128]{1,0:T(8,128)S(1)} %get-tuple-element.51.out, f32[256,128]{1,0:T(8,128)S(1)} %get-tuple-element.52.stats), custom_call_target="tpu_custom_call" | custom-call | flops 1000000 | bytes 1000000 | tf_op jit(solution)/shard_map/merge/pallas_call | solution.py:474
  (1 shorter events, 0.0 us)
Async XLA Ops:
  0.6 1.2 %copy-start = (bf16[1024,512]{1,0:T(8,128)(2,1)S(1)}, bf16[1024,512]{1,0:T(8,128)(2,1)}, u32[]{:S(2)}) copy-start(bf16[1024,512]{1,0:T(8,128)(2,1)} %down.3) | copy-start | bytes 3145732
  1.9 0.7 copy-start.6
  2.5 8.4 %copy-start.5 = (s32[32,1]{0,1:T(1,128)S(1)}, s32[32,1]{0,1:T(1,128)}, u32[]{:S(2)}) copy-start(s32[32,1]{0,1:T(1,128)} %param.21) | copy-start | bytes 388
  2.5 8.5 %copy-start.7 = (s32[32]{0:T(128)S(1)}, s32[32]{0:T(128)}, u32[]{:S(2)}) copy-start(s32[32]{0:T(128)} %adapter_of.3) | copy-start | bytes 388
  2.5 8.5 %copy-start.8 = (bf16[32,1024]{1,0:T(8,128)(2,1)S(1)}, bf16[32,1024]{1,0:T(8,128)(2,1)}, u32[]{:S(2)}) copy-start(bf16[32,1024]{1,0:T(8,128)(2,1)} %latest.1) | copy-start | bytes 196612
  7.2 13.8 %collective-permute-start = (s16[400,512]{1,0:T(8,128)(2,1)S(1)}, s16[400,512]{1,0:T(8,128)(2,1)S(1)}, u32[]{:S(2)}, u32[]{:S(2)}) collective-permute-start(s16[400,512]{1,0:T(8,128)(2,1)S(1)} %get-tuple-element.29), channel_id=1, source_target_pairs={{0,2},{1,3},{2,4},{3,5},{4,6},{5,7},{6,0},{7,1},{8,10},{9,11},{10,... | collective-permute-start | bytes 1228808 | tf_op jit(solution)/shard_map/ppermute | solution.py:497
  9.4 12.1 %collective-permute-start.4 = (s16[400,512]{1,0:T(8,128)(2,1)S(1)}, s16[400,512]{1,0:T(8,128)(2,1)S(1)}, u32[]{:S(2)}, u32[]{:S(2)}) collective-permute-start(s16[400,512]{1,0:T(8,128)(2,1)S(1)} %get-tuple-element.37), channel_id=1, source_target_pairs={{0,6},{1,7},{2,0},{3,1},{4,2},{5,3},{6,4},{7,5},{8,14},{9,15},{10,... | collective-permute-start | bytes 1228808 | tf_op jit(solution)/shard_map/ppermute | solution.py:497
  20.9 1.2 %copy-start.1 = (f32[416,512]{1,0:T(8,128)S(1)}, f32[416,512]{1,0:T(8,128)}, u32[]{:S(2)}) copy-start(f32[416,512]{1,0:T(8,128)} %get-tuple-element.38.near) | copy-start | bytes 2555908
  20.9 5.5 %copy-start.2 = (f32[128,256]{1,0:T(8,128)S(1)}, f32[128,256]{1,0:T(8,128)}, u32[]{:S(2)}) copy-start(f32[128,256]{1,0:T(8,128)} %constant.4.clone.table) | copy-start | bytes 393220
  20.9 5.5 %copy-start.3 = (bf16[32,1024]{1,0:T(8,128)(2,1)S(1)}, bf16[32,1024]{1,0:T(8,128)(2,1)}, u32[]{:S(2)}) copy-start(bf16[32,1024]{1,0:T(8,128)(2,1)} %queries.1) | copy-start | bytes 196612
  20.9 5.5 %copy-start.4 = (s32[32]{0:T(128)S(1)}, s32[32]{0:T(128)}, u32[]{:S(2)}) copy-start(s32[32]{0:T(128)} %lengths.3) | copy-start | bytes 388
  21.4 21.1 %collective-permute-start.6 = (s16[432,512]{1,0:T(8,128)(2,1)S(1)}, s16[432,512]{1,0:T(8,128)(2,1)S(1)}, u32[]{:S(2)}, u32[]{:S(2)}) collective-permute-start(s16[432,512]{1,0:T(8,128)(2,1)S(1)} %get-tuple-element.39), channel_id=1, source_target_pairs={{0,2},{1,3},{2,4},{3,5},{4,6},{5,7},{6,0},{7,1},{8,10},{9,11},{10,... | collective-permute-start | bytes 1327112 | tf_op jit(solution)/shard_map/ppermute | solution.py:497
  22.5 30.5 %copy-start.10 = (bf16[256]{0:T(256)(128)(2,1)S(1)}, bf16[256]{0:T(256)(128)(2,1)}, u32[]{:S(2)}) copy-start(bf16[256]{0:T(256)(128)(2,1)} %param.18) | copy-start | bytes 1540
  22.5 39.1 %copy-start.9 = (f32[56,256]{1,0:T(8,128)S(1)}, f32[56,256]{1,0:T(8,128)}, u32[]{:S(2)}) copy-start(f32[56,256]{1,0:T(8,128)} %constant.5.clone.turns) | copy-start | bytes 172036
  22.5 20.0 %collective-permute-start.5 = (s16[432,512]{1,0:T(8,128)(2,1)S(1)}, s16[432,512]{1,0:T(8,128)(2,1)S(1)}, u32[]{:S(2)}, u32[]{:S(2)}) collective-permute-start(s16[432,512]{1,0:T(8,128)(2,1)S(1)} %relay.3), channel_id=1, source_target_pairs={{0,6},{1,7},{2,0},{3,1},{4,2},{5,3},{6,4},{7,5},{8,14},{9,15},{10,... | collective-permute-start | bytes 1327112 | tf_op jit(solution)/shard_map/ppermute | solution.py:497
  24.7 26.7 %collective-permute-start.2 = (s16[400,512]{1,0:T(8,128)(2,1)}, s16[400,512]{1,0:T(8,128)(2,1)S(1)}, u32[]{:S(2)}, u32[]{:S(2)}) collective-permute-start(s16[400,512]{1,0:T(8,128)(2,1)} %get-tuple-element.34), channel_id=1, source_target_pairs={{0,6},{1,7},{2,0},{3,1},{4,2},{5,3},{6,4},{7,5},{8,14},{9,15},{10,... | collective-permute-start | bytes 1228808 | tf_op jit(solution)/shard_map/ppermute | solution.py:497
  24.8 26.6 %collective-permute-start.1 = (s16[400,512]{1,0:T(8,128)(2,1)S(1)}, s16[400,512]{1,0:T(8,128)(2,1)S(1)}, u32[]{:S(2)}, u32[]{:S(2)}) collective-permute-start(s16[400,512]{1,0:T(8,128)(2,1)S(1)} %relay.2), channel_id=1, source_target_pairs={{0,2},{1,3},{2,4},{3,5},{4,6},{5,7},{6,0},{7,1},{8,10},{9,11},{10,... | collective-permute-start | bytes 1228808 | tf_op jit(solution)/shard_map/ppermute | solution.py:497
  26.1 16.4 %collective-permute-start.7 = (s16[48,512]{1,0:T(8,128)(2,1)S(1)}, s16[48,512]{1,0:T(8,128)(2,1)S(1)}, u32[]{:S(2)}, u32[]{:S(2)}) collective-permute-start(s16[48,512]{1,0:T(8,128)(2,1)S(1)} %get-tuple-element.41), channel_id=1, source_target_pairs={{0,4},{1,5},{2,6},{3,7},{4,0},{5,1},{6,2},{7,3},{8,12},{9,13},{10,... | collective-permute-start | bytes 147464 | tf_op jit(solution)/shard_map/ppermute | solution.py:497
  28.5 24.5 %all-to-all-start = ((bf16[32,16,128]{2,1,0:T(8,128)(2,1)}), bf16[32,16,128]{2,1,0:T(8,128)(2,1)S(1)}, u32[]{:S(2)}, u32[]{:S(2)}) async-start(bf16[32,16,128]{2,1,0:T(8,128)(2,1)} %get-tuple-element.28), calls=%async_computation | async-start | bytes 262144 | tf_op jit(solution)/shard_map/all_to_all | solution.py:513
  44.1 17.5 %collective-permute-start.8 = (s16[432,256]{1,0:T(8,128)(2,1)S(1)}, s16[432,256]{1,0:T(8,128)(2,1)S(1)}, u32[]{:S(2)}, u32[]{:S(2)}) collective-permute-start(s16[432,256]{1,0:T(8,128)(2,1)S(1)} %get-tuple-element.42), channel_id=1, source_target_pairs={{0,1},{1,0},{2,3},{3,2},{4,5},{5,4},{6,7},{7,6},{8,9},{9,8},{10,11... | collective-permute-start | bytes 663560 | tf_op jit(solution)/shard_map/ppermute | solution.py:518
  52.9 8.7 %collective-permute-start.3 = (s16[400,256]{1,0:T(8,128)(2,1)S(1)}, s16[400,256]{1,0:T(8,128)(2,1)S(1)}, u32[]{:S(2)}, u32[]{:S(2)}) collective-permute-start(s16[400,256]{1,0:T(8,128)(2,1)S(1)} %get-tuple-element.36), channel_id=1, source_target_pairs={{0,1},{1,0},{2,3},{3,2},{4,5},{5,4},{6,7},{7,6},{8,9},{9,8},{10,11... | collective-permute-start | bytes 614408 | tf_op jit(solution)/shard_map/ppermute | solution.py:518
  64.1 29.1 %all-to-all-start.1 = ((f32[32,24,128]{2,1,0:T(8,128)}), f32[32,24,128]{2,1,0:T(8,128)S(1)}, u32[]{:S(2)}, u32[]{:S(2)}) async-start(f32[32,24,128]{2,1,0:T(8,128)} %get-tuple-element.50), calls=%async_computation.1 | async-start | bytes 786432 | tf_op jit(solution)/shard_map/all_to_all | solution.py:527

commit v3 on v2

v3 whole, which is shorter than its diff:
```python
import jax
import jax.numpy as jnp
import numpy as np
from jax import lax
from jax.experimental import pallas as pl
from jax.experimental.pallas import tpu as pltpu
from jax.sharding import PartitionSpec as P

HW = 128
RANK = 32
ROPE_BASE = 1000000.0
NEG = -1e30
PARTS = ((0, 384), (384, 384))
LIMIT = 52 * 2**20
FAR_LIMIT = 54 * 2**20
NEAR_LIMIT = 52 * 2**20
BLK = 32
SROWS = 16
QMAX = 32766.0
MAGIC = 12582912.0
TOP_STEPS = (2.0**12, 2.0**-3, 2.0**-18)
TOTAL_STEPS = (2.0**-5, 2.0**-20)
F32 = jnp.float32
BF16 = jnp.bfloat16


def rope_tables(first, count, step=1):
    half = HW // 2
    freq = (ROPE_BASE ** (-(np.arange(half, dtype=np.float64) * 2.0) / HW)).astype(np.float32)
    angle = np.arange(first, first + count, step, dtype=np.float32)[:, None] * freq[None, :]
    cosine = np.cos(angle.astype(np.float64)).astype(np.float32)
    sine = np.sin(angle.astype(np.float64)).astype(np.float32)
    return np.concatenate([cosine, cosine], 1), np.concatenate([-sine, sine], 1)


def turn(values, cosine, sine):
    return values * cosine + pltpu.roll(values, HW // 2, 1) * sine


def nn(a, b):
    return lax.dot_general(a, b, (((1,), (0,)), ((), ())), preferred_element_type=F32)


def nt(a, b):
    return lax.dot_general(a, b, (((1,), (1,)), ((), ())), preferred_element_type=F32)


def near_int(values):
    return (values + MAGIC) - MAGIC


def encode(values, out_ref, peak_ref):
    rows, cols = values.shape
    blocks = rows // BLK
    peak_ref[...] = jnp.full(peak_ref.shape, 1e-30, F32)
    for b in range(blocks):
        peak_ref[b : b + 1, :] = jnp.max(jnp.abs(values[b * BLK : (b + 1) * BLK]), axis=0, keepdims=True)
    level = jnp.ceil(jnp.log2(jnp.maximum(peak_ref[...], 1e-30)) * 256.0) + 1.0
    inverse = jnp.exp2(level * (-1.0 / 256.0)) * QMAX
    for b in range(blocks):
        scaled = values[b * BLK : (b + 1) * BLK] * inverse[b : b + 1, :]
        code = near_int(scaled)
        out_ref[b * BLK : (b + 1) * BLK, :] = code.astype(jnp.int32).astype(jnp.int16)
    out_ref[rows : rows + SROWS, :] = level.astype(jnp.int32).astype(jnp.int16)


def scales(ref, rows):
    level = ref[rows : rows + SROWS, :].astype(jnp.int32).astype(F32)
    return jnp.exp2(level * (1.0 / 256.0)) * (1.0 / QMAX)


def decode(ref, scale, b):
    return ref[b * BLK : (b + 1) * BLK, :].astype(jnp.int32).astype(F32) * scale[b : b + 1, :]


def pieces(value, steps):
    got = []
    for step in steps:
        whole = near_int(value * (1.0 / step))
        value = value - whole * step
        got.append(whole)
    return got


def spread_up(up, span, rows):
    key_row = (lax.broadcasted_iota(jnp.int32, (rows, HW), 0) % (2 * RANK)) < RANK
    zero = jnp.zeros((rows, HW), BF16)
    parts = []
    for other in range(2):
        part = up[span, other * HW : (other + 1) * HW]
        parts += [jnp.where(key_row, part, zero), jnp.where(key_row, zero, part)]
    return jnp.concatenate(parts, axis=1)


def two_parts(values):
    high = values.astype(BF16)
    return high, (values - high.astype(F32)).astype(BF16)


def project_body(offs, places, adapter_of, parents, hidden, weight, down, up, latest, *refs):
    outs, (hx, wx, dp, d, u, tile, peaks, xl, mine, sems) = refs[:-10], refs[-10:]
    depth = hidden.shape[1]
    length, news = hidden.shape[0], latest.shape[0]
    (first0, rows0), (first1, rows1) = PARTS
    tp = lax.axis_index("tp")
    y, z = tp // 2, tp % 2
    adapter = adapter_of[lax.axis_index("rep")]
    pair = pl.ds(pl.multiple_of((adapter // 2) * (4 * RANK), 4 * RANK), 4 * RANK)

    def copy(src, dst, i):
        return pltpu.make_async_copy(src, dst, sems.at[i])

    blocks = []
    for k, off in enumerate(offs):
        made = []
        for other in range(2):
            head = ((y + off) % 4) * 2 + (1 - z if other else z)
            at = pl.ds(pl.multiple_of(head * (2 * HW), 2 * HW), 2 * HW)
            made.append(copy(weight.at[:, at], wx.at[k, pl.ds(0, depth), pl.ds(other * 2 * HW, 2 * HW)], 5 + 4 * k + other))
            at = pl.ds(pl.multiple_of(head * HW, HW), HW)
            made.append(copy(up.at[:, at], u.at[k, :, pl.ds(other * HW, HW)], 7 + 4 * k + other))
        blocks.append(made)
    early = [copy(down.at[:, pair], dp, 0), copy(hidden.at[pl.ds(first0, rows0), :], hx.at[pl.ds(first0, rows0), pl.ds(0, depth)], 1)]
    late = [
        copy(hidden.at[pl.ds(first1, rows1), :], hx.at[pl.ds(first1, rows1), pl.ds(0, depth)], 2),
        copy(latest, hx.at[pl.ds(length, news), pl.ds(0, depth)], 3),
        copy(down, d, 4),
    ]
    for c in early + blocks[0] + late + [c for made in blocks[1:] for c in made]:
        c.start()

    def name(c, carry):
        mine[pl.ds(c, 1), :] = jnp.full((1, HW), adapter_of[parents[c]], jnp.int32)
        return carry

    lax.fori_loop(0, news, name, 0)
    hx[length:, depth:] = jnp.zeros((news, 8 * RANK), BF16)

    def ranks(first, rows):
        span = slice(first, first + rows)
        got = nn(hx[span, :depth], dp[...])
        lane = lax.broadcasted_iota(jnp.int32, got.shape, 1)
        high, low = two_parts(jnp.where((lane // (2 * RANK)) == adapter % 2, got, 0.0))
        hx[span, depth : depth + 4 * RANK] = high
        hx[span, depth + 4 * RANK :] = low

    def part0(k):
        for c in blocks[k]:
            c.wait()
        ups = spread_up(u.at[k], pair, 4 * RANK)
        wx[k, depth : depth + 4 * RANK, :] = ups
        wx[k, depth + 4 * RANK :, :] = ups
        emit(0, offs[k], nn(hx[:rows0, :], wx[k]))

    def emit(part, off, values):
        ref, coded = places(outs, part, off)
        if coded:
            tile[: values.shape[0], :] = values
            encode(tile[: values.shape[0], :], ref, peaks)
        else:
            ref[...] = values

    for c in early:
        c.wait()
    ranks(first0, rows0)
    part0(0)
    for c in late:
        c.wait()
    ranks(first1, rows1)
    got = nn(hx[length:, :depth], d[...])
    lane = lax.broadcasted_iota(jnp.int32, got.shape, 1)
    high, low = two_parts(jnp.where((lane // (2 * RANK)) == mine[:, :1], got, 0.0))
    xl[:news, :] = high
    xl[news:, :] = low
    for k, off in enumerate(offs):
        if k:
            part0(k)
        added = nn(xl[...], spread_up(u.at[k], slice(None), up.shape[0]))
        ref, coded = places(outs, 1, off)
        to = tile if coded else ref
        to[...] = nn(hx[first1:, :], wx[k])
        to[rows1:, :] = to[rows1:, :] + (added[:news] + added[news:])
        if coded:
            encode(tile[...], ref, peaks)


def project_far(*args):
    return project((2,), lambda outs, part, off: (outs[part], True), 2, 0, *args)


def project_near(*args):
    table = {(0, 3): (0, True), (1, 1): (1, True), (0, 1): (2, False), (1, 3): (3, False), (0, 0): (4, False), (1, 0): (5, False)}

    def places(outs, part, off):
        at, coded = table[part, off]
        return outs[at], coded

    return project((3, 1, 0), places, 2, 4, *args)


def project(offs, places, codes, sums, limit, adapter_index, parents, hidden, weight, down, up, latest):
    depth = hidden.shape[1]
    length, news = hidden.shape[0], latest.shape[0]
    vmem = pl.BlockSpec(memory_space=pltpu.VMEM)
    hbm = pl.BlockSpec(memory_space=pltpu.HBM)
    smem = pl.BlockSpec(memory_space=pltpu.SMEM)
    rows = (PARTS[0][1], PARTS[1][1] + news)
    out_shape = [jax.ShapeDtypeStruct((rows[i % 2] + SROWS, 4 * HW), jnp.int16) for i in range(codes)]
    out_shape += [jax.ShapeDtypeStruct((rows[i % 2], 4 * HW), F32) for i in range(sums)]
    n = len(offs)
    return pl.pallas_call(
        lambda *refs: project_body(offs, places, *refs),
        in_specs=[smem, smem] + [hbm] * 5,
        out_specs=[vmem] * len(out_shape),
        out_shape=out_shape,
        scratch_shapes=[
            pltpu.VMEM((length + news, depth + 8 * RANK), BF16),
            pltpu.VMEM((n, depth + 8 * RANK, 4 * HW), BF16),
            pltpu.VMEM((depth, 4 * RANK), BF16),
            pltpu.VMEM(down.shape, BF16),
            pltpu.VMEM((n, up.shape[0], 2 * HW), BF16),
            pltpu.VMEM((rows[1], 4 * HW), F32),
            pltpu.VMEM((SROWS, 4 * HW), F32),
            pltpu.VMEM((2 * news, up.shape[0]), BF16),
            pltpu.VMEM((news, HW), jnp.int32),
            pltpu.SemaphoreType.DMA((5 + 4 * n,)),
        ],
        compiler_params=pltpu.CompilerParams(vmem_limit_bytes=limit),
        cost_estimate=pl.CostEstimate(
            flops=2 * length * depth * 4 * HW * n, bytes_accessed=2 * 10**6 * (n + 2), transcendentals=0),
        name="project%d" % n,
    )(adapter_index, parents, hidden, weight, down, up, latest)


def relay_body(came, near, out, peaks, whole):
    rows = near.shape[0]
    scale = scales(came, rows)
    for k in range(rows // BLK):
        span = slice(k * BLK, (k + 1) * BLK)
        whole[span, :] = near[span, :] + decode(came, scale, k)
    encode(whole[...], out, peaks)


def relay(came, near):
    rows, cols = near.shape
    return pl.pallas_call(
        relay_body,
        out_shape=jax.ShapeDtypeStruct((rows + SROWS, cols), jnp.int16),
        scratch_shapes=[pltpu.VMEM((SROWS, cols), F32), pltpu.VMEM((rows, cols), F32)],
        compiler_params=pltpu.CompilerParams(vmem_limit_bytes=LIMIT),
        cost_estimate=pl.CostEstimate(flops=rows * cols * 8, bytes_accessed=rows * cols * 8, transcendentals=0),
        name="relay",
    )(came, near)


def fold_body(a, b, own, out, keep, peaks, other):
    rows = own.shape[0]
    sa, sb = scales(a, rows), scales(b, rows)
    for k in range(rows // BLK):
        span = slice(k * BLK, (k + 1) * BLK)
        total = own[span, :] + decode(a, sa, k) + decode(b, sb, k)
        keep[span, :] = total[:, : 2 * HW]
        other[span, :] = total[:, 2 * HW :]
    encode(other[...], out, peaks)


def fold(a, b, own):
    rows = own.shape[0]
    return pl.pallas_call(
        fold_body,
        out_shape=[
            jax.ShapeDtypeStruct((rows + SROWS, 2 * HW), jnp.int16),
            jax.ShapeDtypeStruct((rows, 2 * HW), F32),
        ],
        scratch_shapes=[pltpu.VMEM((SROWS, 2 * HW), F32), pltpu.VMEM((rows, 2 * HW), F32)],
        compiler_params=pltpu.CompilerParams(vmem_limit_bytes=LIMIT),
        cost_estimate=pl.CostEstimate(flops=rows * 4 * HW * 8, bytes_accessed=rows * HW * 48, transcendentals=0),
        name="fold",
    )(a, b, own)


def dispatch_body(parents, lengths, queries, table, send, turned, ropes, place, counts, spread):
    comps = queries.shape[0]
    group = queries.shape[1] // HW

    def look(c, carry):
        ropes[pl.ds(c, 1), :] = table[pl.ds(lengths[c] - 1, 1), :]
        return carry

    lax.fori_loop(0, comps, look, 0)
    for h in range(group):
        part = queries[:, h * HW : (h + 1) * HW].astype(F32)
        part = turn(part, ropes[:, :HW], ropes[:, HW:])
        turned[pl.ds(h, comps, stride=group), :] = part.astype(BF16).astype(F32)
    spread[...] = jnp.zeros(spread.shape, F32)

    def clear(i, carry):
        counts[i] = 0
        return carry

    lax.fori_loop(0, counts.shape[0], clear, 0)

    def put(c, carry):
        p = parents[c]
        s = counts[p]
        counts[p] = s + 1
        at = 2 * p + s
        place[c] = at
        to = pl.multiple_of(at * group, group)
        spread[pl.ds(to, group), :] = turned[pl.ds(pl.multiple_of(c * group, group), group), :]
        return carry

    lax.fori_loop(0, comps, put, 0)
    send[...] = spread[...].astype(BF16).reshape(send.shape)


def dispatch(parents, lengths, queries, table, prompts):
    comps = queries.shape[0]
    group = queries.shape[1] // HW
    vmem = pl.BlockSpec(memory_space=pltpu.VMEM)
    smem = pl.BlockSpec(memory_space=pltpu.SMEM)
    return pl.pallas_call(
        dispatch_body,
        in_specs=[smem, smem, vmem, vmem],
        out_specs=[vmem, vmem, vmem, smem],
        out_shape=[
            jax.ShapeDtypeStruct((prompts, 2 * group, HW), BF16),
            jax.ShapeDtypeStruct((comps * group, HW), F32),
            jax.ShapeDtypeStruct((comps, 2 * HW), F32),
            jax.ShapeDtypeStruct((comps,), jnp.int32),
        ],
        scratch_shapes=[pltpu.SMEM((prompts,), jnp.int32), pltpu.VMEM((prompts * 2 * group, HW), F32)],
        compiler_params=pltpu.CompilerParams(vmem_limit_bytes=LIMIT),
        cost_estimate=pl.CostEstimate(flops=10**6, bytes_accessed=10**6, transcendentals=0),
        name="dispatch",
    )(parents, lengths, queries, table)


def suffix_body(lengths, turned, cache, came, keep, bias, ropes, latest, out, stats, scores, weights, whole):
    comps = ropes.shape[0]
    first = keep.shape[0] - comps
    group = turned.shape[0] // comps
    scale = HW ** -0.5
    whole[...] = keep[first:, :] + bias[...] + decode(came, scales(came, keep.shape[0]), first // BLK)
    key = turn(whole[:, :HW], ropes[:, :HW], ropes[:, HW:]).astype(BF16)
    value = whole[:, HW:].astype(BF16)
    latest[:, :HW] = key
    latest[:, HW:] = value

    def wide(rows):
        return jnp.broadcast_to(rows[:, None, :], (comps, group, HW)).reshape(comps * group, HW)

    slot = lax.broadcasted_iota(jnp.int32, (group, HW), 1)
    for c in range(comps):
        span = slice(c * group, (c + 1) * group)
        score = nt(turned[span, :].astype(BF16), cache[c, :, :HW]) * scale
        scores[span, :] = jnp.where(slot < lengths[c], score, NEG)
    own_score = jnp.sum(turned[...] * wide(key.astype(F32)), axis=1, keepdims=True) * scale
    masked = scores[...]
    top = jnp.maximum(jnp.max(masked, axis=1, keepdims=True), own_score)
    weight = jnp.exp(masked - top)
    own_weight = jnp.exp(own_score - top)
    total = jnp.sum(weight, axis=1, keepdims=True) + own_weight
    weights[...] = weight
    for c in range(comps):
        span = slice(c * group, (c + 1) * group)
        out[span, :] = nn(weights[span, :].astype(BF16), cache[c, :, HW:])
    out[...] = out[...] + own_weight.astype(BF16).astype(F32) * wide(value.astype(F32))
    lane = lax.broadcasted_iota(jnp.int32, stats.shape, 1)
    stats[...] = jnp.where(lane < HW // 2, top, total)


def suffix(lengths, turned, cache, came, keep, bias, ropes):
    comps = ropes.shape[0]
    rows = turned.shape[0]
    vmem = pl.BlockSpec(memory_space=pltpu.VMEM)
    return pl.pallas_call(
        suffix_body,
        in_specs=[pl.BlockSpec(memory_space=pltpu.SMEM)] + [vmem] * 6,
        out_shape=[
            jax.ShapeDtypeStruct((comps, 2 * HW), BF16),
            jax.ShapeDtypeStruct((rows, HW), F32),
            jax.ShapeDtypeStruct((rows, HW), F32),
        ],
        scratch_shapes=[pltpu.VMEM((rows, HW), F32), pltpu.VMEM((rows, HW), F32), pltpu.VMEM((comps, 2 * HW), F32)],
        compiler_params=pltpu.CompilerParams(vmem_limit_bytes=LIMIT),
        cost_estimate=pl.CostEstimate(flops=10**7, bytes_accessed=10**7, transcendentals=0),
        name="suffix",
    )(lengths, turned, cache, came, keep, bias, ropes)


def prefix_body(queries, bias, turns, *refs):
    chunks = len(PARTS)
    came, keep = refs[:chunks], refs[chunks : 2 * chunks]
    kv, out = refs[2 * chunks :]
    blocks = kv.shape[0] // BLK
    cos_in, sin_in = turns[blocks:, :HW], turns[blocks:, HW:]
    for i, (first, rows) in enumerate(PARTS):
        scale = scales(came[i], keep[i].shape[0])
        for k in range(rows // BLK):
            span = slice(first + k * BLK, first + (k + 1) * BLK)
            total = keep[i][k * BLK : (k + 1) * BLK, :] + decode(came[i], scale, k) + bias[...]
            at = first // BLK + k
            cos_at, sin_at = turns[at : at + 1, :HW], turns[at : at + 1, HW:]
            cosine, sine = cos_at * cos_in - sin_at * sin_in, sin_at * cos_in + cos_at * sin_in
            kv[span, :HW] = turn(total[:, :HW], cosine, sine).astype(BF16)
            kv[span, HW:] = total[:, HW:].astype(BF16)
    prompts, per, _ = queries.shape
    step = 8
    for s in range(0, prompts, step):
        q = queries[s : s + step].reshape(step * per, HW)
        scores = nt(q, kv[:, :HW]) * (HW ** -0.5)
        top = jnp.max(scores, axis=1, keepdims=True)
        weight = jnp.exp(scores - top)
        total = jnp.sum(weight, axis=1, keepdims=True)
        part = nn(weight.astype(BF16), kv[:, HW:])
        peak = jnp.maximum(jnp.max(jnp.abs(part), axis=1, keepdims=True), 1e-30)
        level = jnp.ceil(jnp.log2(peak) * 256.0) + 1.0
        code = near_int(part * (jnp.exp2(level * (-1.0 / 256.0)) * QMAX))
        lane = lax.broadcasted_iota(jnp.int32, (step * per, HW), 1)
        row = lax.broadcasted_iota(jnp.int32, (step * per, HW), 0) % per
        stat = jnp.zeros((step * per, HW), F32)
        for i, piece in enumerate(pieces(top, TOP_STEPS) + pieces(total, TOTAL_STEPS) + [level]):
            stat = stat + jnp.where(lane == row + i * per, piece, 0.0)
        stat = jnp.sum(stat.reshape(step, per, HW), axis=1, keepdims=True)
        whole = jnp.concatenate([code.reshape(step, per, HW), jnp.broadcast_to(stat, (step, 8, HW))], axis=1)
        out[s : s + step] = whole.astype(jnp.int32).astype(jnp.int16)


def prefix(queries, bias, turns, came, keep, length):
    prompts, per, _ = queries.shape
    return pl.pallas_call(
        prefix_body,
        out_shape=[
            jax.ShapeDtypeStruct((length, 2 * HW), BF16),
            jax.ShapeDtypeStruct((prompts, per + 8, HW), jnp.int16),
        ],
        compiler_params=pltpu.CompilerParams(vmem_limit_bytes=LIMIT),
        cost_estimate=pl.CostEstimate(flops=2 * 10**8, bytes_accessed=10**7, transcendentals=10**6),
        name="prefix",
    )(queries, bias, turns, *came, *keep)


def merge_body(place, back, out, stats, attn, spread, side, joined):
    prompts, per, _ = back.shape
    per -= 8
    rows = out.shape[0]
    comps = attn.shape[0]
    group = rows // comps
    came = back[...].astype(jnp.int32).astype(F32)
    spread[...] = came
    for c in range(comps):
        at = place[c]
        span = slice(c * group, (c + 1) * group)
        slot = at % 2
        joined[span, :] = spread[at // 2, pl.ds(pl.multiple_of(slot * group, group), group), :]
        side[span, :] = jnp.where(
            lax.broadcasted_iota(jnp.int32, (group, HW), 1) % per
            == lax.broadcasted_iota(jnp.int32, (group, HW), 0) + slot * group,
            spread[at // 2, per:, :], 0.0)
    lane = lax.broadcasted_iota(jnp.int32, (rows, HW), 1)
    stat = []
    for i in range(len(TOP_STEPS) + len(TOTAL_STEPS) + 1):
        stat.append(jnp.sum(jnp.where(lane // per == i, side[...], 0.0), axis=1, keepdims=True))
    top_p = sum(piece * step for piece, step in zip(stat, TOP_STEPS))
    total_p = sum(piece * step for piece, step in zip(stat[len(TOP_STEPS) :], TOTAL_STEPS))
    out_p = joined[...] * (jnp.exp2(stat[-1] * (1.0 / 256.0)) * (1.0 / QMAX))
    top_s, total_s = stats[:, :1], stats[:, HW // 2 : HW // 2 + 1]
    top = jnp.maximum(top_p, top_s)
    alpha = jnp.exp(top_p - top)
    beta = jnp.exp(top_s - top)
    joined[...] = (alpha * out_p + beta * out[...]) / (alpha * total_p + beta * total_s)
    for h in range(group):
        attn[:, h * HW : (h + 1) * HW] = joined[pl.ds(h, comps, stride=group), :].astype(BF16)


def merge(place, back, out, stats, comps):
    rows = out.shape[0]
    vmem = pl.BlockSpec(memory_space=pltpu.VMEM)
    smem = pl.BlockSpec(memory_space=pltpu.SMEM)
    return pl.pallas_call(
        merge_body,
        in_specs=[smem, vmem, vmem, vmem],
        out_specs=vmem,
        out_shape=jax.ShapeDtypeStruct((comps, rows // comps * HW), BF16),
        scratch_shapes=[pltpu.VMEM(back.shape, F32), pltpu.VMEM((rows, HW), F32), pltpu.VMEM((rows, HW), F32)],
        compiler_params=pltpu.CompilerParams(vmem_limit_bytes=LIMIT),
        cost_estimate=pl.CostEstimate(flops=10**6, bytes_accessed=10**6, transcendentals=10**5),
        name="merge",
    )(place, back, out, stats)


def on_device(
    prefix_hidden_states, latest_hidden, queries, suffix_key_cache, key_value_weight, key_value_bias,
    adapter_down_weight, adapter_up_weight, parents, adapter_index, suffix_length_count,
):
    length = prefix_hidden_states.shape[1]
    comps = latest_hidden.shape[0]
    prompts = adapter_index.shape[0]
    along_y = lambda d: [(a * 2 + b, ((a + d) % 4) * 2 + b) for a in range(4) for b in range(2)]
    along_z = [(a * 2 + b, a * 2 + 1 - b) for a in range(4) for b in range(2)]

    hidden = prefix_hidden_states[0]
    y_step = lambda value, d: lax.ppermute(value, "tp", along_y(d))
    parent = parents[:, 0]
    inputs = (adapter_index, parent, hidden, key_value_weight, adapter_down_weight, adapter_up_weight, latest_hidden)
    far0, far1 = project_far(FAR_LIMIT, *inputs)
    far0, far1 = y_step(far0, 1), y_step(far1, -1)
    direct0, direct1, near0, near1, own0, own1 = project_near(NEAR_LIMIT, *inputs)
    direct0 = y_step(direct0, -1)
    joined0 = relay(far0, near0)
    joined0, queries, far1 = lax.optimization_barrier((joined0, queries, far1))
    joined0 = y_step(joined0, 1)
    joined1 = relay(far1, near1)

    cos_t, sin_t = rope_tables(length + 1, suffix_key_cache.shape[1])
    table = jnp.asarray(np.concatenate([cos_t, sin_t], 1))
    to_prompts, turned, ropes, place = dispatch(parent, suffix_length_count, queries, table, prompts)
    here = lax.all_to_all(to_prompts, "rep", 0, 0, tiled=True)
    joined1, direct1, to_prompts = lax.optimization_barrier((joined1, direct1, to_prompts))
    direct1, joined1 = y_step(direct1, 1), y_step(joined1, -1)
    joined0, direct0, here = lax.optimization_barrier((joined0, direct0, here))
    code0, keep0 = fold(joined0, direct0, own0)
    came0 = lax.ppermute(code0, "tp", along_z)
    code1, keep1 = fold(joined1, direct1, own1)
    came1 = lax.ppermute(code1, "tp", along_z)
    came, keep = (came0, came1), (keep0, keep1)

    bias = key_value_bias.astype(F32).reshape(1, 2 * HW)
    latest_key_value, out_s, stats = suffix(
        suffix_length_count, turned, suffix_key_cache, came[1], keep[1], bias, ropes)
    blocks, within = rope_tables(0, length, BLK), rope_tables(0, BLK)
    turns = jnp.asarray(np.concatenate([np.concatenate(blocks, 1), np.concatenate(within, 1)], 0))
    prefix_kv, part = prefix(here, bias, turns, came, keep, length)
    back = lax.all_to_all(part, "rep", 0, 0, tiled=True)
    attn_out = merge(place, back, out_s, stats, comps)
    return prefix_kv[None], latest_key_value, attn_out


def solution(mesh):
    in_specs = (
        P("rep", None, "tp"), P("rep", "tp"), P("rep", "tp"), P("rep", None, "tp"), P("tp", None), P("tp"),
        P("tp", None), P(), P("rep", None), P(), P("rep"),
    )
    out_specs = (P("rep", None, "tp"), P("rep", "tp"), P("rep", "tp"))
    return jax.shard_map(on_device, mesh=mesh, in_specs=in_specs, out_specs=out_specs, check_vma=False)
```

time: 95.3 us -> 88.4 us (0.928)
  starting transfers between devices: 41.6 us -> 36 us
  local copies, waits for them, and re-layouts: 2.6 us -> 0.86 us
    all_to_all x1, starting transfers between devices: 15.3 us -> 8.62 us  [on_device(): back = lax.all_to_all(part, 'rep', 0, 0, tiled=True)]
    all_to_all x1, waiting for transfers between devices: 11 us -> 6.88 us  [on_device(): back = lax.all_to_all(part, 'rep', 0, 0, tiled=True)]
    all_to_all x1, waiting for transfers between devices: 0.01 us -> 2.39 us  [on_device(): here = lax.all_to_all(to_prompts, 'rep', 0, 0, tiled=True)]
    ppermute x2, starting transfers between devices: 7.4 us -> 9.21 us  [the longest x1 4.64 us: on_device(): came0 = lax.ppermute(code0, 'tp', along_z)]
    unnamed x23 -> x18, local copies, waits for them, and re-layouts: 2.6 us -> 0.86 us
    ppermute x2, waiting for transfers between devices: 8.57 us -> 10.2 us  [the longest x1 10.2 us: on_device(): came0 = lax.ppermute(code0, 'tp', along_z)]
    ppermute x7 -> x6, starting transfers between devices: 7.77 us -> 7 us  [on_device(): y_step = lambda value, d: lax.ppermute(value, 'tp', along_y(d))]
    ppermute x7 -> x6, waiting for transfers between devices: 2.87 us -> 2.77 us  [on_device(): y_step = lambda value, d: lax.ppermute(value, 'tp', along_y(d))]
  transfers between devices with their start and end apart: 11 -> 10, of which waited for: 3 -> 4; matrix products, arithmetic and copies ran while one was open for 0% -> 0% of each run, Pallas kernels for 20% -> 17%
where the time goes in v3:
time: 88.4 us; the launch traced here: 87.7 us
  starting transfers between devices  36 us (41%)
  Pallas kernels  27.8 us (31%)
  waiting for transfers between devices  22.2 us (25%)
    pallas_call x2, Pallas kernels, project(): pl.pallas_call(lambda *refs: project_body(offs, places, *refs), in_specs=...  14.6 us
    all_to_all x1, starting transfers between devices, on_device(): here = lax.all_to_all(to_prompts, 'rep', 0, 0, tiled=True)  11.2 us
    ppermute x1, waiting for transfers between devices, on_device(): came0 = lax.ppermute(code0, 'tp', along_z)  10.2 us
    all_to_all x1, starting transfers between devices, on_device(): back = lax.all_to_all(part, 'rep', 0, 0, tiled=True)  8.62 us
    ppermute x6, starting transfers between devices, on_device(): y_step = lambda value, d: lax.ppermute(value, 'tp', along_y(d))  7 us
    all_to_all x1, waiting for transfers between devices, on_device(): back = lax.all_to_all(part, 'rep', 0, 0, tiled=True)  6.88 us
    ppermute x1, starting transfers between devices, on_device(): came0 = lax.ppermute(code0, 'tp', along_z)  4.64 us
    ppermute x1, starting transfers between devices, on_device(): came1 = lax.ppermute(code1, 'tp', along_z)  4.57 us
  transfers between devices with their start and end apart: 10, of which 4 were waited for; matrix products, arithmetic and copies ran while one was open for 0% of the time, Pallas kernels for 17%

profile of v3, /device:TPU:1, one launch (start us, length us, event | category | flops | bytes accessed | tf_op | source)
XLA Modules:
  0.0 87.7 jit_solution(10205829139399513397)
XLA Ops:
  0.6 0.0 copy-start.2
  0.6 0.0 copy-start.4
  0.7 0.0 copy-start.6
  0.7 6.0 %project1.1 = (s16[400,512]{1,0:T(8,128)(2,1)}, s16[432,512]{1,0:T(8,128)(2,1)}) custom-call(s32[32]{0:T(128)} %refs_0_.3, s32[32]{0:T(128)} %bitcast.4, bf16[768,1024]{1,0:T(8,128)(2,1)} %bitcast.9, bf16[1024,2048]{1,0:T(8,128)(2,1)} %refs_3_.3, bf16[1024,512]{1,0:T(8,128)(2,1)} %refs_4_.3, bf16[512,1024]{1,0:T(8,128)(2,1)} %refs_5_.3, bf16[32,1024]{1,0:T(8,128)(2,1)} %refs_6_.3), custom_call_target="tpu_custom_call" | custom-call | flops 805306368 | bytes 6000000 | tf_op jit(solution)/shard_map/project1/pallas_call | solution.py:211
  6.6 3.6 %collective-permute-start.1 = (s16[432,512]{1,0:T(8,128)(2,1)}, s16[432,512]{1,0:T(8,128)(2,1)S(1)}, u32[]{:S(2)}, u32[]{:S(2)}) collective-permute-start(s16[432,512]{1,0:T(8,128)(2,1)} %get-tuple-element.34), channel_id=1, source_target_pairs={{0,6},{1,7},{2,0},{3,1},{4,2},{5,3},{6,4},{7,5},{8,14},{9,15},{10,... | collective-permute-start | bytes 1327112 | tf_op jit(solution)/shard_map/ppermute | solution.py:504
  10.3 0.0 collective-permute-start
  10.3 0.0 copy-done.2
  10.3 0.0 copy-done.4
  10.3 0.0 copy-done.6
  10.3 8.6 %project3.1 = (s16[400,512]{1,0:T(8,128)(2,1)}, s16[432,512]{1,0:T(8,128)(2,1)}, f32[384,512]{1,0:T(8,128)S(1)}, f32[416,512]{1,0:T(8,128)}, f32[384,512]{1,0:T(8,128)}, /*index=5*/f32[416,512]{1,0:T(8,128)}) custom-call(s32[32]{0:T(128)S(1)} %copy-done.6, s32[32]{0:T(128)S(1)} %bitcast.5, bf16[768,1024]{1,0:T(8,128)(2,1)} %bitcast.10, ...), custom_call_target="tpu_custom_call" | custom-call | flops 2415919104 | bytes 10000000 | tf_op jit(solution)/shard_map/project3/pallas_call | solution.py:211
  18.9 0.0 copy-start
  18.9 0.0 copy-start.1
  18.9 0.0 copy-start.3
  18.9 0.0 copy-start.5
  18.9 2.8 %collective-permute-done.came = s16[400,512]{1,0:T(8,128)(2,1)S(1)} collective-permute-done((s16[400,512]{1,0:T(8,128)(2,1)}, s16[400,512]{1,0:T(8,128)(2,1)S(1)}, u32[]{:S(2)}, u32[]{:S(2)}) %collective-permute-start) | collective-permute-done | bytes 409632 | tf_op jit(solution)/shard_map/ppermute | solution.py:504
  21.7 0.4 relay.2
  22.1 0.0 collective-permute-done.1.came
  22.1 0.0 copy-done
  22.1 0.4 relay.3
  22.6 0.0 copy-done.1
  22.6 0.0 copy-done.3
  22.6 0.0 copy-done.5
  22.6 0.0 copy-start.8
  22.6 2.0 %dispatch.1 = (bf16[32,16,128]{2,1,0:T(8,128)(2,1)}, f32[256,128]{1,0:T(8,128)S(1)}, f32[32,256]{1,0:T(8,128)S(1)}, s32[32]{0:T(128)S(1)}) custom-call(s32[32]{0:T(128)S(1)} %bitcast.6, s32[32]{0:T(128)S(1)} %copy-done.5, bf16[32,1024]{1,0:T(8,128)(2,1)S(1)} %copy-done.3, f32[128,256]{1,0:T(8,128)S(1)} %copy-done.1), custom_call_target="tpu_custom_call" | custom-call | flops 1000000 | bytes 1000000 | tf_op jit(solution)/shard_map/dispatch/pallas_call | solution.py:322
  24.6 0.7 collective-permute-start.5
  25.3 0.9 collective-permute-start.6
  26.2 1.8 %collective-permute-start.3 = (s16[400,512]{1,0:T(8,128)(2,1)}, s16[400,512]{1,0:T(8,128)(2,1)S(1)}, u32[]{:S(2)}, u32[]{:S(2)}) collective-permute-start(s16[400,512]{1,0:T(8,128)(2,1)} %get-tuple-element.36), channel_id=1, source_target_pairs={{0,6},{1,7},{2,0},{3,1},{4,2},{5,3},{6,4},{7,5},{8,14},{9,15},{10,... | collective-permute-start | bytes 1228808 | tf_op jit(solution)/shard_map/ppermute | solution.py:504
  28.0 0.0 collective-permute-start.2
  28.0 11.2 %all-to-all-start = ((bf16[32,16,128]{2,1,0:T(8,128)(2,1)}), bf16[32,16,128]{2,1,0:T(8,128)(2,1)S(1)}, u32[]{:S(2)}, u32[]{:S(2)}) async-start(bf16[32,16,128]{2,1,0:T(8,128)(2,1)} %get-tuple-element.38), calls=%async_computation | async-start | bytes 262144 | tf_op jit(solution)/shard_map/all_to_all | solution.py:519
  39.2 0.0 collective-permute-done.5.a
  39.2 0.0 collective-permute-done.6.b
  39.2 1.6 %fold.3 = (s16[432,256]{1,0:T(8,128)(2,1)S(1)}, f32[416,256]{1,0:T(8,128)S(1)}) custom-call(s16[432,512]{1,0:T(8,128)(2,1)S(1)} %collective-permute-done.5.a, s16[432,512]{1,0:T(8,128)(2,1)S(1)} %collective-permute-done.6.b, f32[416,512]{1,0:T(8,128)} %get-tuple-element.49.own), custom_call_target="tpu_custom_call" | custom-call | flops 1703936 | bytes 2555904 | tf_op jit(solution)/shard_map/fold/pallas_call | solution.py:269
  40.8 4.6 %collective-permute-start.7 = (s16[432,256]{1,0:T(8,128)(2,1)S(1)}, s16[432,256]{1,0:T(8,128)(2,1)S(1)}, u32[]{:S(2)}, u32[]{:S(2)}) collective-permute-start(s16[432,256]{1,0:T(8,128)(2,1)S(1)} %get-tuple-element.50), channel_id=1, source_target_pairs={{0,1},{1,0},{2,3},{3,2},{4,5},{5,4},{6,7},{7,6},{8,9},{9,8},{10,11... | collective-permute-start | bytes 663560 | tf_op jit(solution)/shard_map/ppermute | solution.py:526
  45.3 0.0 collective-permute-done.3.b
  45.3 2.4 %all-to-all-done.queries = bf16[32,16,128]{2,1,0:T(8,128)(2,1)S(1)} async-done(((bf16[32,16,128]{2,1,0:T(8,128)(2,1)}), bf16[32,16,128]{2,1,0:T(8,128)(2,1)S(1)}, u32[]{:S(2)}, u32[]{:S(2)}) %all-to-all-start) | async-done | bytes 131104 | tf_op jit(solution)/shard_map/all_to_all | solution.py:519
  47.7 0.0 collective-permute-done.2.a
  47.7 1.5 %fold.2 = (s16[400,256]{1,0:T(8,128)(2,1)S(1)}, f32[384,256]{1,0:T(8,128)S(1)}) custom-call(s16[400,512]{1,0:T(8,128)(2,1)S(1)} %collective-permute-done.2.a, s16[400,512]{1,0:T(8,128)(2,1)S(1)} %collective-permute-done.3.b, f32[384,512]{1,0:T(8,128)} %get-tuple-element.42.own), custom_call_target="tpu_custom_call" | custom-call | flops 1572864 | bytes 2359296 | tf_op jit(solution)/shard_map/fold/pallas_call | solution.py:269
  49.2 4.6 %collective-permute-start.4 = (s16[400,256]{1,0:T(8,128)(2,1)S(1)}, s16[400,256]{1,0:T(8,128)(2,1)S(1)}, u32[]{:S(2)}, u32[]{:S(2)}) collective-permute-start(s16[400,256]{1,0:T(8,128)(2,1)S(1)} %get-tuple-element.43), channel_id=1, source_target_pairs={{0,1},{1,0},{2,3},{3,2},{4,5},{5,4},{6,7},{7,6},{8,9},{9,8},{10,11... | collective-permute-start | bytes 614408 | tf_op jit(solution)/shard_map/ppermute | solution.py:524
  53.9 0.0 copy-done.8
  53.9 10.2 %collective-permute-done.4.refs_0_ = s16[400,256]{1,0:T(8,128)(2,1)S(1)} collective-permute-done((s16[400,256]{1,0:T(8,128)(2,1)S(1)}, s16[400,256]{1,0:T(8,128)(2,1)S(1)}, u32[]{:S(2)}, u32[]{:S(2)}) %collective-permute-start.4) | collective-permute-done | bytes 204832 | tf_op jit(solution)/shard_map/ppermute | solution.py:524
  64.1 0.0 collective-permute-done.7.refs_1_.came
  64.1 0.0 copy-start.7
  64.1 0.8 copy-done.7
  64.9 2.7 %prefix.1 = (bf16[768,256]{1,0:T(8,128)(2,1)}, s16[32,24,128]{2,1,0:T(8,128)(2,1)}) custom-call(bf16[32,16,128]{2,1,0:T(8,128)(2,1)S(1)} %all-to-all-done.queries, f32[1,256]{1,0:T(1,128)S(1)} %bitcast.7, f32[56,256]{1,0:T(8,128)S(1)} %copy-done.7, s16[400,256]{1,0:T(8,128)(2,1)S(1)} %collective-permute-done.4.refs_0_, ...), custom_call_target="tpu_custom_call" | custom-call | flops 200000000 | bytes 10000000 | tf_op jit(solution)/shard_map/prefix/pallas_call | solution.py:432
  67.5 8.6 %all-to-all-start.1 = ((s16[32,24,128]{2,1,0:T(8,128)(2,1)}), s16[32,24,128]{2,1,0:T(8,128)(2,1)S(1)}, u32[]{:S(2)}, u32[]{:S(2)}) async-start(s16[32,24,128]{2,1,0:T(8,128)(2,1)} %get-tuple-element.58), calls=%async_computation.1 | async-start | bytes 393216 | tf_op jit(solution)/shard_map/all_to_all | solution.py:535
  76.2 2.8 %suffix.1 = (bf16[32,256]{1,0:T(8,128)(2,1)}, f32[256,128]{1,0:T(8,128)S(1)}, f32[256,128]{1,0:T(8,128)S(1)}) custom-call(s32[32]{0:T(128)S(1)} %copy-done.5, f32[256,128]{1,0:T(8,128)S(1)} %get-tuple-element.54.turned, bf16[32,128,256]{2,1,0:T(8,128)(2,1)} %cache.1, s16[432,256]{1,0:T(8,128)(2,1)S(1)} %collective-permute-done.7.refs_1_.came, ...), custom_call_target="tpu_custom_call" | custom-call | flops 10000000 | bytes 10000000 | tf_op jit(solution)/shard_map/suffix/pallas_call | solution.py:377
  78.9 6.9 %all-to-all-done.1.back = s16[32,24,128]{2,1,0:T(8,128)(2,1)S(1)} async-done(((s16[32,24,128]{2,1,0:T(8,128)(2,1)}), s16[32,24,128]{2,1,0:T(8,128)(2,1)S(1)}, u32[]{:S(2)}, u32[]{:S(2)}) %all-to-all-start.1) | async-done | bytes 196640 | tf_op jit(solution)/shard_map/all_to_all | solution.py:535
  85.8 1.9 %merge.1 = bf16[32,1024]{1,0:T(8,128)(2,1)} custom-call(s32[32]{0:T(128)S(1)} %get-tuple-element.57.place, s16[32,24,128]{2,1,0:T(8,128)(2,1)S(1)} %all-to-all-done.1.back, f32[256,128]{1,0:T(8,128)S(1)} %get-tuple-element.59.out, f32[256,128]{1,0:T(8,128)S(1)} %get-tuple-element.60.stats), custom_call_target="tpu_custom_call" | custom-call | flops 1000000 | bytes 1000000 | tf_op jit(solution)/shard_map/merge/pallas_call | solution.py:481
  (1 shorter events, 0.0 us)
Async XLA Ops:
  0.6 9.6 %copy-start.2 = (bf16[32,1024]{1,0:T(8,128)(2,1)S(1)}, bf16[32,1024]{1,0:T(8,128)(2,1)}, u32[]{:S(2)}) copy-start(bf16[32,1024]{1,0:T(8,128)(2,1)} %refs_6_.3) | copy-start | bytes 196612
  0.6 9.6 %copy-start.4 = (s32[32,1]{0,1:T(1,128)S(1)}, s32[32,1]{0,1:T(1,128)}, u32[]{:S(2)}) copy-start(s32[32,1]{0,1:T(1,128)} %param.21) | copy-start | bytes 388
  0.7 9.6 %copy-start.6 = (s32[32]{0:T(128)S(1)}, s32[32]{0:T(128)}, u32[]{:S(2)}) copy-start(s32[32]{0:T(128)} %refs_0_.3) | copy-start | bytes 388
  6.6 15.5 %collective-permute-start.1 = (s16[432,512]{1,0:T(8,128)(2,1)}, s16[432,512]{1,0:T(8,128)(2,1)S(1)}, u32[]{:S(2)}, u32[]{:S(2)}) collective-permute-start(s16[432,512]{1,0:T(8,128)(2,1)} %get-tuple-element.34), channel_id=1, source_target_pairs={{0,6},{1,7},{2,0},{3,1},{4,2},{5,3},{6,4},{7,5},{8,14},{9,15},{10,... | collective-permute-start | bytes 1327112 | tf_op jit(solution)/shard_map/ppermute | solution.py:504
  10.3 11.4 %collective-permute-start = (s16[400,512]{1,0:T(8,128)(2,1)}, s16[400,512]{1,0:T(8,128)(2,1)S(1)}, u32[]{:S(2)}, u32[]{:S(2)}) collective-permute-start(s16[400,512]{1,0:T(8,128)(2,1)} %get-tuple-element.32), channel_id=1, source_target_pairs={{0,2},{1,3},{2,4},{3,5},{4,6},{5,7},{6,0},{7,1},{8,10},{9,11},{10,... | collective-permute-start | bytes 1228808 | tf_op jit(solution)/shard_map/ppermute | solution.py:504
  18.9 3.2 %copy-start = (f32[416,512]{1,0:T(8,128)S(1)}, f32[416,512]{1,0:T(8,128)}, u32[]{:S(2)}) copy-start(f32[416,512]{1,0:T(8,128)} %get-tuple-element.45.near) | copy-start | bytes 2555908
  18.9 3.6 %copy-start.1 = (f32[128,256]{1,0:T(8,128)S(1)}, f32[128,256]{1,0:T(8,128)}, u32[]{:S(2)}) copy-start(f32[128,256]{1,0:T(8,128)} %constant.4.clone.table) | copy-start | bytes 393220
  18.9 3.6 %copy-start.3 = (bf16[32,1024]{1,0:T(8,128)(2,1)S(1)}, bf16[32,1024]{1,0:T(8,128)(2,1)}, u32[]{:S(2)}) copy-start(bf16[32,1024]{1,0:T(8,128)(2,1)} %queries) | copy-start | bytes 196612
  18.9 3.6 %copy-start.5 = (s32[32]{0:T(128)S(1)}, s32[32]{0:T(128)}, u32[]{:S(2)}) copy-start(s32[32]{0:T(128)} %lengths.3) | copy-start | bytes 388
  22.6 31.3 %copy-start.8 = (bf16[256]{0:T(256)(128)(2,1)S(1)}, bf16[256]{0:T(256)(128)(2,1)}, u32[]{:S(2)}) copy-start(bf16[256]{0:T(256)(128)(2,1)} %param.18) | copy-start | bytes 1540
  24.6 14.5 %collective-permute-start.5 = (s16[432,512]{1,0:T(8,128)(2,1)S(1)}, s16[432,512]{1,0:T(8,128)(2,1)S(1)}, u32[]{:S(2)}, u32[]{:S(2)}) collective-permute-start(s16[432,512]{1,0:T(8,128)(2,1)S(1)} %relay.3), channel_id=1, source_target_pairs={{0,6},{1,7},{2,0},{3,1},{4,2},{5,3},{6,4},{7,5},{8,14},{9,15},{10,... | collective-permute-start | bytes 1327112 | tf_op jit(solution)/shard_map/ppermute | solution.py:504
  25.3 13.9 %collective-permute-start.6 = (s16[432,512]{1,0:T(8,128)(2,1)}, s16[432,512]{1,0:T(8,128)(2,1)S(1)}, u32[]{:S(2)}, u32[]{:S(2)}) collective-permute-start(s16[432,512]{1,0:T(8,128)(2,1)} %get-tuple-element.48), channel_id=1, source_target_pairs={{0,2},{1,3},{2,4},{3,5},{4,6},{5,7},{6,0},{7,1},{8,10},{9,11},{10,... | collective-permute-start | bytes 1327112 | tf_op jit(solution)/shard_map/ppermute | solution.py:504
  26.2 19.1 %collective-permute-start.3 = (s16[400,512]{1,0:T(8,128)(2,1)}, s16[400,512]{1,0:T(8,128)(2,1)S(1)}, u32[]{:S(2)}, u32[]{:S(2)}) collective-permute-start(s16[400,512]{1,0:T(8,128)(2,1)} %get-tuple-element.36), channel_id=1, source_target_pairs={{0,6},{1,7},{2,0},{3,1},{4,2},{5,3},{6,4},{7,5},{8,14},{9,15},{10,... | collective-permute-start | bytes 1228808 | tf_op jit(solution)/shard_map/ppermute | solution.py:504
  28.0 19.7 %collective-permute-start.2 = (s16[400,512]{1,0:T(8,128)(2,1)S(1)}, s16[400,512]{1,0:T(8,128)(2,1)S(1)}, u32[]{:S(2)}, u32[]{:S(2)}) collective-permute-start(s16[400,512]{1,0:T(8,128)(2,1)S(1)} %relay.2), channel_id=1, source_target_pairs={{0,2},{1,3},{2,4},{3,5},{4,6},{5,7},{6,0},{7,1},{8,10},{9,11},{10,... | collective-permute-start | bytes 1228808 | tf_op jit(solution)/shard_map/ppermute | solution.py:504
  28.0 19.7 %all-to-all-start = ((bf16[32,16,128]{2,1,0:T(8,128)(2,1)}), bf16[32,16,128]{2,1,0:T(8,128)(2,1)S(1)}, u32[]{:S(2)}, u32[]{:S(2)}) async-start(bf16[32,16,128]{2,1,0:T(8,128)(2,1)} %get-tuple-element.38), calls=%async_computation | async-start | bytes 262144 | tf_op jit(solution)/shard_map/all_to_all | solution.py:519
  40.8 23.3 %collective-permute-start.7 = (s16[432,256]{1,0:T(8,128)(2,1)S(1)}, s16[432,256]{1,0:T(8,128)(2,1)S(1)}, u32[]{:S(2)}, u32[]{:S(2)}) collective-permute-start(s16[432,256]{1,0:T(8,128)(2,1)S(1)} %get-tuple-element.50), channel_id=1, source_target_pairs={{0,1},{1,0},{2,3},{3,2},{4,5},{5,4},{6,7},{7,6},{8,9},{9,8},{10,11... | collective-permute-start | bytes 663560 | tf_op jit(solution)/shard_map/ppermute | solution.py:526
  49.2 14.8 %collective-permute-start.4 = (s16[400,256]{1,0:T(8,128)(2,1)S(1)}, s16[400,256]{1,0:T(8,128)(2,1)S(1)}, u32[]{:S(2)}, u32[]{:S(2)}) collective-permute-start(s16[400,256]{1,0:T(8,128)(2,1)S(1)} %get-tuple-element.43), channel_id=1, source_target_pairs={{0,1},{1,0},{2,3},{3,2},{4,5},{5,4},{6,7},{7,6},{8,9},{9,8},{10,11... | collective-permute-start | bytes 614408 | tf_op jit(solution)/shard_map/ppermute | solution.py:524
  64.1 0.8 copy-start.7
  67.5 18.3 %all-to-all-start.1 = ((s16[32,24,128]{2,1,0:T(8,128)(2,1)}), s16[32,24,128]{2,1,0:T(8,128)(2,1)S(1)}, u32[]{:S(2)}, u32[]{:S(2)}) async-start(s16[32,24,128]{2,1,0:T(8,128)(2,1)} %get-tuple-element.58), calls=%async_computation.1 | async-start | bytes 393216 | tf_op jit(solution)/shard_map/all_to_all | solution.py:535

commit v4 on v3

--- a/solution.py
+++ b/solution.py
@@ -11,9 +11,9 @@
 ROPE_BASE = 1000000.0
 NEG = -1e30
 PARTS = ((0, 384), (384, 384))
-LIMIT = 52 * 2**20
-FAR_LIMIT = 54 * 2**20
-NEAR_LIMIT = 52 * 2**20
+LIMIT = 16 * 2**20
+FAR_LIMIT = 16 * 2**20
+NEAR_LIMIT = 20 * 2**20
 BLK = 32
 SROWS = 16
 QMAX = 32766.0
@@ -97,8 +97,12 @@
     return high, (values - high.astype(F32)).astype(BF16)
 
 
-def project_body(offs, places, adapter_of, parents, hidden, weight, down, up, latest, *refs):
-    outs, (hx, wx, dp, d, u, tile, peaks, xl, mine, sems) = refs[:-10], refs[-10:]
+def project_body(offs, places, known, adapter_of, parents, hidden, weight, down, up, latest, *refs):
+    if known:
+        (xr_in, xl), refs = refs[:2], refs[2:]
+        outs, (hx, wx, u, tile, peaks, sems) = refs[:-6], refs[-6:]
+    else:
+        outs, (xr_out, xl), (hx, wx, u, tile, peaks, dp, d, mine, sems) = refs[:-11], refs[-11:-9], refs[-9:]
     depth = hidden.shape[1]
     length, news = hidden.shape[0], latest.shape[0]
     (first0, rows0), (first1, rows1) = PARTS
@@ -120,21 +124,26 @@
             at = pl.ds(pl.multiple_of(head * HW, HW), HW)
             made.append(copy(up.at[:, at], u.at[k, :, pl.ds(other * HW, HW)], 7 + 4 * k + other))
         blocks.append(made)
-    early = [copy(down.at[:, pair], dp, 0), copy(hidden.at[pl.ds(first0, rows0), :], hx.at[pl.ds(first0, rows0), pl.ds(0, depth)], 1)]
+    early = [copy(hidden.at[pl.ds(first0, rows0), :], hx.at[pl.ds(first0, rows0), pl.ds(0, depth)], 1)]
     late = [
         copy(hidden.at[pl.ds(first1, rows1), :], hx.at[pl.ds(first1, rows1), pl.ds(0, depth)], 2),
         copy(latest, hx.at[pl.ds(length, news), pl.ds(0, depth)], 3),
-        copy(down, d, 4),
     ]
+    if known:
+        hx[:, depth:] = xr_in[...]
+    else:
+        early.insert(0, copy(down.at[:, pair], dp, 0))
+        late.append(copy(down, d, 4))
     for c in early + blocks[0] + late + [c for made in blocks[1:] for c in made]:
         c.start()
 
-    def name(c, carry):
-        mine[pl.ds(c, 1), :] = jnp.full((1, HW), adapter_of[parents[c]], jnp.int32)
-        return carry
-
-    lax.fori_loop(0, news, name, 0)
-    hx[length:, depth:] = jnp.zeros((news, 8 * RANK), BF16)
+    if not known:
+        def name(c, carry):
+            mine[pl.ds(c, 1), :] = jnp.full((1, HW), adapter_of[parents[c]], jnp.int32)
+            return carry
+
+        lax.fori_loop(0, news, name, 0)
+        hx[length:, depth:] = jnp.zeros((news, 8 * RANK), BF16)
 
     def ranks(first, rows):
         span = slice(first, first + rows)
@@ -162,16 +171,19 @@
 
     for c in early:
         c.wait()
-    ranks(first0, rows0)
+    if not known:
+        ranks(first0, rows0)
     part0(0)
     for c in late:
         c.wait()
-    ranks(first1, rows1)
-    got = nn(hx[length:, :depth], d[...])
-    lane = lax.broadcasted_iota(jnp.int32, got.shape, 1)
-    high, low = two_parts(jnp.where((lane // (2 * RANK)) == mine[:, :1], got, 0.0))
-    xl[:news, :] = high
-    xl[news:, :] = low
+    if not known:
+        ranks(first1, rows1)
+        got = nn(hx[length:, :depth], d[...])
+        lane = lax.broadcasted_iota(jnp.int32, got.shape, 1)
+        high, low = two_parts(jnp.where((lane // (2 * RANK)) == mine[:, :1], got, 0.0))
+        xl[:news, :] = high
+        xl[news:, :] = low
+        xr_out[...] = hx[:, depth:]
     for k, off in enumerate(offs):
         if k:
             part0(k)
@@ -185,7 +197,7 @@
 
 
 def project_far(*args):
-    return project((2,), lambda outs, part, off: (outs[part], True), 2, 0, *args)
+    return project((2,), lambda outs, part, off: (outs[part], True), 2, 0, *args, ())
 
 
 def project_near(*args):
@@ -198,7 +210,7 @@
     return project((3, 1, 0), places, 2, 4, *args)
 
 
-def project(offs, places, codes, sums, limit, adapter_index, parents, hidden, weight, down, up, latest):
+def project(offs, places, codes, sums, limit, adapter_index, parents, hidden, weight, down, up, latest, known):
     depth = hidden.shape[1]
     length, news = hidden.shape[0], latest.shape[0]
     vmem = pl.BlockSpec(memory_space=pltpu.VMEM)
@@ -208,49 +220,56 @@
     out_shape = [jax.ShapeDtypeStruct((rows[i % 2] + SROWS, 4 * HW), jnp.int16) for i in range(codes)]
     out_shape += [jax.ShapeDtypeStruct((rows[i % 2], 4 * HW), F32) for i in range(sums)]
     n = len(offs)
-    return pl.pallas_call(
-        lambda *refs: project_body(offs, places, *refs),
-        in_specs=[smem, smem] + [hbm] * 5,
+    ranks = [
+        jax.ShapeDtypeStruct((length + news, 8 * RANK), BF16),
+        jax.ShapeDtypeStruct((2 * news, up.shape[0]), BF16),
+    ]
+    if known:
+        own = []
+    else:
+        out_shape += ranks
+        own = [pltpu.VMEM((depth, 4 * RANK), BF16), pltpu.VMEM(down.shape, BF16), pltpu.VMEM((news, HW), jnp.int32)]
+    return pl.pallas_call(
+        lambda *refs: project_body(offs, places, bool(known), *refs),
+        in_specs=[smem, smem] + [hbm] * 5 + [vmem] * len(known),
         out_specs=[vmem] * len(out_shape),
         out_shape=out_shape,
         scratch_shapes=[
             pltpu.VMEM((length + news, depth + 8 * RANK), BF16),
             pltpu.VMEM((n, depth + 8 * RANK, 4 * HW), BF16),
-            pltpu.VMEM((depth, 4 * RANK), BF16),
-            pltpu.VMEM(down.shape, BF16),
             pltpu.VMEM((n, up.shape[0], 2 * HW), BF16),
             pltpu.VMEM((rows[1], 4 * HW), F32),
             pltpu.VMEM((SROWS, 4 * HW), F32),
-            pltpu.VMEM((2 * news, up.shape[0]), BF16),
-            pltpu.VMEM((news, HW), jnp.int32),
+            *own,
             pltpu.SemaphoreType.DMA((5 + 4 * n,)),
         ],
         compiler_params=pltpu.CompilerParams(vmem_limit_bytes=limit),
         cost_estimate=pl.CostEstimate(
             flops=2 * length * depth * 4 * HW * n, bytes_accessed=2 * 10**6 * (n + 2), transcendentals=0),
         name="project%d" % n,
-    )(adapter_index, parents, hidden, weight, down, up, latest)
-
-
-def relay_body(came, near, out, peaks, whole):
-    rows = near.shape[0]
-    scale = scales(came, rows)
-    for k in range(rows // BLK):
-        span = slice(k * BLK, (k + 1) * BLK)
-        whole[span, :] = near[span, :] + decode(came, scale, k)
-    encode(whole[...], out, peaks)
-
-
-def relay(came, near):
-    rows, cols = near.shape
+    )(adapter_index, parents, hidden, weight, down, up, latest, *known)
+
+
+def relay_body(came0, near0, came1, near1, out0, out1, peaks, whole):
+    for came, near, out in ((came0, near0, out0), (came1, near1, out1)):
+        rows = near.shape[0]
+        scale = scales(came, rows)
+        for k in range(rows // BLK):
+            span = slice(k * BLK, (k + 1) * BLK)
+            whole[span, :] = near[span, :] + decode(came, scale, k)
+        encode(whole[:rows, :], out, peaks)
+
+
+def relay(came0, near0, came1, near1):
+    rows, cols = max(near0.shape[0], near1.shape[0]), near0.shape[1]
     return pl.pallas_call(
         relay_body,
-        out_shape=jax.ShapeDtypeStruct((rows + SROWS, cols), jnp.int16),
+        out_shape=[jax.ShapeDtypeStruct(came.shape, jnp.int16) for came in (came0, came1)],
         scratch_shapes=[pltpu.VMEM((SROWS, cols), F32), pltpu.VMEM((rows, cols), F32)],
         compiler_params=pltpu.CompilerParams(vmem_limit_bytes=LIMIT),
-        cost_estimate=pl.CostEstimate(flops=rows * cols * 8, bytes_accessed=rows * cols * 8, transcendentals=0),
+        cost_estimate=pl.CostEstimate(flops=1, bytes_accessed=1, transcendentals=0),
         name="relay",
-    )(came, near)
+    )(came0, near0, came1, near1)
 
 
 def fold_body(a, b, own, out, keep, peaks, other):
@@ -274,7 +293,7 @@
         ],
         scratch_shapes=[pltpu.VMEM((SROWS, 2 * HW), F32), pltpu.VMEM((rows, 2 * HW), F32)],
         compiler_params=pltpu.CompilerParams(vmem_limit_bytes=LIMIT),
-        cost_estimate=pl.CostEstimate(flops=rows * 4 * HW * 8, bytes_accessed=rows * HW * 48, transcendentals=0),
+        cost_estimate=pl.CostEstimate(flops=1, bytes_accessed=1, transcendentals=0),
         name="fold",
     )(a, b, own)
 
@@ -331,7 +350,7 @@
         ],
         scratch_shapes=[pltpu.SMEM((prompts,), jnp.int32), pltpu.VMEM((prompts * 2 * group, HW), F32)],
         compiler_params=pltpu.CompilerParams(vmem_limit_bytes=LIMIT),
-        cost_estimate=pl.CostEstimate(flops=10**6, bytes_accessed=10**6, transcendentals=0),
+        cost_estimate=pl.CostEstimate(flops=1, bytes_accessed=1, transcendentals=0),
         name="dispatch",
     )(parents, lengths, queries, table)
 
@@ -503,22 +522,25 @@
     hidden = prefix_hidden_states[0]
     y_step = lambda value, d: lax.ppermute(value, "tp", along_y(d))
     parent = parents[:, 0]
+    in_hbm = lambda value: pltpu.with_memory_space_constraint(value, pltpu.HBM)
+    hidden, key_value_weight, adapter_down_weight, adapter_up_weight, latest_hidden = map(
+        in_hbm, (hidden, key_value_weight, adapter_down_weight, adapter_up_weight, latest_hidden))
+    adapter_index, parent = in_hbm(adapter_index), in_hbm(parent)
     inputs = (adapter_index, parent, hidden, key_value_weight, adapter_down_weight, adapter_up_weight, latest_hidden)
-    far0, far1 = project_far(FAR_LIMIT, *inputs)
+    far0, far1, *known = project_far(FAR_LIMIT, *inputs)
     far0, far1 = y_step(far0, 1), y_step(far1, -1)
-    direct0, direct1, near0, near1, own0, own1 = project_near(NEAR_LIMIT, *inputs)
-    direct0 = y_step(direct0, -1)
-    joined0 = relay(far0, near0)
-    joined0, queries, far1 = lax.optimization_barrier((joined0, queries, far1))
-    joined0 = y_step(joined0, 1)
-    joined1 = relay(far1, near1)
+    direct0, direct1, near0, near1, own0, own1 = project_near(NEAR_LIMIT, *inputs, known)
+    direct0, queries = lax.optimization_barrier((direct0, queries))
 
     cos_t, sin_t = rope_tables(length + 1, suffix_key_cache.shape[1])
     table = jnp.asarray(np.concatenate([cos_t, sin_t], 1))
     to_prompts, turned, ropes, place = dispatch(parent, suffix_length_count, queries, table, prompts)
+    near0, near1, to_prompts = lax.optimization_barrier((near0, near1, to_prompts))
+    joined0, joined1 = relay(far0, near0, far1, near1)
+    joined0, joined1, to_prompts = lax.optimization_barrier((joined0, joined1, to_prompts))
+    joined0, direct0 = y_step(joined0, 1), y_step(direct0, -1)
+    joined1, direct1 = y_step(joined1, -1), y_step(direct1, 1)
     here = lax.all_to_all(to_prompts, "rep", 0, 0, tiled=True)
-    joined1, direct1, to_prompts = lax.optimization_barrier((joined1, direct1, to_prompts))
-    direct1, joined1 = y_step(direct1, 1), y_step(joined1, -1)
     joined0, direct0, here = lax.optimization_barrier((joined0, direct0, here))
     code0, keep0 = fold(joined0, direct0, own0)
     came0 = lax.ppermute(code0, "tp", along_z)
@@ -528,10 +550,10 @@
 
     bias = key_value_bias.astype(F32).reshape(1, 2 * HW)
     latest_key_value, out_s, stats = suffix(
-        suffix_length_count, turned, suffix_key_cache, came[1], keep[1], bias, ropes)
+        suffix_length_count, turned, in_hbm(suffix_key_cache), came[1], keep[1], bias, ropes)
     blocks, within = rope_tables(0, length, BLK), rope_tables(0, BLK)
     turns = jnp.asarray(np.concatenate([np.concatenate(blocks, 1), np.concatenate(within, 1)], 0))
-    prefix_kv, part = prefix(here, bias, turns, came, keep, length)
+    prefix_kv, part = prefix(here, bias, in_hbm(turns), came, keep, length)
     back = lax.all_to_all(part, "rep", 0, 0, tiled=True)
     attn_out = merge(place, back, out_s, stats, comps)
     return prefix_kv[None], latest_key_value, attn_out

time: 88.4 us -> 84.5 us (0.956)
  starting transfers between devices: 36 us -> 34 us
  Pallas kernels: 27.8 us -> 26.7 us
    pallas_call x4 -> x3, Pallas kernels: 15.4 us -> 13.8 us  [the longest x2 12.2 us: project(): pl.pallas_call(lambda *refs: project_body(offs, places, bool(known), *ref...]
    ppermute x6, waiting for transfers between devices: 2.77 us -> 1.8 us  [on_device(): y_step = lambda value, d: lax.ppermute(value, 'tp', along_y(d))]
    pallas_call x1, Pallas kernels: 2.66 us -> 3.59 us  [prefix(): pl.pallas_call(prefix_body, out_shape=[jax.ShapeDtypeStruct((length, 2 *...]
  transfers between devices with their start and end apart: 10 -> 10, of which waited for: 4 -> 4; matrix products, arithmetic and copies ran while one was open for 0% -> 0% of each run, Pallas kernels for 17% -> 19%
where the time goes in v4:
time: 84.5 us; the launch traced here: 84.2 us
  starting transfers between devices  34 us (40%)
  Pallas kernels  26.7 us (32%)
  waiting for transfers between devices  22.8 us (27%)
    pallas_call x2, Pallas kernels, project(): pl.pallas_call(lambda *refs: project_body(offs, places, bool(known), *ref...  12.2 us
    all_to_all x1, starting transfers between devices, on_device(): here = lax.all_to_all(to_prompts, 'rep', 0, 0, tiled=True)  11.3 us
    ppermute x1, waiting for transfers between devices, on_device(): came0 = lax.ppermute(code0, 'tp', along_z)  10.9 us
    all_to_all x1, starting transfers between devices, on_device(): back = lax.all_to_all(part, 'rep', 0, 0, tiled=True)  7.97 us
    all_to_all x1, waiting for transfers between devices, on_device(): back = lax.all_to_all(part, 'rep', 0, 0, tiled=True)  6.88 us
    ppermute x6, starting transfers between devices, on_device(): y_step = lambda value, d: lax.ppermute(value, 'tp', along_y(d))  6.22 us
    ppermute x1, starting transfers between devices, on_device(): came0 = lax.ppermute(code0, 'tp', along_z)  4.3 us
    ppermute x1, starting transfers between devices, on_device(): came1 = lax.ppermute(code1, 'tp', along_z)  4.21 us
  transfers between devices with their start and end apart: 10, of which 4 were waited for; matrix products, arithmetic and copies ran while one was open for 0% of the time, Pallas kernels for 19%

profile of v4, /device:TPU:1, one launch (start us, length us, event | category | flops | bytes accessed | tf_op | source)
XLA Modules:
  0.0 84.2 jit_solution(15833259564164948802)
XLA Ops:
  0.6 5.1 %project1.1 = (s16[400,512]{1,0:T(8,128)(2,1)S(1)}, s16[432,512]{1,0:T(8,128)(2,1)S(1)}, bf16[800,256]{1,0:T(8,128)(2,1)S(1)}, bf16[64,512]{1,0:T(8,128)(2,1)S(1)}) custom-call(s32[32]{0:T(128)} %refs_0_.3, s32[32]{0:T(128)} %bitcast.8, bf16[768,1024]{1,0:T(8,128)(2,1)} %bitcast.6, bf16[1024,2048]{1,0:T(8,128)(2,1)} %refs_3_.3, bf16[1024,512]{1,0:T(8,128)(2,1)} %refs_4_.3, ...), custom_call_target="tpu_custom_call" | custom-call | flops 805306368 | bytes 6000000 | tf_op jit(solution)/shard_map/project1/pallas_call | solution.py:232
  5.7 3.6 %collective-permute-start.1 = (s16[432,512]{1,0:T(8,128)(2,1)S(1)}, s16[432,512]{1,0:T(8,128)(2,1)S(1)}, u32[]{:S(2)}, u32[]{:S(2)}) collective-permute-start(s16[432,512]{1,0:T(8,128)(2,1)S(1)} %get-tuple-element.48), channel_id=1, source_target_pairs={{0,6},{1,7},{2,0},{3,1},{4,2},{5,3},{6,4},{7,5},{8,14},{9,15},{10,... | collective-permute-start | bytes 1327112 | tf_op jit(solution)/shard_map/ppermute | solution.py:523
  9.4 0.0 collective-permute-start
  9.4 0.0 copy-start
  9.4 0.0 copy-start.1
  9.4 0.0 copy-start.2
  9.4 7.1 %project3.1 = (s16[400,512]{1,0:T(8,128)(2,1)}, s16[432,512]{1,0:T(8,128)(2,1)}, f32[384,512]{1,0:T(8,128)S(1)}, f32[416,512]{1,0:T(8,128)S(1)}, f32[384,512]{1,0:T(8,128)S(1)}, /*index=5*/f32[416,512]{1,0:T(8,128)S(1)}) custom-call(s32[32]{0:T(128)} %refs_0_.3, s32[32]{0:T(128)} %bitcast.9, bf16[768,1024]{1,0:T(8,128)(2,1)} %bitcast.7, ...), custom_call_target="tpu_custom_call" | custom-call | flops 2415919104 | bytes 10000000 | tf_op jit(solution)/shard_map/project3/pallas_call | solution.py:232
  16.5 0.1 collective-permute-start.6
  16.6 0.0 copy-done
  16.6 0.0 copy-done.1
  16.7 0.0 copy-done.2
  16.7 2.1 %dispatch.1 = (bf16[32,16,128]{2,1,0:T(8,128)(2,1)}, f32[256,128]{1,0:T(8,128)S(1)}, f32[32,256]{1,0:T(8,128)S(1)}, s32[32]{0:T(128)S(1)}) custom-call(s32[32]{0:T(128)} %bitcast.10, s32[32]{0:T(128)S(1)} %copy-done.2, bf16[32,1024]{1,0:T(8,128)(2,1)S(1)} %copy-done.1, f32[128,256]{1,0:T(8,128)S(1)} %copy-done), custom_call_target="tpu_custom_call" | custom-call | flops 1 | bytes 1 | tf_op jit(solution)/shard_map/dispatch/pallas_call | solution.py:341
  18.8 1.8 %collective-permute-done.came0 = s16[400,512]{1,0:T(8,128)(2,1)S(1)} collective-permute-done((s16[400,512]{1,0:T(8,128)(2,1)S(1)}, s16[400,512]{1,0:T(8,128)(2,1)S(1)}, u32[]{:S(2)}, u32[]{:S(2)}) %collective-permute-start) | collective-permute-done | bytes 409632 | tf_op jit(solution)/shard_map/ppermute | solution.py:523
  20.6 0.0 collective-permute-done.1.came1
  20.6 1.6 %relay.1 = (s16[400,512]{1,0:T(8,128)(2,1)}, s16[432,512]{1,0:T(8,128)(2,1)}) custom-call(s16[400,512]{1,0:T(8,128)(2,1)S(1)} %collective-permute-done.came0, f32[384,512]{1,0:T(8,128)S(1)} %get-tuple-element.47.near0, s16[432,512]{1,0:T(8,128)(2,1)S(1)} %collective-permute-done.1.came1, f32[416,512]{1,0:T(8,128)S(1)} %get-tuple-element.49.near1), custom_call_target="tpu_custom_call" | custom-call | flops 1 | bytes 1 | tf_op jit(solution)/shard_map/relay/pallas_call | solution.py:265
  22.2 0.0 copy-start.3
  22.2 1.0 %collective-permute-start.5 = (s16[432,512]{1,0:T(8,128)(2,1)}, s16[432,512]{1,0:T(8,128)(2,1)S(1)}, u32[]{:S(2)}, u32[]{:S(2)}) collective-permute-start(s16[432,512]{1,0:T(8,128)(2,1)} %get-tuple-element.61), channel_id=1, source_target_pairs={{0,6},{1,7},{2,0},{3,1},{4,2},{5,3},{6,4},{7,5},{8,14},{9,15},{10,... | collective-permute-start | bytes 1327112 | tf_op jit(solution)/shard_map/ppermute | solution.py:523
  23.2 1.3 %collective-permute-start.3 = (s16[400,512]{1,0:T(8,128)(2,1)}, s16[400,512]{1,0:T(8,128)(2,1)S(1)}, u32[]{:S(2)}, u32[]{:S(2)}) collective-permute-start(s16[400,512]{1,0:T(8,128)(2,1)} %get-tuple-element.54), channel_id=1, source_target_pairs={{0,6},{1,7},{2,0},{3,1},{4,2},{5,3},{6,4},{7,5},{8,14},{9,15},{10,... | collective-permute-start | bytes 1228808 | tf_op jit(solution)/shard_map/ppermute | solution.py:523
  24.5 0.2 collective-permute-start.2
  24.7 11.3 %all-to-all-start = ((bf16[32,16,128]{2,1,0:T(8,128)(2,1)}), bf16[32,16,128]{2,1,0:T(8,128)(2,1)}, u32[]{:S(2)}, u32[]{:S(2)}) async-start(bf16[32,16,128]{2,1,0:T(8,128)(2,1)} %get-tuple-element.55), calls=%async_computation | async-start | bytes 262144 | tf_op jit(solution)/shard_map/all_to_all | solution.py:543
  36.0 0.0 collective-permute-done.6.b
  36.0 0.0 collective-permute-done.5.a
  36.0 1.1 %fold.3 = (s16[432,256]{1,0:T(8,128)(2,1)}, f32[416,256]{1,0:T(8,128)S(1)}) custom-call(s16[432,512]{1,0:T(8,128)(2,1)S(1)} %collective-permute-done.5.a, s16[432,512]{1,0:T(8,128)(2,1)S(1)} %collective-permute-done.6.b, f32[416,512]{1,0:T(8,128)S(1)} %get-tuple-element.63.own), custom_call_target="tpu_custom_call" | custom-call | flops 1 | bytes 1 | tf_op jit(solution)/shard_map/fold/pallas_call | solution.py:288
  37.1 4.2 %collective-permute-start.7 = (s16[432,256]{1,0:T(8,128)(2,1)}, s16[432,256]{1,0:T(8,128)(2,1)S(1)}, u32[]{:S(2)}, u32[]{:S(2)}) collective-permute-start(s16[432,256]{1,0:T(8,128)(2,1)} %get-tuple-element.64), channel_id=1, source_target_pairs={{0,1},{1,0},{2,3},{3,2},{4,5},{5,4},{6,7},{7,6},{8,9},{9,8},{10,11... | collective-permute-start | bytes 663560 | tf_op jit(solution)/shard_map/ppermute | solution.py:548
  41.3 0.0 collective-permute-done.3.b
  41.3 3.3 %all-to-all-done.queries = bf16[32,16,128]{2,1,0:T(8,128)(2,1)} async-done(((bf16[32,16,128]{2,1,0:T(8,128)(2,1)}), bf16[32,16,128]{2,1,0:T(8,128)(2,1)}, u32[]{:S(2)}, u32[]{:S(2)}) %all-to-all-start) | async-done | bytes 131104 | tf_op jit(solution)/shard_map/all_to_all | solution.py:543
  44.6 0.0 collective-permute-done.2.a
  44.6 1.4 %fold.2 = (s16[400,256]{1,0:T(8,128)(2,1)S(1)}, f32[384,256]{1,0:T(8,128)S(1)}) custom-call(s16[400,512]{1,0:T(8,128)(2,1)} %collective-permute-done.2.a, s16[400,512]{1,0:T(8,128)(2,1)S(1)} %collective-permute-done.3.b, f32[384,512]{1,0:T(8,128)S(1)} %get-tuple-element.59.own), custom_call_target="tpu_custom_call" | custom-call | flops 1 | bytes 1 | tf_op jit(solution)/shard_map/fold/pallas_call | solution.py:288
  46.0 4.3 %collective-permute-start.4 = (s16[400,256]{1,0:T(8,128)(2,1)S(1)}, s16[400,256]{1,0:T(8,128)(2,1)S(1)}, u32[]{:S(2)}, u32[]{:S(2)}) collective-permute-start(s16[400,256]{1,0:T(8,128)(2,1)S(1)} %get-tuple-element.60), channel_id=1, source_target_pairs={{0,1},{1,0},{2,3},{3,2},{4,5},{5,4},{6,7},{7,6},{8,9},{9,8},{10,11... | collective-permute-start | bytes 614408 | tf_op jit(solution)/shard_map/ppermute | solution.py:546
  50.3 0.0 copy-done.3
  50.3 10.9 %collective-permute-done.4.refs_0_ = s16[400,256]{1,0:T(8,128)(2,1)S(1)} collective-permute-done((s16[400,256]{1,0:T(8,128)(2,1)S(1)}, s16[400,256]{1,0:T(8,128)(2,1)S(1)}, u32[]{:S(2)}, u32[]{:S(2)}) %collective-permute-start.4) | collective-permute-done | bytes 204832 | tf_op jit(solution)/shard_map/ppermute | solution.py:546
  61.1 0.0 collective-permute-done.7.refs_1_.came
  61.1 3.6 %prefix.1 = (bf16[768,256]{1,0:T(8,128)(2,1)}, s16[32,24,128]{2,1,0:T(8,128)(2,1)}) custom-call(bf16[32,16,128]{2,1,0:T(8,128)(2,1)} %all-to-all-done.queries, f32[1,256]{1,0:T(1,128)S(1)} %bitcast.4, f32[56,256]{1,0:T(8,128)} %constant.5.clone.turns, s16[400,256]{1,0:T(8,128)(2,1)S(1)} %collective-permute-done.4.refs_0_, ...), custom_call_target="tpu_custom_call" | custom-call | flops 200000000 | bytes 10000000 | tf_op jit(solution)/shard_map/prefix/pallas_call | solution.py:451
  64.7 8.0 %all-to-all-start.1 = ((s16[32,24,128]{2,1,0:T(8,128)(2,1)}), s16[32,24,128]{2,1,0:T(8,128)(2,1)S(1)}, u32[]{:S(2)}, u32[]{:S(2)}) async-start(s16[32,24,128]{2,1,0:T(8,128)(2,1)} %get-tuple-element.72), calls=%async_computation.1 | async-start | bytes 393216 | tf_op jit(solution)/shard_map/all_to_all | solution.py:557
  72.7 2.8 %suffix.1 = (bf16[32,256]{1,0:T(8,128)(2,1)}, f32[256,128]{1,0:T(8,128)S(1)}, f32[256,128]{1,0:T(8,128)S(1)}) custom-call(s32[32]{0:T(128)S(1)} %copy-done.2, f32[256,128]{1,0:T(8,128)S(1)} %get-tuple-element.68.turned, bf16[32,128,256]{2,1,0:T(8,128)(2,1)} %cache.1, s16[432,256]{1,0:T(8,128)(2,1)S(1)} %collective-permute-done.7.refs_1_.came, ...), custom_call_target="tpu_custom_call" | custom-call | flops 10000000 | bytes 10000000 | tf_op jit(solution)/shard_map/suffix/pallas_call | solution.py:396
  75.4 6.9 %all-to-all-done.1.back = s16[32,24,128]{2,1,0:T(8,128)(2,1)S(1)} async-done(((s16[32,24,128]{2,1,0:T(8,128)(2,1)}), s16[32,24,128]{2,1,0:T(8,128)(2,1)S(1)}, u32[]{:S(2)}, u32[]{:S(2)}) %all-to-all-start.1) | async-done | bytes 196640 | tf_op jit(solution)/shard_map/all_to_all | solution.py:557
  82.3 1.9 %merge.1 = bf16[32,1024]{1,0:T(8,128)(2,1)} custom-call(s32[32]{0:T(128)S(1)} %get-tuple-element.71.place, s16[32,24,128]{2,1,0:T(8,128)(2,1)S(1)} %all-to-all-done.1.back, f32[256,128]{1,0:T(8,128)S(1)} %get-tuple-element.73.out, f32[256,128]{1,0:T(8,128)S(1)} %get-tuple-element.74.stats), custom_call_target="tpu_custom_call" | custom-call | flops 1000000 | bytes 1000000 | tf_op jit(solution)/shard_map/merge/pallas_call | solution.py:500
  (1 shorter events, 0.0 us)
Async XLA Ops:
  5.7 14.9 %collective-permute-start.1 = (s16[432,512]{1,0:T(8,128)(2,1)S(1)}, s16[432,512]{1,0:T(8,128)(2,1)S(1)}, u32[]{:S(2)}, u32[]{:S(2)}) collective-permute-start(s16[432,512]{1,0:T(8,128)(2,1)S(1)} %get-tuple-element.48), channel_id=1, source_target_pairs={{0,6},{1,7},{2,0},{3,1},{4,2},{5,3},{6,4},{7,5},{8,14},{9,15},{10,... | collective-permute-start | bytes 1327112 | tf_op jit(solution)/shard_map/ppermute | solution.py:523
  9.4 11.2 %collective-permute-start = (s16[400,512]{1,0:T(8,128)(2,1)S(1)}, s16[400,512]{1,0:T(8,128)(2,1)S(1)}, u32[]{:S(2)}, u32[]{:S(2)}) collective-permute-start(s16[400,512]{1,0:T(8,128)(2,1)S(1)} %get-tuple-element.39), channel_id=1, source_target_pairs={{0,2},{1,3},{2,4},{3,5},{4,6},{5,7},{6,0},{7,1},{8,10},{9,11},{10,... | collective-permute-start | bytes 1228808 | tf_op jit(solution)/shard_map/ppermute | solution.py:523
  9.4 7.3 %copy-start = (f32[128,256]{1,0:T(8,128)S(1)}, f32[128,256]{1,0:T(8,128)}, u32[]{:S(2)}) copy-start(f32[128,256]{1,0:T(8,128)} %constant.4.clone.table) | copy-start | bytes 393220
  9.4 7.3 %copy-start.1 = (bf16[32,1024]{1,0:T(8,128)(2,1)S(1)}, bf16[32,1024]{1,0:T(8,128)(2,1)}, u32[]{:S(2)}) copy-start(bf16[32,1024]{1,0:T(8,128)(2,1)} %queries) | copy-start | bytes 196612
  9.4 7.3 %copy-start.2 = (s32[32]{0:T(128)S(1)}, s32[32]{0:T(128)}, u32[]{:S(2)}) copy-start(s32[32]{0:T(128)} %lengths.3) | copy-start | bytes 388
  16.5 19.4 %collective-permute-start.6 = (s16[432,512]{1,0:T(8,128)(2,1)}, s16[432,512]{1,0:T(8,128)(2,1)S(1)}, u32[]{:S(2)}, u32[]{:S(2)}) collective-permute-start(s16[432,512]{1,0:T(8,128)(2,1)} %get-tuple-element.62), channel_id=1, source_target_pairs={{0,2},{1,3},{2,4},{3,5},{4,6},{5,7},{6,0},{7,1},{8,10},{9,11},{10,... | collective-permute-start | bytes 1327112 | tf_op jit(solution)/shard_map/ppermute | solution.py:523
  22.2 28.1 %copy-start.3 = (bf16[256]{0:T(256)(128)(2,1)S(1)}, bf16[256]{0:T(256)(128)(2,1)}, u32[]{:S(2)}) copy-start(bf16[256]{0:T(256)(128)(2,1)} %param.18) | copy-start | bytes 1540
  22.2 13.8 %collective-permute-start.5 = (s16[432,512]{1,0:T(8,128)(2,1)}, s16[432,512]{1,0:T(8,128)(2,1)S(1)}, u32[]{:S(2)}, u32[]{:S(2)}) collective-permute-start(s16[432,512]{1,0:T(8,128)(2,1)} %get-tuple-element.61), channel_id=1, source_target_pairs={{0,6},{1,7},{2,0},{3,1},{4,2},{5,3},{6,4},{7,5},{8,14},{9,15},{10,... | collective-permute-start | bytes 1327112 | tf_op jit(solution)/shard_map/ppermute | solution.py:523
  23.2 18.1 %collective-permute-start.3 = (s16[400,512]{1,0:T(8,128)(2,1)}, s16[400,512]{1,0:T(8,128)(2,1)S(1)}, u32[]{:S(2)}, u32[]{:S(2)}) collective-permute-start(s16[400,512]{1,0:T(8,128)(2,1)} %get-tuple-element.54), channel_id=1, source_target_pairs={{0,6},{1,7},{2,0},{3,1},{4,2},{5,3},{6,4},{7,5},{8,14},{9,15},{10,... | collective-permute-start | bytes 1228808 | tf_op jit(solution)/shard_map/ppermute | solution.py:523
  24.5 20.1 %collective-permute-start.2 = (s16[400,512]{1,0:T(8,128)(2,1)}, s16[400,512]{1,0:T(8,128)(2,1)}, u32[]{:S(2)}, u32[]{:S(2)}) collective-permute-start(s16[400,512]{1,0:T(8,128)(2,1)} %get-tuple-element.53), channel_id=1, source_target_pairs={{0,2},{1,3},{2,4},{3,5},{4,6},{5,7},{6,0},{7,1},{8,10},{9,11},{10,... | collective-permute-start | bytes 1228808 | tf_op jit(solution)/shard_map/ppermute | solution.py:523
  24.7 19.9 %all-to-all-start = ((bf16[32,16,128]{2,1,0:T(8,128)(2,1)}), bf16[32,16,128]{2,1,0:T(8,128)(2,1)}, u32[]{:S(2)}, u32[]{:S(2)}) async-start(bf16[32,16,128]{2,1,0:T(8,128)(2,1)} %get-tuple-element.55), calls=%async_computation | async-start | bytes 262144 | tf_op jit(solution)/shard_map/all_to_all | solution.py:543
  37.1 24.0 %collective-permute-start.7 = (s16[432,256]{1,0:T(8,128)(2,1)}, s16[432,256]{1,0:T(8,128)(2,1)S(1)}, u32[]{:S(2)}, u32[]{:S(2)}) collective-permute-start(s16[432,256]{1,0:T(8,128)(2,1)} %get-tuple-element.64), channel_id=1, source_target_pairs={{0,1},{1,0},{2,3},{3,2},{4,5},{5,4},{6,7},{7,6},{8,9},{9,8},{10,11... | collective-permute-start | bytes 663560 | tf_op jit(solution)/shard_map/ppermute | solution.py:548
  46.0 15.2 %collective-permute-start.4 = (s16[400,256]{1,0:T(8,128)(2,1)S(1)}, s16[400,256]{1,0:T(8,128)(2,1)S(1)}, u32[]{:S(2)}, u32[]{:S(2)}) collective-permute-start(s16[400,256]{1,0:T(8,128)(2,1)S(1)} %get-tuple-element.60), channel_id=1, source_target_pairs={{0,1},{1,0},{2,3},{3,2},{4,5},{5,4},{6,7},{7,6},{8,9},{9,8},{10,11... | collective-permute-start | bytes 614408 | tf_op jit(solution)/shard_map/ppermute | solution.py:546
  64.7 17.6 %all-to-all-start.1 = ((s16[32,24,128]{2,1,0:T(8,128)(2,1)}), s16[32,24,128]{2,1,0:T(8,128)(2,1)S(1)}, u32[]{:S(2)}, u32[]{:S(2)}) async-start(s16[32,24,128]{2,1,0:T(8,128)(2,1)} %get-tuple-element.72), calls=%async_computation.1 | async-start | bytes 393216 | tf_op jit(solution)/shard_map/all_to_all | solution.py:557

commit v5 on v4

--- a/solution.py
+++ b/solution.py
@@ -10,7 +10,7 @@
 RANK = 32
 ROPE_BASE = 1000000.0
 NEG = -1e30
-PARTS = ((0, 384), (384, 384))
+PARTS = ((0, 416), (416, 352))
 LIMIT = 16 * 2**20
 FAR_LIMIT = 16 * 2**20
 NEAR_LIMIT = 20 * 2**20
@@ -190,10 +190,10 @@
         added = nn(xl[...], spread_up(u.at[k], slice(None), up.shape[0]))
         ref, coded = places(outs, 1, off)
         to = tile if coded else ref
-        to[...] = nn(hx[first1:, :], wx[k])
-        to[rows1:, :] = to[rows1:, :] + (added[:news] + added[news:])
+        to[: rows1 + news, :] = nn(hx[first1:, :], wx[k])
+        to[rows1 : rows1 + news, :] = to[rows1 : rows1 + news, :] + (added[:news] + added[news:])
         if coded:
-            encode(tile[...], ref, peaks)
+            encode(tile[: rows1 + news, :], ref, peaks)
 
 
 def project_far(*args):
@@ -238,7 +238,7 @@
             pltpu.VMEM((length + news, depth + 8 * RANK), BF16),
             pltpu.VMEM((n, depth + 8 * RANK, 4 * HW), BF16),
             pltpu.VMEM((n, up.shape[0], 2 * HW), BF16),
-            pltpu.VMEM((rows[1], 4 * HW), F32),
+            pltpu.VMEM((max(rows), 4 * HW), F32),
             pltpu.VMEM((SROWS, 4 * HW), F32),
             *own,
             pltpu.SemaphoreType.DMA((5 + 4 * n,)),
@@ -265,6 +265,7 @@
     return pl.pallas_call(
         relay_body,
         out_shape=[jax.ShapeDtypeStruct(came.shape, jnp.int16) for came in (came0, came1)],
+        input_output_aliases={0: 0, 2: 1},
         scratch_shapes=[pltpu.VMEM((SROWS, cols), F32), pltpu.VMEM((rows, cols), F32)],
         compiler_params=pltpu.CompilerParams(vmem_limit_bytes=LIMIT),
         cost_estimate=pl.CostEstimate(flops=1, bytes_accessed=1, transcendentals=0),
@@ -425,7 +426,7 @@
             kv[span, :HW] = turn(total[:, :HW], cosine, sine).astype(BF16)
             kv[span, HW:] = total[:, HW:].astype(BF16)
     prompts, per, _ = queries.shape
-    step = 8
+    step = 16
     for s in range(0, prompts, step):
         q = queries[s : s + step].reshape(step * per, HW)
         scores = nt(q, kv[:, :HW]) * (HW ** -0.5)
@@ -541,7 +542,6 @@
     joined0, direct0 = y_step(joined0, 1), y_step(direct0, -1)
     joined1, direct1 = y_step(joined1, -1), y_step(direct1, 1)
     here = lax.all_to_all(to_prompts, "rep", 0, 0, tiled=True)
-    joined0, direct0, here = lax.optimization_barrier((joined0, direct0, here))
     code0, keep0 = fold(joined0, direct0, own0)
     came0 = lax.ppermute(code0, "tp", along_z)
     code1, keep1 = fold(joined1, direct1, own1)

time: 84.5 us -> 83.5 us (0.988)
  starting transfers between devices: 34 us -> 41.6 us
  waiting for transfers between devices: 22.8 us -> 15.3 us
  Pallas kernels: 26.7 us -> 25.5 us
    ppermute x1, waiting for transfers between devices: 10.9 us -> 0.01 us  [on_device(): came0 = lax.ppermute(code0, 'tp', along_z)]
    ppermute x1, waiting for transfers between devices: 0.01 us -> 7.7 us  [on_device(): came1 = lax.ppermute(code1, 'tp', along_z)]
    all_to_all x1, waiting for transfers between devices: 3.27 us -> 0.01 us  [on_device(): here = lax.all_to_all(to_prompts, 'rep', 0, 0, tiled=True)]
    all_to_all x1, starting transfers between devices: 7.97 us -> 10.9 us  [on_device(): back = lax.all_to_all(part, 'rep', 0, 0, tiled=True)]
    ppermute x1, starting transfers between devices: 4.21 us -> 7.02 us  [on_device(): came1 = lax.ppermute(code1, 'tp', along_z)]
    ppermute x6, starting transfers between devices: 6.22 us -> 8.03 us  [on_device(): y_step = lambda value, d: lax.ppermute(value, 'tp', along_y(d))]
    ppermute x6, waiting for transfers between devices: 1.8 us -> 0.7 us  [on_device(): y_step = lambda value, d: lax.ppermute(value, 'tp', along_y(d))]
  transfers between devices with their start and end apart: 10 -> 10, of which waited for: 4 -> 3; matrix products, arithmetic and copies ran while one was open for 0% -> 0% of each run, Pallas kernels for 19% -> 18%
where the time goes in v5:
time: 83.5 us; the launch traced here: 83.2 us
  starting transfers between devices  41.6 us (50%)
  Pallas kernels  25.5 us (31%)
  waiting for transfers between devices  15.3 us (18%)
    pallas_call x2, Pallas kernels, project(): pl.pallas_call(lambda *refs: project_body(offs, places, bool(known), *ref...  12.3 us
    all_to_all x1, starting transfers between devices, on_device(): here = lax.all_to_all(to_prompts, 'rep', 0, 0, tiled=True)  11.4 us
    all_to_all x1, starting transfers between devices, on_device(): back = lax.all_to_all(part, 'rep', 0, 0, tiled=True)  10.9 us
    ppermute x6, starting transfers between devices, on_device(): y_step = lambda value, d: lax.ppermute(value, 'tp', along_y(d))  8.03 us
    ppermute x1, waiting for transfers between devices, on_device(): came1 = lax.ppermute(code1, 'tp', along_z)  7.7 us
    ppermute x1, starting transfers between devices, on_device(): came1 = lax.ppermute(code1, 'tp', along_z)  7.02 us
    all_to_all x1, waiting for transfers between devices, on_device(): back = lax.all_to_all(part, 'rep', 0, 0, tiled=True)  6.88 us
    ppermute x1, starting transfers between devices, on_device(): came0 = lax.ppermute(code0, 'tp', along_z)  4.22 us
  transfers between devices with their start and end apart: 10, of which 3 were waited for; matrix products, arithmetic and copies ran while one was open for 0% of the time, Pallas kernels for 18%

profile of v5, /device:TPU:1, one launch (start us, length us, event | category | flops | bytes accessed | tf_op | source)
XLA Modules:
  0.0 83.2 jit_solution(13867091280507472838)
XLA Ops:
  0.6 5.1 %project1.1 = (s16[432,512]{1,0:T(8,128)(2,1)S(1)}, s16[400,512]{1,0:T(8,128)(2,1)S(1)}, bf16[800,256]{1,0:T(8,128)(2,1)S(1)}, bf16[64,512]{1,0:T(8,128)(2,1)S(1)}) custom-call(s32[32]{0:T(128)} %refs_0_.3, s32[32]{0:T(128)} %bitcast.8, bf16[768,1024]{1,0:T(8,128)(2,1)} %bitcast.6, bf16[1024,2048]{1,0:T(8,128)(2,1)} %refs_3_.3, bf16[1024,512]{1,0:T(8,128)(2,1)} %refs_4_.3, ...), custom_call_target="tpu_custom_call" | custom-call | flops 805306368 | bytes 6000000 | tf_op jit(solution)/shard_map/project1/pallas_call | solution.py:232
  5.8 2.2 %collective-permute-start = (s16[432,512]{1,0:T(8,128)(2,1)S(1)}, s16[432,512]{1,0:T(8,128)(2,1)S(1)}, u32[]{:S(2)}, u32[]{:S(2)}) collective-permute-start(s16[432,512]{1,0:T(8,128)(2,1)S(1)} %get-tuple-element.36), channel_id=1, source_target_pairs={{0,2},{1,3},{2,4},{3,5},{4,6},{5,7},{6,0},{7,1},{8,10},{9,11},{10,... | collective-permute-start | bytes 1327112 | tf_op jit(solution)/shard_map/ppermute | solution.py:524
  8.0 1.5 %collective-permute-start.1 = (s16[400,512]{1,0:T(8,128)(2,1)S(1)}, s16[400,512]{1,0:T(8,128)(2,1)S(1)}, u32[]{:S(2)}, u32[]{:S(2)}) collective-permute-start(s16[400,512]{1,0:T(8,128)(2,1)S(1)} %get-tuple-element.45), channel_id=1, source_target_pairs={{0,6},{1,7},{2,0},{3,1},{4,2},{5,3},{6,4},{7,5},{8,14},{9,15},{10,... | collective-permute-start | bytes 1228808 | tf_op jit(solution)/shard_map/ppermute | solution.py:524
  9.5 0.0 copy-start
  9.5 0.0 copy-start.2
  9.5 0.0 copy-start.3
  9.5 7.1 %project3.1 = (s16[432,512]{1,0:T(8,128)(2,1)}, s16[400,512]{1,0:T(8,128)(2,1)}, f32[416,512]{1,0:T(8,128)S(1)}, f32[384,512]{1,0:T(8,128)S(1)}, f32[416,512]{1,0:T(8,128)S(1)}, /*index=5*/f32[384,512]{1,0:T(8,128)S(1)}) custom-call(s32[32]{0:T(128)} %refs_0_.3, s32[32]{0:T(128)} %bitcast.9, bf16[768,1024]{1,0:T(8,128)(2,1)} %bitcast.7, ...), custom_call_target="tpu_custom_call" | custom-call | flops 2415919104 | bytes 10000000 | tf_op jit(solution)/shard_map/project3/pallas_call | solution.py:232
  16.7 1.4 %collective-permute-start.3 = (s16[432,512]{1,0:T(8,128)(2,1)}, s16[432,512]{1,0:T(8,128)(2,1)S(1)}, u32[]{:S(2)}, u32[]{:S(2)}) collective-permute-start(s16[432,512]{1,0:T(8,128)(2,1)} %get-tuple-element.52), channel_id=1, source_target_pairs={{0,6},{1,7},{2,0},{3,1},{4,2},{5,3},{6,4},{7,5},{8,14},{9,15},{10,... | collective-permute-start | bytes 1327112 | tf_op jit(solution)/shard_map/ppermute | solution.py:524
  18.1 0.0 copy-done
  18.1 0.0 copy-done.2
  18.1 0.0 copy-done.3
  18.1 2.0 %dispatch.1 = (bf16[32,16,128]{2,1,0:T(8,128)(2,1)S(1)}, f32[256,128]{1,0:T(8,128)S(1)}, f32[32,256]{1,0:T(8,128)S(1)}, s32[32]{0:T(128)S(1)}) custom-call(s32[32]{0:T(128)} %bitcast.10, s32[32]{0:T(128)S(1)} %copy-done.3, bf16[32,1024]{1,0:T(8,128)(2,1)S(1)} %copy-done.2, f32[128,256]{1,0:T(8,128)S(1)} %copy-done), custom_call_target="tpu_custom_call" | custom-call | flops 1 | bytes 1 | tf_op jit(solution)/shard_map/dispatch/pallas_call | solution.py:342
  20.1 0.0 copy-start.1
  20.1 0.0 collective-permute-done.1.came1
  20.1 0.0 collective-permute-done.came0
  20.2 0.8 relay.1
  20.9 0.0 copy-start.4
  21.0 0.2 collective-permute-start.2
  21.2 0.1 collective-permute-start.6
  21.3 0.0 copy-done.1
  21.3 2.6 %collective-permute-start.5 = (s16[400,512]{1,0:T(8,128)(2,1)S(1)}, s16[400,512]{1,0:T(8,128)(2,1)}, u32[]{:S(2)}, u32[]{:S(2)}) collective-permute-start(s16[400,512]{1,0:T(8,128)(2,1)S(1)} %get-tuple-element.55), channel_id=1, source_target_pairs={{0,6},{1,7},{2,0},{3,1},{4,2},{5,3},{6,4},{7,5},{8,14},{9,15},{10,... | collective-permute-start | bytes 1228808 | tf_op jit(solution)/shard_map/ppermute | solution.py:524
  23.9 11.4 %all-to-all-start = ((bf16[32,16,128]{2,1,0:T(8,128)(2,1)}), bf16[32,16,128]{2,1,0:T(8,128)(2,1)}, u32[]{:S(2)}, u32[]{:S(2)}) async-start(bf16[32,16,128]{2,1,0:T(8,128)(2,1)} %copy-done.1), calls=%async_computation | async-start | bytes 262144 | tf_op jit(solution)/shard_map/all_to_all | solution.py:544
  35.2 0.0 collective-permute-done.3.b
  35.2 0.0 collective-permute-done.2.a
  35.2 1.1 %fold.2 = (s16[432,256]{1,0:T(8,128)(2,1)}, f32[416,256]{1,0:T(8,128)S(1)}) custom-call(s16[432,512]{1,0:T(8,128)(2,1)S(1)} %collective-permute-done.2.a, s16[432,512]{1,0:T(8,128)(2,1)S(1)} %collective-permute-done.3.b, f32[416,512]{1,0:T(8,128)S(1)} %get-tuple-element.53.own), custom_call_target="tpu_custom_call" | custom-call | flops 1 | bytes 1 | tf_op jit(solution)/shard_map/fold/pallas_call | solution.py:289
  36.3 4.2 %collective-permute-start.4 = (s16[432,256]{1,0:T(8,128)(2,1)}, s16[432,256]{1,0:T(8,128)(2,1)S(1)}, u32[]{:S(2)}, u32[]{:S(2)}) collective-permute-start(s16[432,256]{1,0:T(8,128)(2,1)} %get-tuple-element.54), channel_id=1, source_target_pairs={{0,1},{1,0},{2,3},{3,2},{4,5},{5,4},{6,7},{7,6},{8,9},{9,8},{10,11... | collective-permute-start | bytes 663560 | tf_op jit(solution)/shard_map/ppermute | solution.py:546
  40.6 0.7 collective-permute-done.6.b
  41.2 0.0 collective-permute-done.5.a
  41.3 1.5 %fold.3 = (s16[400,256]{1,0:T(8,128)(2,1)S(1)}, f32[384,256]{1,0:T(8,128)S(1)}) custom-call(s16[400,512]{1,0:T(8,128)(2,1)} %collective-permute-done.5.a, s16[400,512]{1,0:T(8,128)(2,1)} %collective-permute-done.6.b, f32[384,512]{1,0:T(8,128)S(1)} %get-tuple-element.57.own), custom_call_target="tpu_custom_call" | custom-call | flops 1 | bytes 1 | tf_op jit(solution)/shard_map/fold/pallas_call | solution.py:289
  42.8 7.0 %collective-permute-start.7 = (s16[400,256]{1,0:T(8,128)(2,1)S(1)}, s16[400,256]{1,0:T(8,128)(2,1)S(1)}, u32[]{:S(2)}, u32[]{:S(2)}) collective-permute-start(s16[400,256]{1,0:T(8,128)(2,1)S(1)} %get-tuple-element.58), channel_id=1, source_target_pairs={{0,1},{1,0},{2,3},{3,2},{4,5},{5,4},{6,7},{7,6},{8,9},{9,8},{10,11... | collective-permute-start | bytes 614408 | tf_op jit(solution)/shard_map/ppermute | solution.py:548
  49.8 0.0 copy-done.4
  49.8 0.0 all-to-all-done.queries
  49.8 7.7 %collective-permute-done.7.refs_1_.came = s16[400,256]{1,0:T(8,128)(2,1)S(1)} collective-permute-done((s16[400,256]{1,0:T(8,128)(2,1)S(1)}, s16[400,256]{1,0:T(8,128)(2,1)S(1)}, u32[]{:S(2)}, u32[]{:S(2)}) %collective-permute-start.7) | collective-permute-done | bytes 204832 | tf_op jit(solution)/shard_map/ppermute | solution.py:548
  57.5 0.0 collective-permute-done.4.refs_0_
  57.5 3.2 %prefix.1 = (bf16[768,256]{1,0:T(8,128)(2,1)}, s16[32,24,128]{2,1,0:T(8,128)(2,1)}) custom-call(bf16[32,16,128]{2,1,0:T(8,128)(2,1)} %all-to-all-done.queries, f32[1,256]{1,0:T(1,128)S(1)} %bitcast.4, f32[56,256]{1,0:T(8,128)} %constant.5.clone.turns, s16[432,256]{1,0:T(8,128)(2,1)S(1)} %collective-permute-done.4.refs_0_, ...), custom_call_target="tpu_custom_call" | custom-call | flops 200000000 | bytes 10000000 | tf_op jit(solution)/shard_map/prefix/pallas_call | solution.py:452
  60.7 10.9 %all-to-all-start.1 = ((s16[32,24,128]{2,1,0:T(8,128)(2,1)}), s16[32,24,128]{2,1,0:T(8,128)(2,1)S(1)}, u32[]{:S(2)}, u32[]{:S(2)}) async-start(s16[32,24,128]{2,1,0:T(8,128)(2,1)} %get-tuple-element.66), calls=%async_computation.1 | async-start | bytes 393216 | tf_op jit(solution)/shard_map/all_to_all | solution.py:557
  71.7 2.8 %suffix.1 = (bf16[32,256]{1,0:T(8,128)(2,1)}, f32[256,128]{1,0:T(8,128)S(1)}, f32[256,128]{1,0:T(8,128)S(1)}) custom-call(s32[32]{0:T(128)S(1)} %copy-done.3, f32[256,128]{1,0:T(8,128)S(1)} %get-tuple-element.62.turned, bf16[32,128,256]{2,1,0:T(8,128)(2,1)} %cache.1, s16[400,256]{1,0:T(8,128)(2,1)S(1)} %collective-permute-done.7.refs_1_.came, ...), custom_call_target="tpu_custom_call" | custom-call | flops 10000000 | bytes 10000000 | tf_op jit(solution)/shard_map/suffix/pallas_call | solution.py:397
  74.4 6.9 %all-to-all-done.1.back = s16[32,24,128]{2,1,0:T(8,128)(2,1)S(1)} async-done(((s16[32,24,128]{2,1,0:T(8,128)(2,1)}), s16[32,24,128]{2,1,0:T(8,128)(2,1)S(1)}, u32[]{:S(2)}, u32[]{:S(2)}) %all-to-all-start.1) | async-done | bytes 196640 | tf_op jit(solution)/shard_map/all_to_all | solution.py:557
  81.3 1.9 %merge.1 = bf16[32,1024]{1,0:T(8,128)(2,1)} custom-call(s32[32]{0:T(128)S(1)} %get-tuple-element.65.place, s16[32,24,128]{2,1,0:T(8,128)(2,1)S(1)} %all-to-all-done.1.back, f32[256,128]{1,0:T(8,128)S(1)} %get-tuple-element.67.out, f32[256,128]{1,0:T(8,128)S(1)} %get-tuple-element.68.stats), custom_call_target="tpu_custom_call" | custom-call | flops 1000000 | bytes 1000000 | tf_op jit(solution)/shard_map/merge/pallas_call | solution.py:501
  (1 shorter events, 0.0 us)
Async XLA Ops:
  5.8 14.4 %collective-permute-start = (s16[432,512]{1,0:T(8,128)(2,1)S(1)}, s16[432,512]{1,0:T(8,128)(2,1)S(1)}, u32[]{:S(2)}, u32[]{:S(2)}) collective-permute-start(s16[432,512]{1,0:T(8,128)(2,1)S(1)} %get-tuple-element.36), channel_id=1, source_target_pairs={{0,2},{1,3},{2,4},{3,5},{4,6},{5,7},{6,0},{7,1},{8,10},{9,11},{10,... | collective-permute-start | bytes 1327112 | tf_op jit(solution)/shard_map/ppermute | solution.py:524
  8.0 12.2 %collective-permute-start.1 = (s16[400,512]{1,0:T(8,128)(2,1)S(1)}, s16[400,512]{1,0:T(8,128)(2,1)S(1)}, u32[]{:S(2)}, u32[]{:S(2)}) collective-permute-start(s16[400,512]{1,0:T(8,128)(2,1)S(1)} %get-tuple-element.45), channel_id=1, source_target_pairs={{0,6},{1,7},{2,0},{3,1},{4,2},{5,3},{6,4},{7,5},{8,14},{9,15},{10,... | collective-permute-start | bytes 1228808 | tf_op jit(solution)/shard_map/ppermute | solution.py:524
  9.5 8.6 %copy-start = (f32[128,256]{1,0:T(8,128)S(1)}, f32[128,256]{1,0:T(8,128)}, u32[]{:S(2)}) copy-start(f32[128,256]{1,0:T(8,128)} %constant.4.clone.table) | copy-start | bytes 393220
  9.5 8.6 %copy-start.2 = (bf16[32,1024]{1,0:T(8,128)(2,1)S(1)}, bf16[32,1024]{1,0:T(8,128)(2,1)}, u32[]{:S(2)}) copy-start(bf16[32,1024]{1,0:T(8,128)(2,1)} %queries) | copy-start | bytes 196612
  9.5 8.6 %copy-start.3 = (s32[32]{0:T(128)S(1)}, s32[32]{0:T(128)}, u32[]{:S(2)}) copy-start(s32[32]{0:T(128)} %lengths.3) | copy-start | bytes 388
  16.7 18.6 %collective-permute-start.3 = (s16[432,512]{1,0:T(8,128)(2,1)}, s16[432,512]{1,0:T(8,128)(2,1)S(1)}, u32[]{:S(2)}, u32[]{:S(2)}) collective-permute-start(s16[432,512]{1,0:T(8,128)(2,1)} %get-tuple-element.52), channel_id=1, source_target_pairs={{0,6},{1,7},{2,0},{3,1},{4,2},{5,3},{6,4},{7,5},{8,14},{9,15},{10,... | collective-permute-start | bytes 1327112 | tf_op jit(solution)/shard_map/ppermute | solution.py:524
  20.1 1.1 %copy-start.1 = (bf16[32,16,128]{2,1,0:T(8,128)(2,1)}, bf16[32,16,128]{2,1,0:T(8,128)(2,1)S(1)}, u32[]{:S(2)}) copy-start(bf16[32,16,128]{2,1,0:T(8,128)(2,1)S(1)} %get-tuple-element.50) | copy-start | bytes 393220
  20.9 28.8 %copy-start.4 = (bf16[256]{0:T(256)(128)(2,1)S(1)}, bf16[256]{0:T(256)(128)(2,1)}, u32[]{:S(2)}) copy-start(bf16[256]{0:T(256)(128)(2,1)} %param.18) | copy-start | bytes 1540
  21.0 14.3 %collective-permute-start.2 = (s16[432,512]{1,0:T(8,128)(2,1)S(1)}, s16[432,512]{1,0:T(8,128)(2,1)S(1)}, u32[]{:S(2)}, u32[]{:S(2)}) collective-permute-start(s16[432,512]{1,0:T(8,128)(2,1)S(1)} %get-tuple-element.51), channel_id=1, source_target_pairs={{0,2},{1,3},{2,4},{3,5},{4,6},{5,7},{6,0},{7,1},{8,10},{9,11},{10,... | collective-permute-start | bytes 1327112 | tf_op jit(solution)/shard_map/ppermute | solution.py:524
  21.2 20.1 %collective-permute-start.6 = (s16[400,512]{1,0:T(8,128)(2,1)}, s16[400,512]{1,0:T(8,128)(2,1)}, u32[]{:S(2)}, u32[]{:S(2)}) collective-permute-start(s16[400,512]{1,0:T(8,128)(2,1)} %get-tuple-element.56), channel_id=1, source_target_pairs={{0,2},{1,3},{2,4},{3,5},{4,6},{5,7},{6,0},{7,1},{8,10},{9,11},{10,... | collective-permute-start | bytes 1228808 | tf_op jit(solution)/shard_map/ppermute | solution.py:524
  21.3 20.0 %collective-permute-start.5 = (s16[400,512]{1,0:T(8,128)(2,1)S(1)}, s16[400,512]{1,0:T(8,128)(2,1)}, u32[]{:S(2)}, u32[]{:S(2)}) collective-permute-start(s16[400,512]{1,0:T(8,128)(2,1)S(1)} %get-tuple-element.55), channel_id=1, source_target_pairs={{0,6},{1,7},{2,0},{3,1},{4,2},{5,3},{6,4},{7,5},{8,14},{9,15},{10,... | collective-permute-start | bytes 1228808 | tf_op jit(solution)/shard_map/ppermute | solution.py:524
  23.9 25.9 %all-to-all-start = ((bf16[32,16,128]{2,1,0:T(8,128)(2,1)}), bf16[32,16,128]{2,1,0:T(8,128)(2,1)}, u32[]{:S(2)}, u32[]{:S(2)}) async-start(bf16[32,16,128]{2,1,0:T(8,128)(2,1)} %copy-done.1), calls=%async_computation | async-start | bytes 262144 | tf_op jit(solution)/shard_map/all_to_all | solution.py:544
  36.3 21.2 %collective-permute-start.4 = (s16[432,256]{1,0:T(8,128)(2,1)}, s16[432,256]{1,0:T(8,128)(2,1)S(1)}, u32[]{:S(2)}, u32[]{:S(2)}) collective-permute-start(s16[432,256]{1,0:T(8,128)(2,1)} %get-tuple-element.54), channel_id=1, source_target_pairs={{0,1},{1,0},{2,3},{3,2},{4,5},{5,4},{6,7},{7,6},{8,9},{9,8},{10,11... | collective-permute-start | bytes 663560 | tf_op jit(solution)/shard_map/ppermute | solution.py:546
  42.8 14.7 %collective-permute-start.7 = (s16[400,256]{1,0:T(8,128)(2,1)S(1)}, s16[400,256]{1,0:T(8,128)(2,1)S(1)}, u32[]{:S(2)}, u32[]{:S(2)}) collective-permute-start(s16[400,256]{1,0:T(8,128)(2,1)S(1)} %get-tuple-element.58), channel_id=1, source_target_pairs={{0,1},{1,0},{2,3},{3,2},{4,5},{5,4},{6,7},{7,6},{8,9},{9,8},{10,11... | collective-permute-start | bytes 614408 | tf_op jit(solution)/shard_map/ppermute | solution.py:548
  60.7 20.6 %all-to-all-start.1 = ((s16[32,24,128]{2,1,0:T(8,128)(2,1)}), s16[32,24,128]{2,1,0:T(8,128)(2,1)S(1)}, u32[]{:S(2)}, u32[]{:S(2)}) async-start(s16[32,24,128]{2,1,0:T(8,128)(2,1)} %get-tuple-element.66), calls=%async_computation.1 | async-start | bytes 393216 | tf_op jit(solution)/shard_map/all_to_all | solution.py:557

commit v6 on v5

--- a/solution.py
+++ b/solution.py
@@ -250,27 +250,26 @@
     )(adapter_index, parents, hidden, weight, down, up, latest, *known)
 
 
-def relay_body(came0, near0, came1, near1, out0, out1, peaks, whole):
-    for came, near, out in ((came0, near0, out0), (came1, near1, out1)):
-        rows = near.shape[0]
-        scale = scales(came, rows)
-        for k in range(rows // BLK):
-            span = slice(k * BLK, (k + 1) * BLK)
-            whole[span, :] = near[span, :] + decode(came, scale, k)
-        encode(whole[:rows, :], out, peaks)
-
-
-def relay(came0, near0, came1, near1):
-    rows, cols = max(near0.shape[0], near1.shape[0]), near0.shape[1]
+def relay_body(came, near, out, peaks, whole):
+    rows = near.shape[0]
+    scale = scales(came, rows)
+    for k in range(rows // BLK):
+        span = slice(k * BLK, (k + 1) * BLK)
+        whole[span, :] = near[span, :] + decode(came, scale, k)
+    encode(whole[...], out, peaks)
+
+
+def relay(came, near):
+    rows, cols = near.shape
     return pl.pallas_call(
         relay_body,
-        out_shape=[jax.ShapeDtypeStruct(came.shape, jnp.int16) for came in (came0, came1)],
-        input_output_aliases={0: 0, 2: 1},
+        out_shape=jax.ShapeDtypeStruct(came.shape, jnp.int16),
+        input_output_aliases={0: 0},
         scratch_shapes=[pltpu.VMEM((SROWS, cols), F32), pltpu.VMEM((rows, cols), F32)],
         compiler_params=pltpu.CompilerParams(vmem_limit_bytes=LIMIT),
         cost_estimate=pl.CostEstimate(flops=1, bytes_accessed=1, transcendentals=0),
         name="relay",
-    )(came0, near0, came1, near1)
+    )(came, near)
 
 
 def fold_body(a, b, own, out, keep, peaks, other):
@@ -537,8 +536,8 @@
     table = jnp.asarray(np.concatenate([cos_t, sin_t], 1))
     to_prompts, turned, ropes, place = dispatch(parent, suffix_length_count, queries, table, prompts)
     near0, near1, to_prompts = lax.optimization_barrier((near0, near1, to_prompts))
-    joined0, joined1 = relay(far0, near0, far1, near1)
-    joined0, joined1, to_prompts = lax.optimization_barrier((joined0, joined1, to_prompts))
+    joined0, joined1 = relay(far0, near0), relay(far1, near1)
+    joined1, to_prompts = lax.optimization_barrier((joined1, to_prompts))
     joined0, direct0 = y_step(joined0, 1), y_step(direct0, -1)
     joined1, direct1 = y_step(joined1, -1), y_step(direct1, 1)
     here = lax.all_to_all(to_prompts, "rep", 0, 0, tiled=True)

time: 83.5 us -> 86.5 us (1.036)
  waiting for transfers between devices: 15.3 us -> 11.1 us
  starting transfers between devices: 41.6 us -> 45.2 us
  local copies, waits for them, and re-layouts: 0.02 us -> 1.78 us
  Pallas kernels: 25.5 us -> 27.2 us
    all_to_all x1, starting transfers between devices: 10.9 us -> 16.8 us  [on_device(): back = lax.all_to_all(part, 'rep', 0, 0, tiled=True)]
    ppermute x1, waiting for transfers between devices: 7.7 us -> 4.18 us  [on_device(): came1 = lax.ppermute(code1, 'tp', along_z)]
    pallas_call x1 -> x2, Pallas kernels: 0.78 us -> 2.59 us  [relay(): pl.pallas_call(relay_body, out_shape=jax.ShapeDtypeStruct(came.shape, jnp...]
    unnamed x10 -> x14, local copies, waits for them, and re-layouts: 0.02 us -> 1.78 us
    ppermute x1, starting transfers between devices: 7.02 us -> 5.37 us  [on_device(): came1 = lax.ppermute(code1, 'tp', along_z)]
  transfers between devices with their start and end apart: 10 -> 10, of which waited for: 3 -> 2; matrix products, arithmetic and copies ran while one was open for 0% -> 0% of each run, Pallas kernels for 18% -> 20%
where the time goes in v6:
time: 86.5 us; the launch traced here: 86 us
  starting transfers between devices  45.2 us (52%)
  Pallas kernels  27.2 us (31%)
  waiting for transfers between devices  11.1 us (13%)
  local copies, waits for them, and re-layouts  1.78 us (2%)
    all_to_all x1, starting transfers between devices, on_device(): back = lax.all_to_all(part, 'rep', 0, 0, tiled=True)  16.8 us
    pallas_call x2, Pallas kernels, project(): pl.pallas_call(lambda *refs: project_body(offs, places, bool(known), *ref...  12.3 us
    all_to_all x1, starting transfers between devices, on_device(): here = lax.all_to_all(to_prompts, 'rep', 0, 0, tiled=True)  10.8 us
    ppermute x6, starting transfers between devices, on_device(): y_step = lambda value, d: lax.ppermute(value, 'tp', along_y(d))  8.03 us
    all_to_all x1, waiting for transfers between devices, on_device(): back = lax.all_to_all(part, 'rep', 0, 0, tiled=True)  6.88 us
    ppermute x1, starting transfers between devices, on_device(): came1 = lax.ppermute(code1, 'tp', along_z)  5.37 us
    ppermute x1, starting transfers between devices, on_device(): came0 = lax.ppermute(code0, 'tp', along_z)  4.21 us
    ppermute x1, waiting for transfers between devices, on_device(): came1 = lax.ppermute(code1, 'tp', along_z)  4.18 us
  transfers between devices with their start and end apart: 10, of which 2 were waited for; matrix products, arithmetic and copies ran while one was open for 0% of the time, Pallas kernels for 20%

profile of v6, /device:TPU:1, one launch (start us, length us, event | category | flops | bytes accessed | tf_op | source)
XLA Modules:
  0.0 86.0 jit_solution(1885984802649617225)
XLA Ops:
  0.6 5.1 %project1.1 = (s16[432,512]{1,0:T(8,128)(2,1)S(1)}, s16[400,512]{1,0:T(8,128)(2,1)S(1)}, bf16[800,256]{1,0:T(8,128)(2,1)S(1)}, bf16[64,512]{1,0:T(8,128)(2,1)S(1)}) custom-call(s32[32]{0:T(128)} %refs_0_.3, s32[32]{0:T(128)} %bitcast.8, bf16[768,1024]{1,0:T(8,128)(2,1)} %bitcast.6, bf16[1024,2048]{1,0:T(8,128)(2,1)} %refs_3_.3, bf16[1024,512]{1,0:T(8,128)(2,1)} %refs_4_.3, ...), custom_call_target="tpu_custom_call" | custom-call | flops 805306368 | bytes 6000000 | tf_op jit(solution)/shard_map/project1/pallas_call | solution.py:232
  5.8 2.2 %collective-permute-start.1 = (s16[432,512]{1,0:T(8,128)(2,1)S(1)}, s16[432,512]{1,0:T(8,128)(2,1)S(1)}, u32[]{:S(2)}, u32[]{:S(2)}) collective-permute-start(s16[432,512]{1,0:T(8,128)(2,1)S(1)} %get-tuple-element.44), channel_id=1, source_target_pairs={{0,2},{1,3},{2,4},{3,5},{4,6},{5,7},{6,0},{7,1},{8,10},{9,11},{10,... | collective-permute-start | bytes 1327112 | tf_op jit(solution)/shard_map/ppermute | solution.py:523
  8.0 1.5 %collective-permute-start = (s16[400,512]{1,0:T(8,128)(2,1)S(1)}, s16[400,512]{1,0:T(8,128)(2,1)}, u32[]{:S(2)}, u32[]{:S(2)}) collective-permute-start(s16[400,512]{1,0:T(8,128)(2,1)S(1)} %get-tuple-element.33), channel_id=1, source_target_pairs={{0,6},{1,7},{2,0},{3,1},{4,2},{5,3},{6,4},{7,5},{8,14},{9,15},{10,... | collective-permute-start | bytes 1228808 | tf_op jit(solution)/shard_map/ppermute | solution.py:523
  9.5 0.0 copy-start
  9.5 0.0 copy-start.2
  9.5 0.0 copy-start.3
  9.5 7.1 %project3.1 = (s16[432,512]{1,0:T(8,128)(2,1)}, s16[400,512]{1,0:T(8,128)(2,1)}, f32[416,512]{1,0:T(8,128)S(1)}, f32[384,512]{1,0:T(8,128)S(1)}, f32[416,512]{1,0:T(8,128)S(1)}, /*index=5*/f32[384,512]{1,0:T(8,128)S(1)}) custom-call(s32[32]{0:T(128)} %refs_0_.3, s32[32]{0:T(128)} %bitcast.9, bf16[768,1024]{1,0:T(8,128)(2,1)} %bitcast.7, ...), custom_call_target="tpu_custom_call" | custom-call | flops 2415919104 | bytes 10000000 | tf_op jit(solution)/shard_map/project3/pallas_call | solution.py:232
  16.7 1.4 %collective-permute-start.3 = (s16[432,512]{1,0:T(8,128)(2,1)}, s16[432,512]{1,0:T(8,128)(2,1)S(1)}, u32[]{:S(2)}, u32[]{:S(2)}) collective-permute-start(s16[432,512]{1,0:T(8,128)(2,1)} %get-tuple-element.46), channel_id=1, source_target_pairs={{0,6},{1,7},{2,0},{3,1},{4,2},{5,3},{6,4},{7,5},{8,14},{9,15},{10,... | collective-permute-start | bytes 1327112 | tf_op jit(solution)/shard_map/ppermute | solution.py:523
  18.1 0.0 copy-done
  18.1 0.0 copy-done.2
  18.1 0.0 copy-done.3
  18.1 2.0 %dispatch.1 = (bf16[32,16,128]{2,1,0:T(8,128)(2,1)S(1)}, f32[256,128]{1,0:T(8,128)S(1)}, f32[32,256]{1,0:T(8,128)S(1)}, s32[32]{0:T(128)S(1)}) custom-call(s32[32]{0:T(128)} %bitcast.10, s32[32]{0:T(128)S(1)} %copy-done.3, bf16[32,1024]{1,0:T(8,128)(2,1)S(1)} %copy-done.2, f32[128,256]{1,0:T(8,128)S(1)} %copy-done), custom_call_target="tpu_custom_call" | custom-call | flops 1 | bytes 1 | tf_op jit(solution)/shard_map/dispatch/pallas_call | solution.py:341
  20.1 0.0 copy-start.1
  20.1 0.0 collective-permute-done.1.came
  20.1 0.4 relay.3
  20.6 0.2 collective-permute-start.2
  20.8 0.0 copy-done.1
  20.8 0.1 collective-permute-start.6
  20.9 0.0 collective-permute-done.came
  20.9 2.2 %relay.2 = s16[400,512]{1,0:T(8,128)(2,1)} custom-call(s16[400,512]{1,0:T(8,128)(2,1)} %collective-permute-done.came, f32[384,512]{1,0:T(8,128)S(1)} %get-tuple-element.41.near), custom_call_target="tpu_custom_call", output_to_operand_aliasing={{}: (0, {})} | custom-call | flops 1 | bytes 1 | tf_op jit(solution)/shard_map/relay/pallas_call | solution.py:264
  23.1 0.0 copy-start.6
  23.1 2.5 %collective-permute-start.5 = (s16[400,512]{1,0:T(8,128)(2,1)}, s16[400,512]{1,0:T(8,128)(2,1)}, u32[]{:S(2)}, u32[]{:S(2)}) collective-permute-start(s16[400,512]{1,0:T(8,128)(2,1)} %relay.2), channel_id=1, source_target_pairs={{0,6},{1,7},{2,0},{3,1},{4,2},{5,3},{6,4},{7,5},{8,14},{9,15},{10,... | collective-permute-start | bytes 1228808 | tf_op jit(solution)/shard_map/ppermute | solution.py:523
  25.6 10.8 %all-to-all-start = ((bf16[32,16,128]{2,1,0:T(8,128)(2,1)}), bf16[32,16,128]{2,1,0:T(8,128)(2,1)}, u32[]{:S(2)}, u32[]{:S(2)}) async-start(bf16[32,16,128]{2,1,0:T(8,128)(2,1)} %copy-done.1), calls=%async_computation | async-start | bytes 262144 | tf_op jit(solution)/shard_map/all_to_all | solution.py:543
  36.4 0.0 collective-permute-done.3.b
  36.4 0.0 collective-permute-done.2.a
  36.5 1.1 %fold.2 = (s16[432,256]{1,0:T(8,128)(2,1)}, f32[416,256]{1,0:T(8,128)S(1)}) custom-call(s16[432,512]{1,0:T(8,128)(2,1)S(1)} %collective-permute-done.2.a, s16[432,512]{1,0:T(8,128)(2,1)S(1)} %collective-permute-done.3.b, f32[416,512]{1,0:T(8,128)S(1)} %get-tuple-element.47.own), custom_call_target="tpu_custom_call" | custom-call | flops 1 | bytes 1 | tf_op jit(solution)/shard_map/fold/pallas_call | solution.py:288
  37.5 0.0 copy-start.4
  37.5 0.8 copy-done.4
  38.3 4.2 %collective-permute-start.4 = (s16[432,256]{1,0:T(8,128)(2,1)}, s16[432,256]{1,0:T(8,128)(2,1)S(1)}, u32[]{:S(2)}, u32[]{:S(2)}) collective-permute-start(s16[432,256]{1,0:T(8,128)(2,1)} %get-tuple-element.48), channel_id=1, source_target_pairs={{0,1},{1,0},{2,3},{3,2},{4,5},{5,4},{6,7},{7,6},{8,9},{9,8},{10,11... | collective-permute-start | bytes 663560 | tf_op jit(solution)/shard_map/ppermute | solution.py:545
  42.5 0.0 collective-permute-done.6.b
  42.5 0.0 collective-permute-done.5.a
  42.5 1.4 %fold.3 = (s16[400,256]{1,0:T(8,128)(2,1)S(1)}, f32[384,256]{1,0:T(8,128)S(1)}) custom-call(s16[400,512]{1,0:T(8,128)(2,1)} %collective-permute-done.5.a, s16[400,512]{1,0:T(8,128)(2,1)S(1)} %collective-permute-done.6.b, f32[384,512]{1,0:T(8,128)S(1)} %get-tuple-element.51.own), custom_call_target="tpu_custom_call" | custom-call | flops 1 | bytes 1 | tf_op jit(solution)/shard_map/fold/pallas_call | solution.py:288
  43.9 5.4 %collective-permute-start.7 = (s16[400,256]{1,0:T(8,128)(2,1)S(1)}, s16[400,256]{1,0:T(8,128)(2,1)S(1)}, u32[]{:S(2)}, u32[]{:S(2)}) collective-permute-start(s16[400,256]{1,0:T(8,128)(2,1)S(1)} %get-tuple-element.52), channel_id=1, source_target_pairs={{0,1},{1,0},{2,3},{3,2},{4,5},{5,4},{6,7},{7,6},{8,9},{9,8},{10,11... | collective-permute-start | bytes 614408 | tf_op jit(solution)/shard_map/ppermute | solution.py:547
  49.3 0.0 copy-done.6
  49.3 0.0 all-to-all-done.queries
  49.3 4.2 %collective-permute-done.7.refs_1_.came = s16[400,256]{1,0:T(8,128)(2,1)S(1)} collective-permute-done((s16[400,256]{1,0:T(8,128)(2,1)S(1)}, s16[400,256]{1,0:T(8,128)(2,1)S(1)}, u32[]{:S(2)}, u32[]{:S(2)}) %collective-permute-start.7) | collective-permute-done | bytes 204832 | tf_op jit(solution)/shard_map/ppermute | solution.py:547
  53.5 0.0 collective-permute-done.4.refs_0_
  53.5 0.0 copy-start.5
  53.5 1.0 %copy-done.5 = f32[416,256]{1,0:T(8,128)S(1)} copy-done((f32[416,256]{1,0:T(8,128)S(1)}, f32[416,256]{1,0:T(8,128)}, u32[]{:S(2)}) %copy-start.5) | copy-done | bytes 426008
  54.5 3.2 %prefix.1 = (bf16[768,256]{1,0:T(8,128)(2,1)}, s16[32,24,128]{2,1,0:T(8,128)(2,1)}) custom-call(bf16[32,16,128]{2,1,0:T(8,128)(2,1)} %all-to-all-done.queries, f32[1,256]{1,0:T(1,128)S(1)} %bitcast.4, f32[56,256]{1,0:T(8,128)} %constant.5.clone.turns, s16[432,256]{1,0:T(8,128)(2,1)S(1)} %collective-permute-done.4.refs_0_, ...), custom_call_target="tpu_custom_call" | custom-call | flops 200000000 | bytes 10000000 | tf_op jit(solution)/shard_map/prefix/pallas_call | solution.py:451
  57.7 16.8 %all-to-all-start.1 = ((s16[32,24,128]{2,1,0:T(8,128)(2,1)}), s16[32,24,128]{2,1,0:T(8,128)(2,1)S(1)}, u32[]{:S(2)}, u32[]{:S(2)}) async-start(s16[32,24,128]{2,1,0:T(8,128)(2,1)} %get-tuple-element.60), calls=%async_computation.1 | async-start | bytes 393216 | tf_op jit(solution)/shard_map/all_to_all | solution.py:556
  74.5 2.8 %suffix.1 = (bf16[32,256]{1,0:T(8,128)(2,1)}, f32[256,128]{1,0:T(8,128)S(1)}, f32[256,128]{1,0:T(8,128)S(1)}) custom-call(s32[32]{0:T(128)S(1)} %copy-done.3, f32[256,128]{1,0:T(8,128)S(1)} %get-tuple-element.56.turned, bf16[32,128,256]{2,1,0:T(8,128)(2,1)} %cache.1, s16[400,256]{1,0:T(8,128)(2,1)S(1)} %collective-permute-done.7.refs_1_.came, ...), custom_call_target="tpu_custom_call" | custom-call | flops 10000000 | bytes 10000000 | tf_op jit(solution)/shard_map/suffix/pallas_call | solution.py:396
  77.3 6.9 %all-to-all-done.1.back = s16[32,24,128]{2,1,0:T(8,128)(2,1)S(1)} async-done(((s16[32,24,128]{2,1,0:T(8,128)(2,1)}), s16[32,24,128]{2,1,0:T(8,128)(2,1)S(1)}, u32[]{:S(2)}, u32[]{:S(2)}) %all-to-all-start.1) | async-done | bytes 196640 | tf_op jit(solution)/shard_map/all_to_all | solution.py:556
  84.2 1.9 %merge.1 = bf16[32,1024]{1,0:T(8,128)(2,1)} custom-call(s32[32]{0:T(128)S(1)} %get-tuple-element.59.place, s16[32,24,128]{2,1,0:T(8,128)(2,1)S(1)} %all-to-all-done.1.back, f32[256,128]{1,0:T(8,128)S(1)} %get-tuple-element.61.out, f32[256,128]{1,0:T(8,128)S(1)} %get-tuple-element.62.stats), custom_call_target="tpu_custom_call" | custom-call | flops 1000000 | bytes 1000000 | tf_op jit(solution)/shard_map/merge/pallas_call | solution.py:500
  (1 shorter events, 0.0 us)
Async XLA Ops:
  5.8 14.4 %collective-permute-start.1 = (s16[432,512]{1,0:T(8,128)(2,1)S(1)}, s16[432,512]{1,0:T(8,128)(2,1)S(1)}, u32[]{:S(2)}, u32[]{:S(2)}) collective-permute-start(s16[432,512]{1,0:T(8,128)(2,1)S(1)} %get-tuple-element.44), channel_id=1, source_target_pairs={{0,2},{1,3},{2,4},{3,5},{4,6},{5,7},{6,0},{7,1},{8,10},{9,11},{10,... | collective-permute-start | bytes 1327112 | tf_op jit(solution)/shard_map/ppermute | solution.py:523
  8.0 13.0 %collective-permute-start = (s16[400,512]{1,0:T(8,128)(2,1)S(1)}, s16[400,512]{1,0:T(8,128)(2,1)}, u32[]{:S(2)}, u32[]{:S(2)}) collective-permute-start(s16[400,512]{1,0:T(8,128)(2,1)S(1)} %get-tuple-element.33), channel_id=1, source_target_pairs={{0,6},{1,7},{2,0},{3,1},{4,2},{5,3},{6,4},{7,5},{8,14},{9,15},{10,... | collective-permute-start | bytes 1228808 | tf_op jit(solution)/shard_map/ppermute | solution.py:523
  9.5 8.6 %copy-start = (f32[128,256]{1,0:T(8,128)S(1)}, f32[128,256]{1,0:T(8,128)}, u32[]{:S(2)}) copy-start(f32[128,256]{1,0:T(8,128)} %constant.4.clone.table) | copy-start | bytes 393220
  9.5 8.6 %copy-start.2 = (bf16[32,1024]{1,0:T(8,128)(2,1)S(1)}, bf16[32,1024]{1,0:T(8,128)(2,1)}, u32[]{:S(2)}) copy-start(bf16[32,1024]{1,0:T(8,128)(2,1)} %queries) | copy-start | bytes 196612
  9.5 8.6 %copy-start.3 = (s32[32]{0:T(128)S(1)}, s32[32]{0:T(128)}, u32[]{:S(2)}) copy-start(s32[32]{0:T(128)} %lengths.3) | copy-start | bytes 388
  16.7 19.8 %collective-permute-start.3 = (s16[432,512]{1,0:T(8,128)(2,1)}, s16[432,512]{1,0:T(8,128)(2,1)S(1)}, u32[]{:S(2)}, u32[]{:S(2)}) collective-permute-start(s16[432,512]{1,0:T(8,128)(2,1)} %get-tuple-element.46), channel_id=1, source_target_pairs={{0,6},{1,7},{2,0},{3,1},{4,2},{5,3},{6,4},{7,5},{8,14},{9,15},{10,... | collective-permute-start | bytes 1327112 | tf_op jit(solution)/shard_map/ppermute | solution.py:523
  20.1 0.7 copy-start.1
  20.6 15.9 %collective-permute-start.2 = (s16[432,512]{1,0:T(8,128)(2,1)S(1)}, s16[432,512]{1,0:T(8,128)(2,1)S(1)}, u32[]{:S(2)}, u32[]{:S(2)}) collective-permute-start(s16[432,512]{1,0:T(8,128)(2,1)S(1)} %relay.3), channel_id=1, source_target_pairs={{0,2},{1,3},{2,4},{3,5},{4,6},{5,7},{6,0},{7,1},{8,10},{9,11},{10,... | collective-permute-start | bytes 1327112 | tf_op jit(solution)/shard_map/ppermute | solution.py:523
  20.8 21.7 %collective-permute-start.6 = (s16[400,512]{1,0:T(8,128)(2,1)}, s16[400,512]{1,0:T(8,128)(2,1)S(1)}, u32[]{:S(2)}, u32[]{:S(2)}) collective-permute-start(s16[400,512]{1,0:T(8,128)(2,1)} %get-tuple-element.50), channel_id=1, source_target_pairs={{0,2},{1,3},{2,4},{3,5},{4,6},{5,7},{6,0},{7,1},{8,10},{9,11},{10,... | collective-permute-start | bytes 1228808 | tf_op jit(solution)/shard_map/ppermute | solution.py:523
  23.1 26.2 %copy-start.6 = (bf16[256]{0:T(256)(128)(2,1)S(1)}, bf16[256]{0:T(256)(128)(2,1)}, u32[]{:S(2)}) copy-start(bf16[256]{0:T(256)(128)(2,1)} %param.18) | copy-start | bytes 1540
  23.1 19.4 %collective-permute-start.5 = (s16[400,512]{1,0:T(8,128)(2,1)}, s16[400,512]{1,0:T(8,128)(2,1)}, u32[]{:S(2)}, u32[]{:S(2)}) collective-permute-start(s16[400,512]{1,0:T(8,128)(2,1)} %relay.2), channel_id=1, source_target_pairs={{0,6},{1,7},{2,0},{3,1},{4,2},{5,3},{6,4},{7,5},{8,14},{9,15},{10,... | collective-permute-start | bytes 1228808 | tf_op jit(solution)/shard_map/ppermute | solution.py:523
  25.6 23.6 %all-to-all-start = ((bf16[32,16,128]{2,1,0:T(8,128)(2,1)}), bf16[32,16,128]{2,1,0:T(8,128)(2,1)}, u32[]{:S(2)}, u32[]{:S(2)}) async-start(bf16[32,16,128]{2,1,0:T(8,128)(2,1)} %copy-done.1), calls=%async_computation | async-start | bytes 262144 | tf_op jit(solution)/shard_map/all_to_all | solution.py:543
  37.5 0.8 copy-start.4
  38.3 15.2 %collective-permute-start.4 = (s16[432,256]{1,0:T(8,128)(2,1)}, s16[432,256]{1,0:T(8,128)(2,1)S(1)}, u32[]{:S(2)}, u32[]{:S(2)}) collective-permute-start(s16[432,256]{1,0:T(8,128)(2,1)} %get-tuple-element.48), channel_id=1, source_target_pairs={{0,1},{1,0},{2,3},{3,2},{4,5},{5,4},{6,7},{7,6},{8,9},{9,8},{10,11... | collective-permute-start | bytes 663560 | tf_op jit(solution)/shard_map/ppermute | solution.py:545
  43.9 9.6 %collective-permute-start.7 = (s16[400,256]{1,0:T(8,128)(2,1)S(1)}, s16[400,256]{1,0:T(8,128)(2,1)S(1)}, u32[]{:S(2)}, u32[]{:S(2)}) collective-permute-start(s16[400,256]{1,0:T(8,128)(2,1)S(1)} %get-tuple-element.52), channel_id=1, source_target_pairs={{0,1},{1,0},{2,3},{3,2},{4,5},{5,4},{6,7},{7,6},{8,9},{9,8},{10,11... | collective-permute-start | bytes 614408 | tf_op jit(solution)/shard_map/ppermute | solution.py:547
  53.5 1.0 %copy-start.5 = (f32[416,256]{1,0:T(8,128)S(1)}, f32[416,256]{1,0:T(8,128)}, u32[]{:S(2)}) copy-start(f32[416,256]{1,0:T(8,128)} %copy-done.4) | copy-start | bytes 1277956
  57.7 26.5 %all-to-all-start.1 = ((s16[32,24,128]{2,1,0:T(8,128)(2,1)}), s16[32,24,128]{2,1,0:T(8,128)(2,1)S(1)}, u32[]{:S(2)}, u32[]{:S(2)}) async-start(s16[32,24,128]{2,1,0:T(8,128)(2,1)} %get-tuple-element.60), calls=%async_computation.1 | async-start | bytes 393216 | tf_op jit(solution)/shard_map/all_to_all | solution.py:556
